TPU v7x, 512 devices: a whole 4x4x16 slice. The times are simulated.
512 devices in a mesh: row: 16 (over x, y), col: 32 (over z, core).
Axes of the slice: x: 4, y: 4, z: 16, core: 2. Of those that a mesh axis runs over, the one named last changes fastest.
Arguments:
- amplitudes: float32 [2048, 12288], P(('col', 'row')), may hold values from -6 to 6
- integrals: float32 [12288, 16384], P('row', 'col'), may hold values from -0.15625 to 0.15625
- ij_irrep: int32 [2048], replicated, may hold values from 0 to 7, as said below
- cd_irrep: int32 [12288], P('row'), may hold values from 0 to 7, as said below
- ab_irrep: int32 [16384], P('col'), may hold values from 0 to 7, as said below
Outputs:
- ladder: float32 [2048, 16384], P('row', 'col')
Inputs may be any that keep to these rules, and one draw needn't show every extreme that they name: `ij_irrep`: irrep labels of D2h. `cd_irrep`: irrep labels of D2h. `ab_irrep`: irrep labels of D2h.
All inputs are finite; a program needn't handle non-finite values.
Results may differ from a plain program's by a relative error of at most 0.00009.
Values sent between devices are 32-bit elements; how exact they have to be, the bound alone decides.
No kernel may reach another device: no remote copies, remote signals or barrier semaphores. Data moves between devices by JAX's collectives and lax.ppermute only.
A program may use at most 64 MiB of HBM per device.

v0:
```python
import jax
import jax.numpy as jnp
from jax import lax
from jax.sharding import PartitionSpec as P


def body(amplitudes, integrals, ij_irrep, cd_irrep, ab_irrep):
    panel = jnp.where(cd_irrep[:, None] == ab_irrep[None, :], integrals, jnp.float32(0.0))
    regrouped = lax.all_to_all(amplitudes, "row", split_axis=1, concat_axis=0, tiled=True)
    masked = jnp.where(
        ij_irrep[:, None] == cd_irrep[None, :],
        lax.all_gather(regrouped, "col", axis=0, tiled=True),
        jnp.float32(0.0),
    )
    partial_sum = jnp.dot(
        masked, panel, precision=lax.Precision.HIGHEST, preferred_element_type=jnp.float32
    )
    summed = lax.psum_scatter(partial_sum, "row", scatter_dimension=0, tiled=True)
    return 0.5 * summed


def solution(mesh):
    in_specs = (P(("col", "row"), None), P("row", "col"), P(), P("row"), P("col"))
    out_specs = P("row", "col")
    return jax.shard_map(body, mesh=mesh, in_specs=in_specs, out_specs=out_specs, check_vma=False)
```

profile of v0, /device:TPU:6, one launch (start us, length us, event | category | flops | bytes accessed | tf_op | source)
XLA Modules:
  0.0 214.3 jit_solution(13405361974157868185)
XLA Ops:
  6.5 0.0 all-gather.2.cloned.1.call-start
  6.5 15.3 %all_to_all.19 = f32[4,16,768]{2,0,1:T(4,128)S(1)} all-to-all(f32[4,16,768]{2,0,1:T(4,128)} %bitcast.3), channel_id=1, replica_groups=mesh['row'=16,'col'=32] {'row'}, dimensions={1} | all-to-all | bytes 393216 | tf_op jit(solution)/shard_map/all_to_all | solution.py:9
  21.8 0.7 all_to_all.17
  22.6 0.0 all-gather.2.cloned.1.call-update
  22.6 0.0 reduce-scatter.2.cloned.1.call-start
  22.6 77.9 %all-gather.2.cloned.1.call-done = f32[2048,768]{1,0:T(8,128)} async-done(((f32[64,768]{1,0:T(8,128)}), f32[2048,768]{1,0:T(8,128)}) %all-gather.2.cloned.1.call-update) | async-done | bytes 6291472 | tf_op jit(solution)/shard_map/all_gather | solution.py:12
  100.5 15.2 %fusion = f32[2048,512]{1,0:T(8,128)} fusion(f32[2048,768]{1,0:T(8,128)} %all-gather.2.cloned.1.call-done, s32[768]{0:T(1024)} %param.8, s32[2048]{0:T(1024)} %param.7, f32[768,512]{1,0:T(8,128)} %param.6, s32[512]{0:T(512)} %param.9), kind=kOutput, calls=%fused_computation | convolution fusion | flops 9667608576 | bytes 12071936 | tf_op jit(solution)/shard_map/dot_general | solution.py:15
  115.8 0.0 reduce-scatter.2.cloned.1.call-update
  115.8 90.0 %reduce-scatter.2.cloned.1.call-done = f32[128,512]{1,0:T(8,128)} async-done(((f32[2048,512]{1,0:T(8,128)}), f32[128,512]{1,0:T(8,128)}) %reduce-scatter.2.cloned.1.call-update) | async-done | bytes 262160 | tf_op jit(solution)/shard_map/reduce_scatter | solution.py:18
  205.8 1.7 broadcast_multiply_fusion
Async XLA Ops:
  6.5 94.0 %all-gather.2.cloned.1.call-start = ((), (), s32[]{:S(2)}) async-start(), calls=%async_computation.2 | async-start | bytes 6488064 | tf_op jit(solution)/shard_map/all_gather | solution.py:12
  22.6 183.2 %reduce-scatter.2.cloned.1.call-start = ((), (), s32[]{:S(2)}) async-start(), calls=%async_computation.3 | async-start | bytes 4456448 | tf_op jit(solution)/shard_map/reduce_scatter | solution.py:18
Sparse Core Ops, SparseCore 0:
  22.7 77.7 all-gather.1
  115.9 89.7 reduce-scatter.1
where the time goes:
time: 215 us; the launch traced here: 214 us
  waiting for transfers between devices  168 us (78%)
  blocking collectives  15.3 us (7%)
  matrix products  15.2 us (7%)
  between operations  13.4 us (6%)
    reduce_scatter x1, waiting for transfers between devices, body(): lax.psum_scatter(partial_sum, 'row', scatter_dimension=0, tiled=True)  90 us
    all_gather x1, waiting for transfers between devices, body(): lax.all_gather(regrouped, 'col', axis=0, tiled=True)  77.9 us
    all_to_all x1, blocking collectives, body(): lax.all_to_all(amplitudes, 'row', split_axis=1, concat_axis=0, tiled=True)  15.3 us
    dot_general x1, matrix products, body(): jnp.dot(masked, panel, precision=lax.Precision.HIGHEST, preferred_element...  15.2 us
  transfers between devices with their start and end apart: 2, of which 2 were waited for; matrix products, arithmetic and copies ran while one was open for 0% of the time, Pallas kernels for 0%

commit v1 on v0

v1 whole, which is shorter than its diff:
```python
import functools

import jax
import jax.numpy as jnp
from jax import lax
from jax.experimental import pallas as pl
from jax.experimental.pallas import tpu as pltpu
from jax.sharding import Mesh
from jax.sharding import PartitionSpec as P

BLOCK = 128
BLOCKS = 16
LABELS = 8
OWN = 16
HALF = BLOCKS * OWN
SLOTS = 2 * HALF
CD_CORE = 384
CD_DEV = 24
F32, BF16, I32 = jnp.float32, jnp.bfloat16, jnp.int32


def call(kernel, out_shape, in_specs=None, cost=(1_000_000, 1_000_000), **kwargs):
    return pl.pallas_call(
        kernel,
        out_shape=out_shape,
        compiler_params=pltpu.CompilerParams(vmem_limit_bytes=48 * 1024 * 1024),
        cost_estimate=pl.CostEstimate(flops=cost[0], bytes_accessed=cost[1], transcendentals=0),
        **({} if in_specs is None else {"in_specs": in_specs}),
        **kwargs,
    )


def split3(x):
    hi = x.astype(BF16)
    rest = x - hi.astype(F32)
    mid = rest.astype(BF16)
    return hi, mid, (rest - mid.astype(F32)).astype(BF16)


def down(row):
    return jnp.transpose(jnp.broadcast_to(row, (BLOCK, BLOCK)))


def arrival(rows):
    n = lax.broadcasted_iota(I32, (BLOCK, BLOCK), 0)
    p = lax.broadcasted_iota(I32, (BLOCK, BLOCK), 1)
    move = n == ((p >> 2) & 1) * 64 + (p >> 3) * 4 + (p & 3)
    return jnp.dot(rows, move.astype(F32), precision=lax.Precision.HIGHEST, preferred_element_type=F32)


def turn_kernel(place_ref, x_ref, ij_ref, cd_ref, out_ref):
    core, z = place_ref[0], place_ref[1]
    labels = jnp.broadcast_to(ij_ref[pl.ds(z, 1), :], (8, BLOCK)).astype(F32)
    labels = arrival(labels)[0:1, :].astype(I32)
    for j in range(CD_CORE // BLOCK):
        cols = slice(j * BLOCK, (j + 1) * BLOCK)
        cd = down(cd_ref[pl.ds(core * (CD_CORE // BLOCK) + j, 1), :])
        out_ref[cols, :] = jnp.where(cd == labels, jnp.transpose(x_ref[:, cols]), 0.0)


def pack_kernel(round_ref, x_ref, ij_ref, packed_ref, slot_ref):
    ij = ij_ref[...]
    label = lax.broadcasted_iota(I32, (BLOCKS, LABELS, BLOCK), 1)
    same = (jnp.broadcast_to(ij[:, None, :], label.shape) == label).astype(F32)
    upto = lax.broadcasted_iota(I32, (BLOCK, BLOCK), 0) <= lax.broadcasted_iota(I32, (BLOCK, BLOCK), 1)
    count = jnp.dot(
        same.reshape(BLOCKS * LABELS, BLOCK).astype(BF16), upto.astype(BF16), preferred_element_type=F32
    ).reshape(BLOCKS, LABELS, BLOCK)
    excess = jnp.maximum(count[:, :, BLOCK - 1 :] - OWN, 0.0)
    before = jnp.zeros((1, LABELS, 1), F32)
    rows = []
    for b in range(BLOCKS):
        rank = count[b : b + 1] - 1.0
        slot = jnp.where(rank < OWN, rank + b * OWN, rank - OWN + before + HALF)
        rows.append(jnp.sum(slot * same[b : b + 1], axis=1))
        before = before + excess[b : b + 1]
    slots = jnp.concatenate(rows, axis=0)
    slot_ref[...] = slots.astype(I32)
    here = arrival(slots).astype(I32) - round_ref[0] * SLOTS
    want = lax.broadcasted_iota(I32, (SLOTS, 2 * BLOCK), 0)
    total = jnp.zeros((3 * CD_DEV, SLOTS), F32)
    for b in range(0, BLOCKS, 2):
        pair = jnp.concatenate([here[b : b + 1], here[b + 1 : b + 2]], axis=1)
        chosen = jnp.where(want == pair, 1.0, 0.0).astype(BF16)
        x = jnp.concatenate([x_ref[b], x_ref[b + 1]], axis=1)
        parts = jnp.concatenate([p.astype(F32) for p in split3(x)], axis=0).astype(BF16)
        total += lax.dot_general(parts, chosen, (((1,), (1,)), ((), ())), preferred_element_type=F32)
    packed_ref[...] = total[:CD_DEV] + total[CD_DEV : 2 * CD_DEV] + total[2 * CD_DEV :]


def panel_kernel(v_ref, cd_ref, ab_ref, hi_ref, lo_ref):
    for j in range(v_ref.shape[0] // BLOCK):
        cd = down(cd_ref[j : j + 1, :])
        for k in range(v_ref.shape[1] // BLOCK):
            at = (slice(j * BLOCK, (j + 1) * BLOCK), slice(k * BLOCK, (k + 1) * BLOCK))
            v = jnp.where(cd == ab_ref[:, at[1]], v_ref[at], 0.0)
            hi = v.astype(BF16)
            hi_ref[at] = hi
            lo_ref[at] = (v - hi.astype(F32)).astype(BF16)


def product_kernel(place_ref, mine_ref, other_ref, hi_ref, lo_ref, own_ref, shared_ref):
    core = place_ref[0]
    total = None
    for part, half in ((mine_ref, core), (other_ref, 1 - core)):
        rows = pl.ds(pl.multiple_of(half * CD_CORE, CD_CORE), CD_CORE)
        t = part[...]
        t_hi = t.astype(BF16)
        t_lo = (t - t_hi.astype(F32)).astype(BF16)
        for a, b in ((t_hi, hi_ref), (t_hi, lo_ref), (t_lo, hi_ref)):
            term = lax.dot_general(a, b[rows, :], (((0,), (0,)), ((), ())), preferred_element_type=F32)
            total = term if total is None else total + term
    own_ref[...] = total[:HALF]
    shared_ref[...] = total[HALF:]


def spread(a, slots, labels, ab_ref, out_ref):
    chosen = jnp.where(lax.broadcasted_iota(I32, (a.shape[0], BLOCK), 0) == slots, 1.0, 0.0).astype(BF16)
    total = None
    for part in split3(a):
        term = lax.dot_general(chosen, part, (((0,), (0,)), ((), ())), preferred_element_type=F32)
        total = term if total is None else total + term
    ij = down(labels)
    for k in range(out_ref.shape[1] // BLOCK):
        cols = slice(k * BLOCK, (k + 1) * BLOCK)
        out_ref[:, cols] = jnp.where(ij == ab_ref[:, cols], 0.5 * total[:, cols], 0.0)


def first_kernel(place_ref, own_ref, shared_ref, slot_ref, ij_ref, ab_ref, out_ref):
    row = place_ref[2]
    own = own_ref[0]
    for b in range(1, BLOCKS):
        own = own + own_ref[b]
    slots = slot_ref[pl.ds(row, 1), :]
    slots = jnp.where(slots < HALF, slots - row * OWN, slots - HALF + OWN)
    spread(jnp.concatenate([own, shared_ref[...]], axis=0), slots, ij_ref[pl.ds(row, 1), :], ab_ref, out_ref)


def later_kernel(place_ref, round_ref, a_ref, slot_ref, ij_ref, ab_ref, out_ref):
    row = place_ref[2]
    slots = slot_ref[pl.ds(row, 1), :] - round_ref[0] * SLOTS
    spread(a_ref[...], slots, ij_ref[pl.ds(row, 1), :], ab_ref, out_ref)


def body(amplitudes, integrals, ij_irrep, cd_irrep, ab_irrep):
    smem = pl.BlockSpec(memory_space=pltpu.SMEM)
    vmem = pl.BlockSpec(memory_space=pltpu.VMEM)
    shape = jax.ShapeDtypeStruct
    place = jnp.stack([lax.axis_index("core"), lax.axis_index("z"), lax.axis_index("row")]).astype(I32)
    ij = ij_irrep.reshape(BLOCKS, BLOCK)
    cd = cd_irrep.reshape(-1, BLOCK)
    ab = ab_irrep.reshape(1, -1)
    cds, abs_ = integrals.shape

    arrived = lax.all_to_all(amplitudes, ("row", "core"), split_axis=1, concat_axis=0, tiled=True)
    turned = call(turn_kernel, shape((CD_CORE, BLOCK), F32), [smem, vmem, vmem, vmem])(place, arrived, ij, cd)
    mine = lax.all_to_all(turned, "z", split_axis=0, concat_axis=0, tiled=True).reshape(BLOCKS, CD_DEV, BLOCK)

    v_hi, v_lo = call(panel_kernel, [shape((cds, abs_), BF16)] * 2, [vmem] * 3, (2_000_000, 3_200_000))(integrals, cd, ab)

    def products(number):
        packed, slots = call(
            pack_kernel, [shape((CD_DEV, SLOTS), F32), shape((BLOCKS, BLOCK), I32)], [smem, vmem, vmem]
        )(number, mine, ij)
        gathered = lax.all_gather(packed, "z", axis=0, tiled=True)
        other = lax.ppermute(gathered, "core", [(0, 1), (1, 0)])
        own, shared = call(
            product_kernel, [shape((HALF, abs_), F32)] * 2, [smem] + [vmem] * 4, (1_200_000_000, 5_000_000)
        )(place, gathered, other, v_hi, v_lo)
        return own, shared, slots

    own, shared, slots = products(jnp.zeros((1,), I32))
    shared = lax.all_to_all(shared, "row", split_axis=0, concat_axis=0, tiled=True)
    shared = jnp.sum(shared.reshape(BLOCKS, OWN, abs_), axis=0)
    shared = lax.all_gather(shared, "row", axis=0, tiled=True)
    own = lax.all_to_all(own, "row", split_axis=0, concat_axis=0, tiled=True)
    out = call(first_kernel, shape((BLOCK, abs_), F32), [smem] + [vmem] * 5)(
        place, own.reshape(BLOCKS, OWN, abs_), shared, slots, ij, ab
    )
    rounds = (jnp.max(slots) >> 9) + 1

    def again(state):
        number, out = state
        own, shared, slots = products(number[None])
        whole = lax.psum(jnp.concatenate([own, shared], axis=0), "row")
        more = call(later_kernel, shape((BLOCK, abs_), F32), [smem] * 2 + [vmem] * 4)(
            place, number[None], whole, slots, ij, ab
        )
        return number + 1, out + more

    return lax.while_loop(lambda state: state[0] < rounds, again, (jnp.int32(1), out))[1]


def solution(mesh):
    finer = Mesh(mesh.devices.reshape(16, 16, 2), ("row", "z", "core"))
    in_specs = (P(("z", "core", "row"), None), P("row", ("z", "core")), P(), P("row"), P(("z", "core")))
    out_specs = P("row", ("z", "core"))
    return jax.shard_map(body, mesh=finer, in_specs=in_specs, out_specs=out_specs, check_vma=False)
```

time: 215 us -> 152 us (0.71)
  waiting for transfers between devices: 168 us -> 8.12 us
  blocking collectives: 15.3 us -> 103 us
  starting transfers between devices: 0.04 us -> 17.1 us
  matrix products: 15.2 us -> 0 us
  Pallas kernels: 0 us -> 7.35 us
    reduce_scatter x1 -> x0, waiting for transfers between devices: 90 us -> none  [body(): lax.psum_scatter(partial_sum, 'row', scatter_dimension=0, tiled=True)]
    all_gather x1 -> x0, waiting for transfers between devices: 77.9 us -> none  [body(): lax.all_gather(regrouped, 'col', axis=0, tiled=True)]
    all_gather x0 -> x2, blocking collectives: none -> 58.9 us  [the longest x1 34.9 us: products(): gathered = lax.all_gather(packed, 'z', axis=0, tiled=True)]
    all_to_all x1 -> x2, blocking collectives: 15.3 us -> 43.7 us  [the longest x1 28.8 us: body(): lax.all_to_all(turned, 'z', split_axis=0, concat_axis=0, tiled=True)]
    dot_general x1 -> x0, matrix products: 15.2 us -> none  [body(): jnp.dot(masked, panel, precision=lax.Precision.HIGHEST, preferred_element...]
    all_to_all x0 -> x2, starting transfers between devices: none -> 15.2 us  [the longest x1 9.66 us: body(): lax.all_to_all(amplitudes, ('row', 'core'), split_axis=1, concat_axis=0,...]
    pallas_call x0 -> x5, Pallas kernels: none -> 7.35 us  [the longest x1 3.11 us: products(): call(product_kernel, [shape((HALF, abs_), F32)] * 2, [smem] + [vmem] * 4,...]
    all_to_all x0 -> x2, waiting for transfers between devices: none -> 6.29 us  [the longest x1 6.29 us: body(): lax.all_to_all(amplitudes, ('row', 'core'), split_axis=1, concat_axis=0,...]
  transfers between devices with their start and end apart: 2 -> 3, of which waited for: 2 -> 2; matrix products, arithmetic and copies ran while one was open for 0% -> 0% of each run, Pallas kernels for 0% -> 0%
where the time goes in v1:
time: 152 us
  blocking collectives  103 us (68%)
  starting transfers between devices  17.1 us (11%)
  between operations  14.1 us (9%)
  waiting for transfers between devices  8.12 us (5%)
  Pallas kernels  7.35 us (5%)
    all_gather x1, blocking collectives, products(): gathered = lax.all_gather(packed, 'z', axis=0, tiled=True)  34.9 us
    all_to_all x1, blocking collectives, body(): lax.all_to_all(turned, 'z', split_axis=0, concat_axis=0, tiled=True)  28.8 us
    all_gather x1, blocking collectives, body(): shared = lax.all_gather(shared, 'row', axis=0, tiled=True)  24 us
    all_to_all x1, blocking collectives, body(): lax.all_to_all(shared, 'row', split_axis=0, concat_axis=0, tiled=True)  14.9 us
    all_to_all x1, starting transfers between devices, body(): lax.all_to_all(amplitudes, ('row', 'core'), split_axis=1, concat_axis=0,...  9.66 us
    all_to_all x1, waiting for transfers between devices, body(): lax.all_to_all(amplitudes, ('row', 'core'), split_axis=1, concat_axis=0,...  6.29 us
    all_to_all x1, starting transfers between devices, body(): own = lax.all_to_all(own, 'row', split_axis=0, concat_axis=0, tiled=True)  5.56 us
    pallas_call x1, Pallas kernels, products(): call(product_kernel, [shape((HALF, abs_), F32)] * 2, [smem] + [vmem] * 4,...  3.11 us
  transfers between devices with their start and end apart: 3, of which 2 were waited for; matrix products, arithmetic and copies ran while one was open for 0% of the time, Pallas kernels for 0%

profile of v1, /device:TPU:6, one launch (start us, length us, event | category | flops | bytes accessed | tf_op | source)
XLA Modules:
  0.0 151.5 jit_solution(5053362049252064317)
XLA Ops:
  6.5 0.0 copy-start.1
  6.5 9.7 %all-to-all-start = ((f32[4,32,384]{2,0,1:T(4,128)}), f32[4,32,384]{2,0,1:T(4,128)S(1)}, u32[]{:S(2)}, u32[]{:S(2)}) async-start(f32[4,32,384]{2,0,1:T(4,128)} %bitcast.23), calls=%async_computation | async-start | bytes 393216 | tf_op jit(solution)/shard_map/all_to_all | solution.py:155
  16.2 0.1 pad_add_fusion.place_ref
  16.3 6.3 %all-to-all-done = f32[4,32,384]{2,0,1:T(4,128)S(1)} async-done(((f32[4,32,384]{2,0,1:T(4,128)}), f32[4,32,384]{2,0,1:T(4,128)S(1)}, u32[]{:S(2)}, u32[]{:S(2)}) %all-to-all-start) | async-done | bytes 196640 | tf_op jit(solution)/shard_map/all_to_all | solution.py:155
  22.6 0.1 all_to_all.35.x_ref
  22.6 0.0 copy-start.2
  22.7 0.7 copy-done.2
  23.3 0.0 copy-start.5
  23.3 0.9 shard_map.55
  24.3 28.8 %all_to_all.46.x_ref = f32[16,24,128]{2,1,0:T(8,128)S(1)} all-to-all(f32[16,24,128]{2,1,0:T(8,128)S(1)} %bitcast.14), channel_id=1, replica_groups=mesh['row'=16,'z'=16,'core'=2] {'z'}, dimensions={0} | all-to-all | bytes 393216 | tf_op jit(solution)/shard_map/all_to_all | solution.py:157
  53.1 2.0 %shard_map.56 = (f32[24,512]{1,0:T(8,128)S(1)}, s32[16,128]{1,0:T(8,128)S(1)}) custom-call(s32[1]{0:T(128)} %constant.20.clone.1.round_ref, f32[16,24,128]{2,1,0:T(8,128)S(1)} %all_to_all.46.x_ref, s32[16,128]{1,0:T(8,128)} %bitcast.19), custom_call_target="tpu_custom_call" | custom-call | flops 1000000 | bytes 1000000 | tf_op jit(solution)/shard_map/pallas_call | solution.py:162
  55.0 34.9 %all_gather.9.mine_ref = f32[384,512]{1,0:T(8,128)S(1)} all-gather(f32[24,512]{1,0:T(8,128)S(1)} %get-tuple-element.63), channel_id=1, replica_groups=mesh['row'=16,'z'=16,'core'=2] {'z'}, dimensions={0}, use_global_device_ids=true | all-gather | bytes 835584 | tf_op jit(solution)/shard_map/all_gather | solution.py:165
  90.0 1.9 %collective-permute-start.1 = (f32[384,512]{1,0:T(8,128)S(1)}, f32[384,512]{1,0:T(8,128)S(1)}, u32[]{:S(2)}, u32[]{:S(2)}) collective-permute-start(f32[384,512]{1,0:T(8,128)S(1)} %all_gather.9.mine_ref), channel_id=1, source_target_pairs={{0,1},{1,0},{2,3},{3,2},{4,5},{5,4},{6,7},{7,6},{8,9},{9,8},{10,11... | collective-permute-start | bytes 2359304 | tf_op jit(solution)/shard_map/ppermute | solution.py:166
  91.9 0.0 copy-done.1
  91.9 0.0 copy-done.5
  91.9 0.4 shard_map.57
  92.3 1.8 %collective-permute-done.1.other_ref = f32[384,512]{1,0:T(8,128)S(1)} collective-permute-done((f32[384,512]{1,0:T(8,128)S(1)}, f32[384,512]{1,0:T(8,128)S(1)}, u32[]{:S(2)}, u32[]{:S(2)}) %collective-permute-start.1) | collective-permute-done | bytes 786464 | tf_op jit(solution)/shard_map/ppermute | solution.py:166
  94.1 3.1 %shard_map.58 = (f32[256,512]{1,0:T(8,128)}, f32[256,512]{1,0:T(8,128)S(1)}) custom-call(s32[3]{0:T(128)S(1)} %pad_add_fusion.place_ref, f32[384,512]{1,0:T(8,128)S(1)} %all_gather.9.mine_ref, f32[384,512]{1,0:T(8,128)S(1)} %collective-permute-done.1.other_ref, bf16[768,512]{1,0:T(8,128)(2,1)S(1)} %get-tuple-element.158.hi_ref, ...), custom_call_target="tpu_custom_call" | custom-call | flops 1200000000 | bytes 5000000 | tf_op jit(solution)/shard_map/pallas_call | solution.py:167
  97.2 0.0 copy-start.4
  97.2 14.9 %all_to_all.47 = f32[16,16,512]{2,1,0:T(8,128)S(1)} all-to-all(f32[16,16,512]{2,1,0:T(8,128)S(1)} %bitcast.15), channel_id=1, replica_groups=mesh['row'=16,'z'=16,'core'=2] {'row'}, dimensions={0} | all-to-all | bytes 1048576 | tf_op jit(solution)/shard_map/all_to_all | solution.py:173
  112.1 5.6 %all-to-all-start.2 = ((f32[16,16,512]{2,1,0:T(8,128)}), f32[16,16,512]{2,1,0:T(8,128)S(1)}, u32[]{:S(2)}, u32[]{:S(2)}) async-start(f32[16,16,512]{2,1,0:T(8,128)} %bitcast.10), calls=%async_computation.2 | async-start | bytes 1048576 | tf_op jit(solution)/shard_map/all_to_all | solution.py:176
  117.7 0.6 reduce_max.9
  119.0 24.0 %all_gather.10.shared_ref = f32[256,512]{1,0:T(8,128)S(1)} all-gather(f32[16,512]{1,0:T(8,128)S(1)} %reduce_sum.9), channel_id=1, replica_groups=mesh['row'=16,'z'=16,'core'=2] {'row'}, dimensions={0}, use_global_device_ids=true | all-gather | bytes 557056 | tf_op jit(solution)/shard_map/all_gather | solution.py:175
  143.0 0.0 all-to-all-done.2.own_ref
  143.0 0.0 copy-done.4
  143.0 1.0 shard_map.59
  144.0 0.0 copy-start.3
  144.0 0.7 copy-done.3
  (2 shorter events, 0.0 us)
Async XLA Ops:
  6.5 85.3 %copy-start.1 = (f32[768,512]{1,0:T(8,128)S(1)}, f32[768,512]{1,0:T(8,128)}, u32[]{:S(2)}) copy-start(f32[768,512]{1,0:T(8,128)} %v_ref.1) | copy-start | bytes 4718596
  6.5 16.0 %all-to-all-start = ((f32[4,32,384]{2,0,1:T(4,128)}), f32[4,32,384]{2,0,1:T(4,128)S(1)}, u32[]{:S(2)}, u32[]{:S(2)}) async-start(f32[4,32,384]{2,0,1:T(4,128)} %bitcast.23), calls=%async_computation | async-start | bytes 393216 | tf_op jit(solution)/shard_map/all_to_all | solution.py:155
  22.6 0.7 copy-start.2
  23.3 68.5 %copy-start.5 = (s32[512]{0:T(512)S(1)}, s32[512]{0:T(512)}, u32[]{:S(2)}) copy-start(s32[512]{0:T(512)} %param.11) | copy-start | bytes 6148
  90.0 4.2 %collective-permute-start.1 = (f32[384,512]{1,0:T(8,128)S(1)}, f32[384,512]{1,0:T(8,128)S(1)}, u32[]{:S(2)}, u32[]{:S(2)}) collective-permute-start(f32[384,512]{1,0:T(8,128)S(1)} %all_gather.9.mine_ref), channel_id=1, source_target_pairs={{0,1},{1,0},{2,3},{3,2},{4,5},{5,4},{6,7},{7,6},{8,9},{9,8},{10,11... | collective-permute-start | bytes 2359304 | tf_op jit(solution)/shard_map/ppermute | solution.py:166
  97.2 45.8 %copy-start.4 = (s32[2048]{0:T(1024)S(1)}, s32[2048]{0:T(1024)}, u32[]{:S(2)}) copy-start(s32[2048]{0:T(1024)} %param.9) | copy-start | bytes 24580
  112.1 30.8 %all-to-all-start.2 = ((f32[16,16,512]{2,1,0:T(8,128)}), f32[16,16,512]{2,1,0:T(8,128)S(1)}, u32[]{:S(2)}, u32[]{:S(2)}) async-start(f32[16,16,512]{2,1,0:T(8,128)} %bitcast.10), calls=%async_computation.2 | async-start | bytes 1048576 | tf_op jit(solution)/shard_map/all_to_all | solution.py:176
  144.0 0.7 copy-start.3

commit v2 on v1

v2 whole, which is shorter than its diff:
```python
import jax
import jax.numpy as jnp
from jax import lax
from jax.experimental import pallas as pl
from jax.experimental.pallas import tpu as pltpu
from jax.sharding import Mesh
from jax.sharding import PartitionSpec as P

BLOCK = 128
BLOCKS = 16
LABELS = 8
OWN = 16
HALF = BLOCKS * OWN
SLOTS = 2 * HALF
CD_CORE = 384
STEP = 4
F32, BF16, I32 = jnp.float32, jnp.bfloat16, jnp.int32


def call(kernel, out_shape, in_specs=None, cost=(1_000_000, 1_000_000), **kwargs):
    return pl.pallas_call(
        kernel,
        out_shape=out_shape,
        compiler_params=pltpu.CompilerParams(vmem_limit_bytes=48 * 1024 * 1024),
        cost_estimate=pl.CostEstimate(flops=cost[0], bytes_accessed=cost[1], transcendentals=0),
        **({} if in_specs is None else {"in_specs": in_specs}),
        **kwargs,
    )


def split3(x):
    hi = x.astype(BF16)
    rest = x - hi.astype(F32)
    mid = rest.astype(BF16)
    return hi, mid, (rest - mid.astype(F32)).astype(BF16)


def down(row):
    return jnp.transpose(jnp.broadcast_to(row, (BLOCK, BLOCK)))


def arrival(rows):
    n = lax.broadcasted_iota(I32, (BLOCK, BLOCK), 0)
    p = lax.broadcasted_iota(I32, (BLOCK, BLOCK), 1)
    move = n == ((p >> 2) & 1) * 64 + (p >> 3) * 4 + (p & 3)
    return jnp.dot(rows, move.astype(F32), precision=lax.Precision.HIGHEST, preferred_element_type=F32)


def turn_kernel(place_ref, x_ref, ij_ref, cd_ref, out_ref):
    core, z = place_ref[0], place_ref[1]
    labels = jnp.broadcast_to(ij_ref[pl.ds(z, 1), :], (8, BLOCK)).astype(F32)
    labels = arrival(labels)[0:1, :].astype(I32)
    for j in range(CD_CORE // BLOCK):
        cols = slice(j * BLOCK, (j + 1) * BLOCK)
        cd = down(cd_ref[pl.ds(core * (CD_CORE // BLOCK) + j, 1), :])
        out_ref[cols, :] = jnp.where(cd == labels, jnp.transpose(x_ref[:, cols]), 0.0)


def table_kernel(round_ref, ij_ref, slot_ref, chosen_ref):
    ij = ij_ref[...]
    label = lax.broadcasted_iota(I32, (BLOCKS, LABELS, BLOCK), 1)
    same = (jnp.broadcast_to(ij[:, None, :], label.shape) == label).astype(F32)
    upto = lax.broadcasted_iota(I32, (BLOCK, BLOCK), 0) <= lax.broadcasted_iota(I32, (BLOCK, BLOCK), 1)
    count = jnp.dot(
        same.reshape(BLOCKS * LABELS, BLOCK).astype(BF16), upto.astype(BF16), preferred_element_type=F32
    ).reshape(BLOCKS, LABELS, BLOCK)
    excess = jnp.maximum(count[:, :, BLOCK - 1 :] - OWN, 0.0)
    before = jnp.zeros((1, LABELS, 1), F32)
    own_rows, over_rows = [], []
    for b in range(BLOCKS):
        rank = count[b : b + 1] - 1.0
        over = jnp.where(rank < OWN, -1.0, rank - OWN + before)
        own_rows.append(jnp.sum(rank * same[b : b + 1], axis=1) + b * 2 * OWN)
        over_rows.append(jnp.sum(over * same[b : b + 1], axis=1))
        before = before + excess[b : b + 1]
    own = jnp.concatenate(own_rows, axis=0).astype(I32)
    over = jnp.concatenate(over_rows, axis=0).astype(I32)
    shared = (over >> 4) * (2 * OWN) + OWN + (over & (OWN - 1))
    slots = jnp.where(over < 0, own, jnp.where(over < HALF, shared, over + HALF))
    slot_ref[...] = slots
    here = arrival(slots.astype(F32)).astype(I32) - round_ref[0] * SLOTS
    want = lax.broadcasted_iota(I32, (SLOTS, BLOCK), 0)
    for b in range(BLOCKS):
        chosen_ref[:, b * BLOCK : (b + 1) * BLOCK] = jnp.where(want == here[b : b + 1], 1.0, 0.0).astype(BF16)


def pack_kernel(x_ref, chosen_ref, packed_ref):
    @pl.when(pl.program_id(0) == 0)
    def _():
        packed_ref[...] = jnp.zeros_like(packed_ref)

    x = jnp.concatenate([x_ref[b] for b in range(STEP)], axis=1)
    hi = x.astype(BF16)
    lo = (x - hi.astype(F32)).astype(BF16)
    dims = (((1,), (1,)), ((), ()))
    packed_ref[...] += lax.dot_general(hi, chosen_ref[...], dims, preferred_element_type=F32) + lax.dot_general(
        lo, chosen_ref[...], dims, preferred_element_type=F32
    )


def panel_kernel(v_ref, cd_ref, ab_ref, hi_ref, lo_ref):
    for j in range(v_ref.shape[0] // BLOCK):
        cd = down(cd_ref[j : j + 1, :])
        for k in range(v_ref.shape[1] // BLOCK):
            at = (slice(j * BLOCK, (j + 1) * BLOCK), slice(k * BLOCK, (k + 1) * BLOCK))
            v = jnp.where(cd == ab_ref[:, at[1]], v_ref[at], 0.0)
            hi = v.astype(BF16)
            hi_ref[at] = hi
            lo_ref[at] = (v - hi.astype(F32)).astype(BF16)


def product(t, rows, hi_ref, lo_ref):
    t_hi = t.astype(BF16)
    t_lo = (t - t_hi.astype(F32)).astype(BF16)
    total = None
    for a, b in ((t_hi, hi_ref), (t_hi, lo_ref), (t_lo, hi_ref)):
        term = lax.dot_general(a, b[rows, :], (((0,), (0,)), ((), ())), preferred_element_type=F32)
        total = term if total is None else total + term
    return total


def mine_kernel(place_ref, t_ref, hi_ref, lo_ref, out_ref):
    rows = pl.ds(pl.multiple_of(place_ref[0] * CD_CORE, CD_CORE), CD_CORE)
    out_ref[...] = product(t_ref[...], rows, hi_ref, lo_ref)


def other_kernel(place_ref, t_ref, hi_ref, lo_ref, mine_ref, out_ref):
    rows = pl.ds(pl.multiple_of((1 - place_ref[0]) * CD_CORE, CD_CORE), CD_CORE)
    out_ref[...] = mine_ref[...] + product(t_ref[...], rows, hi_ref, lo_ref)


def sum_kernel(x_ref, own_ref, shared_ref):
    total = x_ref[0]
    for b in range(1, BLOCKS):
        total = total + x_ref[b]
    own_ref[...] = total[:OWN]
    shared_ref[...] = total[OWN:]


def spread(a, slots, labels, ab_ref, out_ref):
    chosen = jnp.where(lax.broadcasted_iota(I32, (a.shape[0], BLOCK), 0) == slots, 1.0, 0.0).astype(BF16)
    total = None
    for part in split3(a):
        term = lax.dot_general(chosen, part, (((0,), (0,)), ((), ())), preferred_element_type=F32)
        total = term if total is None else total + term
    ij = down(labels)
    for k in range(out_ref.shape[1] // BLOCK):
        cols = slice(k * BLOCK, (k + 1) * BLOCK)
        out_ref[:, cols] = jnp.where(ij == ab_ref[:, cols], 0.5 * total[:, cols], 0.0)


def first_kernel(place_ref, own_ref, y0_ref, y1_ref, y2_ref, y3_ref, slot_ref, ij_ref, ab_ref, out_ref):
    x, y = place_ref[2], place_ref[3]
    row = 4 * x + y
    slots = slot_ref[pl.ds(row, 1), :]
    block, inner = slots >> 5, slots & (2 * OWN - 1)
    away = (((block >> 2) - x) & 3) * 4 + ((block - y) & 3)
    place = jnp.where(inner < OWN, inner, inner + away * OWN)
    place = jnp.where(slots < SLOTS, place, -1)
    a = jnp.concatenate([own_ref[...], y0_ref[...], y1_ref[...], y2_ref[...], y3_ref[...]], axis=0)
    spread(a, place, ij_ref[pl.ds(row, 1), :], ab_ref, out_ref)


def later_kernel(place_ref, round_ref, a_ref, slot_ref, ij_ref, ab_ref, out_ref):
    row = 4 * place_ref[2] + place_ref[3]
    slots = slot_ref[pl.ds(row, 1), :] - round_ref[0] * SLOTS
    spread(a_ref[...], slots, ij_ref[pl.ds(row, 1), :], ab_ref, out_ref)


def from_next(value, axis, step):
    return lax.ppermute(value, axis, [((i + step) % 4, i) for i in range(4)])


def body(amplitudes, integrals, ij_irrep, cd_irrep, ab_irrep):
    smem = pl.BlockSpec(memory_space=pltpu.SMEM)
    vmem = pl.BlockSpec(memory_space=pltpu.VMEM)
    shape = jax.ShapeDtypeStruct
    place = jnp.stack([lax.axis_index(axis) for axis in ("core", "z", "x", "y")]).astype(I32)
    ij = ij_irrep.reshape(BLOCKS, BLOCK)
    cd = cd_irrep.reshape(-1, BLOCK)
    ab = ab_irrep.reshape(1, -1)
    cds, abs_ = integrals.shape
    row = ("x", "y")

    arrived = lax.all_to_all(amplitudes, ("x", "y", "core"), split_axis=1, concat_axis=0, tiled=True)
    turned = call(turn_kernel, shape((CD_CORE, BLOCK), F32), [smem, vmem, vmem, vmem])(place, arrived, ij, cd)
    line = lax.all_gather(turned, "z", axis=0, tiled=True).reshape(BLOCKS, CD_CORE, BLOCK)

    v_hi, v_lo = call(panel_kernel, [shape((cds, abs_), BF16)] * 2, [vmem] * 3, (2_000_000, 3_200_000))(integrals, cd, ab)

    def tables(number):
        return call(
            table_kernel,
            [shape((BLOCKS, BLOCK), I32), shape((SLOTS, BLOCKS * BLOCK), BF16)],
            [smem, vmem],
            (4_000_000, 2_100_000),
        )(number, ij)

    def products(chosen):
        packed = call(
            pack_kernel,
            shape((CD_CORE, SLOTS), F32),
            [
                pl.BlockSpec((STEP, CD_CORE, BLOCK), lambda i: (i, 0, 0)),
                pl.BlockSpec((SLOTS, STEP * BLOCK), lambda i: (0, i)),
            ],
            (1_600_000_000, 6_000_000),
            grid=(BLOCKS // STEP,),
            out_specs=pl.BlockSpec((CD_CORE, SLOTS), lambda i: (0, 0)),
        )(line, chosen)
        other = lax.ppermute(packed, "core", [(0, 1), (1, 0)])
        cost = (600_000_000, 3_000_000)
        full = shape((SLOTS, abs_), F32)
        mine = call(mine_kernel, full, [smem] + [vmem] * 3, cost)(place, packed, v_hi, v_lo)
        return call(other_kernel, full, [smem] + [vmem] * 4, cost)(place, other, v_hi, v_lo, mine)

    slots, chosen = tables(jnp.zeros((1,), I32))
    partial = lax.all_to_all(products(chosen), row, split_axis=0, concat_axis=0, tiled=True)
    piece = shape((OWN, abs_), F32)
    own, shared = call(sum_kernel, [piece, piece], [vmem])(partial.reshape(BLOCKS, 2 * OWN, abs_))
    along_y = jnp.concatenate([shared] + [from_next(shared, "y", j) for j in (1, 2, 3)], axis=0)
    parts = [along_y] + [from_next(along_y, "x", i) for i in (1, 2, 3)]
    out = call(first_kernel, shape((BLOCK, abs_), F32), [smem] + [vmem] * 8)(place, own, *parts, slots, ij, ab)
    rounds = (jnp.max(slots) >> 9) + 1

    def again(state):
        number, out = state
        _, chosen = tables(number[None])
        whole = lax.psum(products(chosen), row)
        more = call(later_kernel, shape((BLOCK, abs_), F32), [smem] * 2 + [vmem] * 4)(
            place, number[None], whole, slots, ij, ab
        )
        return number + 1, out + more

    return lax.while_loop(lambda state: state[0] < rounds, again, (jnp.int32(1), out))[1]


def solution(mesh):
    finer = Mesh(mesh.devices.reshape(4, 4, 16, 2), ("x", "y", "z", "core"))
    in_specs = (P(("z", "core", "x", "y"), None), P(("x", "y"), ("z", "core")), P(), P(("x", "y")), P(("z", "core")))
    out_specs = P(("x", "y"), ("z", "core"))
    return jax.shard_map(body, mesh=finer, in_specs=in_specs, out_specs=out_specs, check_vma=False)
```

time: 152 us -> 172 us (1.13)
  waiting for transfers between devices: 8.12 us -> 89.8 us
  blocking collectives: 103 us -> 22.5 us
  starting transfers between devices: 17.1 us -> 29.2 us
  Pallas kernels: 7.35 us -> 12.7 us
    all_gather x0 -> x1, waiting for transfers between devices: none -> 74.7 us  [body(): lax.all_gather(turned, 'z', axis=0, tiled=True)]
    all_gather x2 -> x0, blocking collectives: 58.9 us -> none  [the longest x1 34.9 us: products(): gathered = lax.all_gather(packed, 'z', axis=0, tiled=True)]
    all_to_all x2 -> x1, blocking collectives: 43.7 us -> 22.5 us  [body(): lax.all_to_all(products(chosen), row, split_axis=0, concat_axis=0, tiled=...]
    ppermute x1 -> x7, starting transfers between devices: 1.91 us -> 19.7 us  [the longest x6 17.7 us: from_next(): return lax.ppermute(value, axis, [((i + step) % 4, i) for i in range(4)])]
    ppermute x1 -> x7, waiting for transfers between devices: 1.82 us -> 8.91 us  [the longest x6 8.67 us: from_next(): return lax.ppermute(value, axis, [((i + step) % 4, i) for i in range(4)])]
    all_to_all x2 -> x1, starting transfers between devices: 15.2 us -> 9.53 us  [body(): lax.all_to_all(amplitudes, ('x', 'y', 'core'), split_axis=1, concat_axis=...]
    pallas_call x3 -> x6, Pallas kernels: 6.05 us -> 10.8 us  [the longest x1 4.43 us: products(): call(pack_kernel, shape((CD_CORE, SLOTS), F32), [pl.BlockSpec((STEP, CD_C...]
    all_to_all x2 -> x1, waiting for transfers between devices: 6.29 us -> 6.24 us  [body(): lax.all_to_all(amplitudes, ('x', 'y', 'core'), split_axis=1, concat_axis=...]
  transfers between devices with their start and end apart: 3 -> 9, of which waited for: 2 -> 6; matrix products, arithmetic and copies ran while one was open for 0% -> 0% of each run, Pallas kernels for 0% -> 2%
where the time goes in v2:
time: 172 us; the launch traced here: 171 us
  waiting for transfers between devices  89.8 us (52%)
  starting transfers between devices  29.2 us (17%)
  blocking collectives  22.5 us (13%)
  between operations  14.2 us (8%)
  Pallas kernels  12.7 us (7%)
    all_gather x1, waiting for transfers between devices, body(): lax.all_gather(turned, 'z', axis=0, tiled=True)  74.7 us
    all_to_all x1, blocking collectives, body(): lax.all_to_all(products(chosen), row, split_axis=0, concat_axis=0, tiled=...  22.5 us
    ppermute x6, starting transfers between devices, from_next(): return lax.ppermute(value, axis, [((i + step) % 4, i) for i in range(4)])  17.7 us
    all_to_all x1, starting transfers between devices, body(): lax.all_to_all(amplitudes, ('x', 'y', 'core'), split_axis=1, concat_axis=...  9.53 us
    ppermute x6, waiting for transfers between devices, from_next(): return lax.ppermute(value, axis, [((i + step) % 4, i) for i in range(4)])  8.67 us
    all_to_all x1, waiting for transfers between devices, body(): lax.all_to_all(amplitudes, ('x', 'y', 'core'), split_axis=1, concat_axis=...  6.24 us
    pallas_call x1, Pallas kernels, products(): call(pack_kernel, shape((CD_CORE, SLOTS), F32), [pl.BlockSpec((STEP, CD_C...  4.43 us
  transfers between devices with their start and end apart: 9, of which 6 were waited for; matrix products, arithmetic and copies ran while one was open for 0% of the time, Pallas kernels for 2%

profile of v2, /device:TPU:6, one launch (start us, length us, event | category | flops | bytes accessed | tf_op | source)
XLA Modules:
  0.0 170.8 jit_solution(15846914547492666169)
XLA Ops:
  6.5 9.5 %all-to-all-start = ((f32[4,32,384]{2,0,1:T(4,128)}), f32[4,32,384]{2,0,1:T(4,128)S(1)}, u32[]{:S(2)}, u32[]{:S(2)}) async-start(f32[4,32,384]{2,0,1:T(4,128)} %bitcast.24), calls=%async_computation | async-start | bytes 393216 | tf_op jit(solution)/shard_map/all_to_all | solution.py:185
  16.1 0.0 all-gather.2.cloned.1.call-start
  16.1 0.1 pad_add_fusion.place_ref
  16.2 6.2 %all-to-all-done = f32[4,32,384]{2,0,1:T(4,128)S(1)} async-done(((f32[4,32,384]{2,0,1:T(4,128)}), f32[4,32,384]{2,0,1:T(4,128)S(1)}, u32[]{:S(2)}, u32[]{:S(2)}) %all-to-all-start) | async-done | bytes 196640 | tf_op jit(solution)/shard_map/all_to_all | solution.py:185
  22.4 0.1 all_to_all.23.x_ref
  22.5 0.0 copy-start.2
  22.5 0.7 copy-done.2
  23.2 1.6 shard_map.55
  24.8 0.0 all-gather.2.cloned.1.call-update
  24.8 2.2 %shard_map.56 = (s32[16,128]{1,0:T(8,128)S(1)}, bf16[512,2048]{1,0:T(8,128)(2,1)S(1)}) custom-call(s32[1]{0:T(128)} %constant.25.clone.1.round_ref, s32[16,128]{1,0:T(8,128)} %bitcast.21), custom_call_target="tpu_custom_call" | custom-call | flops 4000000 | bytes 2100000 | tf_op jit(solution)/shard_map/pallas_call | solution.py:192
  27.0 74.7 %all-gather.2.cloned.1.call-done = f32[6144,128]{1,0:T(8,128)} async-done(((f32[384,128]{1,0:T(8,128)}), f32[6144,128]{1,0:T(8,128)}) %all-gather.2.cloned.1.call-update) | async-done | bytes 3145744 | tf_op jit(solution)/shard_map/all_gather | solution.py:187
  101.7 0.0 copy-start.1
  101.7 0.0 copy-start.3
  101.7 0.0 copy-start.6
  101.7 4.4 %shard_map.57.t_ref = f32[384,512]{1,0:T(8,128)S(1)} custom-call(f32[16,384,128]{2,1,0:T(8,128)} %bitcast.17, bf16[512,2048]{1,0:T(8,128)(2,1)S(1)} %get-tuple-element.65.chosen_ref), custom_call_target="tpu_custom_call" | custom-call | flops 1600000000 | bytes 6000000 | tf_op jit(solution)/shard_map/pallas_call | solution.py:200
  106.1 1.9 %collective-permute-start.1 = (f32[384,512]{1,0:T(8,128)S(1)}, f32[384,512]{1,0:T(8,128)S(1)}, u32[]{:S(2)}, u32[]{:S(2)}) collective-permute-start(f32[384,512]{1,0:T(8,128)S(1)} %shard_map.57.t_ref), channel_id=1, source_target_pairs={{0,1},{1,0},{2,3},{3,2},{4,5},{5,4},{6,7},{7,6},{8,9},{9,8},{10,11... | collective-permute-start | bytes 2359304 | tf_op jit(solution)/shard_map/ppermute | solution.py:211
  108.0 0.0 copy-done.1
  108.1 0.0 copy-done.3
  108.1 0.0 copy-done.6
  108.1 0.4 shard_map.58
  108.5 1.6 shard_map.59.mine_ref
  110.0 0.2 collective-permute-done.1.t_ref
  110.3 1.6 shard_map.60
  111.9 0.0 copy-start.5
  111.9 22.5 %all_to_all.28.x_ref = f32[16,32,512]{2,1,0:T(8,128)S(1)} all-to-all(f32[16,32,512]{2,1,0:T(8,128)S(1)} %bitcast.14), channel_id=1, replica_groups=mesh['x'=4,'y'=4,'z'=16,'core'=2] {'x','y'}, dimensions={0} | all-to-all | bytes 2097152 | tf_op jit(solution)/shard_map/all_to_all | solution.py:218
  134.4 0.1 shard_map.61
  134.5 2.5 %collective-permute-start.2 = (f32[16,512]{1,0:T(8,128)S(1)}, f32[16,512]{1,0:T(8,128)S(1)}, u32[]{:S(2)}, u32[]{:S(2)}) collective-permute-start(f32[16,512]{1,0:T(8,128)S(1)} %get-tuple-element.69), channel_id=1, source_target_pairs={{32,0},{64,32},{96,64},{0,96},{33,1},{65,33},{97,65},{1,97},{34,2}... | collective-permute-start | bytes 98312 | tf_op jit(solution)/shard_map/ppermute | solution.py:171
  137.0 3.9 %collective-permute-start.3 = (f32[16,512]{1,0:T(8,128)S(1)}, f32[16,512]{1,0:T(8,128)S(1)}, u32[]{:S(2)}, u32[]{:S(2)}) collective-permute-start(f32[16,512]{1,0:T(8,128)S(1)} %get-tuple-element.69), channel_id=1, source_target_pairs={{64,0},{96,32},{0,64},{32,96},{65,1},{97,33},{1,65},{33,97},{66,2}... | collective-permute-start | bytes 98312 | tf_op jit(solution)/shard_map/ppermute | solution.py:171
  141.0 1.9 %collective-permute-start.4 = (f32[16,512]{1,0:T(8,128)S(1)}, f32[16,512]{1,0:T(8,128)S(1)}, u32[]{:S(2)}, u32[]{:S(2)}) collective-permute-start(f32[16,512]{1,0:T(8,128)S(1)} %get-tuple-element.69), channel_id=1, source_target_pairs={{96,0},{0,32},{32,64},{64,96},{97,1},{1,33},{33,65},{65,97},{98,2}... | collective-permute-start | bytes 98312 | tf_op jit(solution)/shard_map/ppermute | solution.py:171
  142.9 0.0 collective-permute-done.2
  142.9 1.4 collective-permute-done.3
  144.4 3.6 %collective-permute-done.4 = f32[16,512]{1,0:T(8,128)S(1)} collective-permute-done((f32[16,512]{1,0:T(8,128)S(1)}, f32[16,512]{1,0:T(8,128)S(1)}, u32[]{:S(2)}, u32[]{:S(2)}) %collective-permute-start.4) | collective-permute-done | bytes 32800 | tf_op jit(solution)/shard_map/ppermute | solution.py:171
  148.0 2.3 %collective-permute-start.5 = (f32[64,512]{1,0:T(8,128)S(1)}, f32[64,512]{1,0:T(8,128)S(1)}, u32[]{:S(2)}, u32[]{:S(2)}) collective-permute-start(f32[64,512]{1,0:T(8,128)S(1)} %constant_dynamic-update-slice_fusion.y0_ref), channel_id=1, source_target_pairs={{128,0},{256,128},{384,256},{0,384},{129,1},{257,129},{385,257},{1... | collective-permute-start | bytes 393224 | tf_op jit(solution)/shard_map/ppermute | solution.py:171
  150.3 5.1 %collective-permute-start.6 = (f32[64,512]{1,0:T(8,128)S(1)}, f32[64,512]{1,0:T(8,128)S(1)}, u32[]{:S(2)}, u32[]{:S(2)}) collective-permute-start(f32[64,512]{1,0:T(8,128)S(1)} %constant_dynamic-update-slice_fusion.y0_ref), channel_id=1, source_target_pairs={{256,0},{384,128},{0,256},{128,384},{257,1},{385,129},{1,257},{129... | collective-permute-start | bytes 393224 | tf_op jit(solution)/shard_map/ppermute | solution.py:171
  155.4 2.0 %collective-permute-start.7 = (f32[64,512]{1,0:T(8,128)S(1)}, f32[64,512]{1,0:T(8,128)S(1)}, u32[]{:S(2)}, u32[]{:S(2)}) collective-permute-start(f32[64,512]{1,0:T(8,128)S(1)} %constant_dynamic-update-slice_fusion.y0_ref), channel_id=1, source_target_pairs={{384,0},{0,128},{128,256},{256,384},{385,1},{1,129},{129,257},{257... | collective-permute-start | bytes 393224 | tf_op jit(solution)/shard_map/ppermute | solution.py:171
  157.4 0.6 reduce_max.9
  158.6 0.0 collective-permute-done.5.y1_ref
  158.7 0.0 collective-permute-done.6.y2_ref
  158.7 3.6 %collective-permute-done.7.y3_ref = f32[64,512]{1,0:T(8,128)S(1)} collective-permute-done((f32[64,512]{1,0:T(8,128)S(1)}, f32[64,512]{1,0:T(8,128)S(1)}, u32[]{:S(2)}, u32[]{:S(2)}) %collective-permute-start.7) | collective-permute-done | bytes 131104 | tf_op jit(solution)/shard_map/ppermute | solution.py:171
  162.3 0.0 copy-done.5
  162.3 1.0 shard_map.62
  163.3 0.0 copy-start.4
  163.3 0.7 copy-done.4
  (5 shorter events, 0.0 us)
Async XLA Ops:
  6.5 15.9 %all-to-all-start = ((f32[4,32,384]{2,0,1:T(4,128)}), f32[4,32,384]{2,0,1:T(4,128)S(1)}, u32[]{:S(2)}, u32[]{:S(2)}) async-start(f32[4,32,384]{2,0,1:T(4,128)} %bitcast.24), calls=%async_computation | async-start | bytes 393216 | tf_op jit(solution)/shard_map/all_to_all | solution.py:185
  16.1 85.6 %all-gather.2.cloned.1.call-start = ((), (), s32[]{:S(2)}) async-start(), calls=%async_computation.2 | async-start | bytes 3342336 | tf_op jit(solution)/shard_map/all_gather | solution.py:187
  22.5 0.7 copy-start.2
  101.7 6.4 %copy-start.1 = (f32[768,512]{1,0:T(8,128)S(1)}, f32[768,512]{1,0:T(8,128)}, u32[]{:S(2)}) copy-start(f32[768,512]{1,0:T(8,128)} %v_ref.1) | copy-start | bytes 4718596
  101.7 6.4 %copy-start.3 = (s32[768]{0:T(1024)S(1)}, s32[768]{0:T(1024)}, u32[]{:S(2)}) copy-start(s32[768]{0:T(1024)} %param.10) | copy-start | bytes 9220
  101.7 6.4 %copy-start.6 = (s32[512]{0:T(512)S(1)}, s32[512]{0:T(512)}, u32[]{:S(2)}) copy-start(s32[512]{0:T(512)} %param.11) | copy-start | bytes 6148
  106.1 4.2 %collective-permute-start.1 = (f32[384,512]{1,0:T(8,128)S(1)}, f32[384,512]{1,0:T(8,128)S(1)}, u32[]{:S(2)}, u32[]{:S(2)}) collective-permute-start(f32[384,512]{1,0:T(8,128)S(1)} %shard_map.57.t_ref), channel_id=1, source_target_pairs={{0,1},{1,0},{2,3},{3,2},{4,5},{5,4},{6,7},{7,6},{8,9},{9,8},{10,11... | collective-permute-start | bytes 2359304 | tf_op jit(solution)/shard_map/ppermute | solution.py:211
  111.9 50.4 %copy-start.5 = (s32[2048]{0:T(1024)S(1)}, s32[2048]{0:T(1024)}, u32[]{:S(2)}) copy-start(s32[2048]{0:T(1024)} %param.9) | copy-start | bytes 24580
  134.5 8.4 %collective-permute-start.2 = (f32[16,512]{1,0:T(8,128)S(1)}, f32[16,512]{1,0:T(8,128)S(1)}, u32[]{:S(2)}, u32[]{:S(2)}) collective-permute-start(f32[16,512]{1,0:T(8,128)S(1)} %get-tuple-element.69), channel_id=1, source_target_pairs={{32,0},{64,32},{96,64},{0,96},{33,1},{65,33},{97,65},{1,97},{34,2}... | collective-permute-start | bytes 98312 | tf_op jit(solution)/shard_map/ppermute | solution.py:171
  137.0 7.3 %collective-permute-start.3 = (f32[16,512]{1,0:T(8,128)S(1)}, f32[16,512]{1,0:T(8,128)S(1)}, u32[]{:S(2)}, u32[]{:S(2)}) collective-permute-start(f32[16,512]{1,0:T(8,128)S(1)} %get-tuple-element.69), channel_id=1, source_target_pairs={{64,0},{96,32},{0,64},{32,96},{65,1},{97,33},{1,65},{33,97},{66,2}... | collective-permute-start | bytes 98312 | tf_op jit(solution)/shard_map/ppermute | solution.py:171
  141.0 7.0 %collective-permute-start.4 = (f32[16,512]{1,0:T(8,128)S(1)}, f32[16,512]{1,0:T(8,128)S(1)}, u32[]{:S(2)}, u32[]{:S(2)}) collective-permute-start(f32[16,512]{1,0:T(8,128)S(1)} %get-tuple-element.69), channel_id=1, source_target_pairs={{96,0},{0,32},{32,64},{64,96},{97,1},{1,33},{33,65},{65,97},{98,2}... | collective-permute-start | bytes 98312 | tf_op jit(solution)/shard_map/ppermute | solution.py:171
  148.0 10.7 %collective-permute-start.5 = (f32[64,512]{1,0:T(8,128)S(1)}, f32[64,512]{1,0:T(8,128)S(1)}, u32[]{:S(2)}, u32[]{:S(2)}) collective-permute-start(f32[64,512]{1,0:T(8,128)S(1)} %constant_dynamic-update-slice_fusion.y0_ref), channel_id=1, source_target_pairs={{128,0},{256,128},{384,256},{0,384},{129,1},{257,129},{385,257},{1... | collective-permute-start | bytes 393224 | tf_op jit(solution)/shard_map/ppermute | solution.py:171
  150.3 8.4 %collective-permute-start.6 = (f32[64,512]{1,0:T(8,128)S(1)}, f32[64,512]{1,0:T(8,128)S(1)}, u32[]{:S(2)}, u32[]{:S(2)}) collective-permute-start(f32[64,512]{1,0:T(8,128)S(1)} %constant_dynamic-update-slice_fusion.y0_ref), channel_id=1, source_target_pairs={{256,0},{384,128},{0,256},{128,384},{257,1},{385,129},{1,257},{129... | collective-permute-start | bytes 393224 | tf_op jit(solution)/shard_map/ppermute | solution.py:171
  155.4 6.9 %collective-permute-start.7 = (f32[64,512]{1,0:T(8,128)S(1)}, f32[64,512]{1,0:T(8,128)S(1)}, u32[]{:S(2)}, u32[]{:S(2)}) collective-permute-start(f32[64,512]{1,0:T(8,128)S(1)} %constant_dynamic-update-slice_fusion.y0_ref), channel_id=1, source_target_pairs={{384,0},{0,128},{128,256},{256,384},{385,1},{1,129},{129,257},{257... | collective-permute-start | bytes 393224 | tf_op jit(solution)/shard_map/ppermute | solution.py:171
  163.3 0.7 copy-start.4
Sparse Core Ops, SparseCore 0:
  24.9 76.7 all-gather.1

commit v3 on v2

--- a/solution.py
+++ b/solution.py
@@ -13,7 +13,7 @@
 HALF = BLOCKS * OWN
 SLOTS = 2 * HALF
 CD_CORE = 384
-STEP = 4
+CD_DEV = 24
 F32, BF16, I32 = jnp.float32, jnp.bfloat16, jnp.int32
 
 
@@ -46,14 +46,15 @@
     return jnp.dot(rows, move.astype(F32), precision=lax.Precision.HIGHEST, preferred_element_type=F32)
 
 
-def turn_kernel(place_ref, x_ref, ij_ref, cd_ref, out_ref):
+def turn_kernel(place_ref, x_ref, ij_ref, cd_ref, chosen_ref, hi_ref, out_ref):
     core, z = place_ref[0], place_ref[1]
     labels = jnp.broadcast_to(ij_ref[pl.ds(z, 1), :], (8, BLOCK)).astype(F32)
     labels = arrival(labels)[0:1, :].astype(I32)
     for j in range(CD_CORE // BLOCK):
         cols = slice(j * BLOCK, (j + 1) * BLOCK)
         cd = down(cd_ref[pl.ds(core * (CD_CORE // BLOCK) + j, 1), :])
-        out_ref[cols, :] = jnp.where(cd == labels, jnp.transpose(x_ref[:, cols]), 0.0)
+        x = x_ref[:, :, cols].reshape(BLOCK, BLOCK)
+        out_ref[cols, :] = jnp.where(cd == labels, jnp.transpose(x), 0.0)
 
 
 def table_kernel(round_ref, ij_ref, slot_ref, chosen_ref):
@@ -85,17 +86,14 @@
 
 
 def pack_kernel(x_ref, chosen_ref, packed_ref):
-    @pl.when(pl.program_id(0) == 0)
-    def _():
-        packed_ref[...] = jnp.zeros_like(packed_ref)
-
-    x = jnp.concatenate([x_ref[b] for b in range(STEP)], axis=1)
-    hi = x.astype(BF16)
-    lo = (x - hi.astype(F32)).astype(BF16)
-    dims = (((1,), (1,)), ((), ()))
-    packed_ref[...] += lax.dot_general(hi, chosen_ref[...], dims, preferred_element_type=F32) + lax.dot_general(
-        lo, chosen_ref[...], dims, preferred_element_type=F32
-    )
+    total = jnp.zeros((2 * CD_DEV, SLOTS), F32)
+    for b in range(0, BLOCKS, 2):
+        x = jnp.concatenate([x_ref[b], x_ref[b + 1]], axis=1)
+        hi = x.astype(BF16).astype(F32)
+        parts = jnp.concatenate([hi, x - hi], axis=0).astype(BF16)
+        chosen = chosen_ref[:, b * BLOCK : (b + 2) * BLOCK]
+        total += lax.dot_general(parts, chosen, (((1,), (1,)), ((), ())), preferred_element_type=F32)
+    packed_ref[...] = total[:CD_DEV] + total[CD_DEV:]
 
 
 def panel_kernel(v_ref, cd_ref, ab_ref, hi_ref, lo_ref):
@@ -129,12 +127,13 @@
     out_ref[...] = mine_ref[...] + product(t_ref[...], rows, hi_ref, lo_ref)
 
 
-def sum_kernel(x_ref, own_ref, shared_ref):
+def sum_kernel(x_ref, own_ref, copies_ref):
     total = x_ref[0]
     for b in range(1, BLOCKS):
         total = total + x_ref[b]
     own_ref[...] = total[:OWN]
-    shared_ref[...] = total[OWN:]
+    for b in range(BLOCKS):
+        copies_ref[b] = total[OWN:]
 
 
 def spread(a, slots, labels, ab_ref, out_ref):
@@ -149,44 +148,31 @@
         out_ref[:, cols] = jnp.where(ij == ab_ref[:, cols], 0.5 * total[:, cols], 0.0)
 
 
-def first_kernel(place_ref, own_ref, y0_ref, y1_ref, y2_ref, y3_ref, slot_ref, ij_ref, ab_ref, out_ref):
-    x, y = place_ref[2], place_ref[3]
-    row = 4 * x + y
+def first_kernel(place_ref, own_ref, shared_ref, slot_ref, ij_ref, ab_ref, out_ref):
+    row = place_ref[2]
     slots = slot_ref[pl.ds(row, 1), :]
     block, inner = slots >> 5, slots & (2 * OWN - 1)
-    away = (((block >> 2) - x) & 3) * 4 + ((block - y) & 3)
-    place = jnp.where(inner < OWN, inner, inner + away * OWN)
+    place = jnp.where(inner < OWN, inner, inner + block * OWN)
     place = jnp.where(slots < SLOTS, place, -1)
-    a = jnp.concatenate([own_ref[...], y0_ref[...], y1_ref[...], y2_ref[...], y3_ref[...]], axis=0)
-    spread(a, place, ij_ref[pl.ds(row, 1), :], ab_ref, out_ref)
+    spread(jnp.concatenate([own_ref[...], shared_ref[...]], axis=0), place, ij_ref[pl.ds(row, 1), :], ab_ref, out_ref)
 
 
 def later_kernel(place_ref, round_ref, a_ref, slot_ref, ij_ref, ab_ref, out_ref):
-    row = 4 * place_ref[2] + place_ref[3]
+    row = place_ref[2]
     slots = slot_ref[pl.ds(row, 1), :] - round_ref[0] * SLOTS
     spread(a_ref[...], slots, ij_ref[pl.ds(row, 1), :], ab_ref, out_ref)
-
-
-def from_next(value, axis, step):
-    return lax.ppermute(value, axis, [((i + step) % 4, i) for i in range(4)])
 
 
 def body(amplitudes, integrals, ij_irrep, cd_irrep, ab_irrep):
     smem = pl.BlockSpec(memory_space=pltpu.SMEM)
     vmem = pl.BlockSpec(memory_space=pltpu.VMEM)
+    anywhere = pl.BlockSpec(memory_space=pl.ANY)
     shape = jax.ShapeDtypeStruct
-    place = jnp.stack([lax.axis_index(axis) for axis in ("core", "z", "x", "y")]).astype(I32)
+    place = jnp.stack([lax.axis_index("core"), lax.axis_index("z"), lax.axis_index("row")]).astype(I32)
     ij = ij_irrep.reshape(BLOCKS, BLOCK)
     cd = cd_irrep.reshape(-1, BLOCK)
     ab = ab_irrep.reshape(1, -1)
     cds, abs_ = integrals.shape
-    row = ("x", "y")
-
-    arrived = lax.all_to_all(amplitudes, ("x", "y", "core"), split_axis=1, concat_axis=0, tiled=True)
-    turned = call(turn_kernel, shape((CD_CORE, BLOCK), F32), [smem, vmem, vmem, vmem])(place, arrived, ij, cd)
-    line = lax.all_gather(turned, "z", axis=0, tiled=True).reshape(BLOCKS, CD_CORE, BLOCK)
-
-    v_hi, v_lo = call(panel_kernel, [shape((cds, abs_), BF16)] * 2, [vmem] * 3, (2_000_000, 3_200_000))(integrals, cd, ab)
 
     def tables(number):
         return call(
@@ -196,37 +182,37 @@
             (4_000_000, 2_100_000),
         )(number, ij)
 
+    arrived = lax.all_to_all(
+        amplitudes.reshape(4, 2 * BLOCKS, CD_CORE), ("row", "core"), split_axis=1, concat_axis=0, tiled=False
+    )
+    slots, chosen = tables(jnp.zeros((1,), I32))
+    v_hi, v_lo = call(panel_kernel, [shape((cds, abs_), BF16)] * 2, [vmem] * 3, (2_000_000, 3_200_000))(integrals, cd, ab)
+    turned = call(turn_kernel, shape((CD_CORE, BLOCK), F32), [smem] + [vmem] * 3 + [anywhere] * 2)(
+        place, arrived, ij, cd, chosen, v_hi
+    )
+    mine = lax.all_to_all(turned, "z", split_axis=0, concat_axis=0, tiled=True).reshape(BLOCKS, CD_DEV, BLOCK)
+
     def products(chosen):
-        packed = call(
-            pack_kernel,
-            shape((CD_CORE, SLOTS), F32),
-            [
-                pl.BlockSpec((STEP, CD_CORE, BLOCK), lambda i: (i, 0, 0)),
-                pl.BlockSpec((SLOTS, STEP * BLOCK), lambda i: (0, i)),
-            ],
-            (1_600_000_000, 6_000_000),
-            grid=(BLOCKS // STEP,),
-            out_specs=pl.BlockSpec((CD_CORE, SLOTS), lambda i: (0, 0)),
-        )(line, chosen)
-        other = lax.ppermute(packed, "core", [(0, 1), (1, 0)])
+        packed = call(pack_kernel, shape((CD_DEV, SLOTS), F32), [vmem] * 2)(mine, chosen)
+        gathered = lax.all_gather(packed, "z", axis=0, tiled=True)
+        other = lax.ppermute(gathered, "core", [(0, 1), (1, 0)])
         cost = (600_000_000, 3_000_000)
         full = shape((SLOTS, abs_), F32)
-        mine = call(mine_kernel, full, [smem] + [vmem] * 3, cost)(place, packed, v_hi, v_lo)
-        return call(other_kernel, full, [smem] + [vmem] * 4, cost)(place, other, v_hi, v_lo, mine)
-
-    slots, chosen = tables(jnp.zeros((1,), I32))
-    partial = lax.all_to_all(products(chosen), row, split_axis=0, concat_axis=0, tiled=True)
-    piece = shape((OWN, abs_), F32)
-    own, shared = call(sum_kernel, [piece, piece], [vmem])(partial.reshape(BLOCKS, 2 * OWN, abs_))
-    along_y = jnp.concatenate([shared] + [from_next(shared, "y", j) for j in (1, 2, 3)], axis=0)
-    parts = [along_y] + [from_next(along_y, "x", i) for i in (1, 2, 3)]
-    out = call(first_kernel, shape((BLOCK, abs_), F32), [smem] + [vmem] * 8)(place, own, *parts, slots, ij, ab)
+        half = call(mine_kernel, full, [smem] + [vmem] * 3, cost)(place, gathered, v_hi, v_lo)
+        return call(other_kernel, full, [smem] + [vmem] * 4, cost)(place, other, v_hi, v_lo, half)
+
+    partial = lax.all_to_all(products(chosen), "row", split_axis=0, concat_axis=0, tiled=True)
+    own, copies = call(sum_kernel, [shape((OWN, abs_), F32), shape((BLOCKS, OWN, abs_), F32)], [vmem])(
+        partial.reshape(BLOCKS, 2 * OWN, abs_)
+    )
+    shared = lax.all_to_all(copies.reshape(HALF, abs_), "row", split_axis=0, concat_axis=0, tiled=True)
+    out = call(first_kernel, shape((BLOCK, abs_), F32), [smem] + [vmem] * 5)(place, own, shared, slots, ij, ab)
     rounds = (jnp.max(slots) >> 9) + 1
 
     def again(state):
         number, out = state
         _, chosen = tables(number[None])
-        whole = lax.psum(products(chosen), row)
+        whole = lax.psum(products(chosen), "row")
         more = call(later_kernel, shape((BLOCK, abs_), F32), [smem] * 2 + [vmem] * 4)(
             place, number[None], whole, slots, ij, ab
         )
@@ -236,7 +222,7 @@
 
 
 def solution(mesh):
-    finer = Mesh(mesh.devices.reshape(4, 4, 16, 2), ("x", "y", "z", "core"))
-    in_specs = (P(("z", "core", "x", "y"), None), P(("x", "y"), ("z", "core")), P(), P(("x", "y")), P(("z", "core")))
-    out_specs = P(("x", "y"), ("z", "core"))
+    finer = Mesh(mesh.devices.reshape(16, 16, 2), ("row", "z", "core"))
+    in_specs = (P(("z", "core", "row"), None), P("row", ("z", "core")), P(), P("row"), P(("z", "core")))
+    out_specs = P("row", ("z", "core"))
     return jax.shard_map(body, mesh=finer, in_specs=in_specs, out_specs=out_specs, check_vma=False)

time: 172 us -> 142 us (0.83)
  waiting for transfers between devices: 89.8 us -> 7.95 us
  blocking collectives: 22.5 us -> 86.2 us
  starting transfers between devices: 29.2 us -> 17 us
  local copies, waits for them, and re-layouts: 1.48 us -> 3.49 us
  Pallas kernels: 12.7 us -> 10.7 us
    all_gather x1 -> x0, waiting for transfers between devices: 74.7 us -> none  [body(): lax.all_gather(turned, 'z', axis=0, tiled=True)]
    all_gather x0 -> x1, blocking collectives: none -> 34.9 us  [products(): gathered = lax.all_gather(packed, 'z', axis=0, tiled=True)]
    all_to_all x1 -> x2, blocking collectives: 22.5 us -> 51.3 us  [the longest x1 29 us: body(): lax.all_to_all(turned, 'z', split_axis=0, concat_axis=0, tiled=True)]
    ppermute x7 -> x1, starting transfers between devices: 19.7 us -> 1.91 us  [products(): other = lax.ppermute(gathered, 'core', [(0, 1), (1, 0)])]
    ppermute x7 -> x1, waiting for transfers between devices: 8.91 us -> 0.69 us  [products(): other = lax.ppermute(gathered, 'core', [(0, 1), (1, 0)])]
    all_to_all x1 -> x2, starting transfers between devices: 9.53 us -> 15.1 us  [the longest x1 9.53 us: body(): lax.all_to_all(amplitudes.reshape(4, 2 * BLOCKS, CD_CORE), ('row', 'core'...]
    pallas_call x4, Pallas kernels: 7.03 us -> 3.49 us  [the longest x1 0.97 us: body(): call(first_kernel, shape((BLOCK, abs_), F32), [smem] + [vmem] * 5)]
    unnamed x15 -> x16, local copies, waits for them, and re-layouts: 1.41 us -> 3.49 us
  transfers between devices with their start and end apart: 9 -> 3, of which waited for: 6 -> 2; matrix products, arithmetic and copies ran while one was open for 0% -> 1% of each run, Pallas kernels for 2% -> 4%
where the time goes in v3:
time: 142 us; the launch traced here: 140 us
  blocking collectives  86.2 us (61%)
  starting transfers between devices  17 us (12%)
  between operations  14.2 us (10%)
  Pallas kernels  10.7 us (8%)
  waiting for transfers between devices  7.95 us (6%)
  local copies, waits for them, and re-layouts  3.49 us (2%)
    all_gather x1, blocking collectives, products(): gathered = lax.all_gather(packed, 'z', axis=0, tiled=True)  34.9 us
    all_to_all x1, blocking collectives, body(): lax.all_to_all(turned, 'z', split_axis=0, concat_axis=0, tiled=True)  29 us
    all_to_all x1, blocking collectives, body(): lax.all_to_all(products(chosen), 'row', split_axis=0, concat_axis=0, tile...  22.3 us
    all_to_all x1, starting transfers between devices, body(): lax.all_to_all(amplitudes.reshape(4, 2 * BLOCKS, CD_CORE), ('row', 'core'...  9.53 us
    all_to_all x1, waiting for transfers between devices, body(): lax.all_to_all(copies.reshape(HALF, abs_), 'row', split_axis=0, concat_ax...  7.23 us
    all_to_all x1, starting transfers between devices, body(): lax.all_to_all(copies.reshape(HALF, abs_), 'row', split_axis=0, concat_ax...  5.56 us
    unnamed x16, local copies, waits for them, and re-layouts  3.49 us
  transfers between devices with their start and end apart: 3, of which 2 were waited for; matrix products, arithmetic and copies ran while one was open for 1% of the time, Pallas kernels for 4%

profile of v3, /device:TPU:6, one launch (start us, length us, event | category | flops | bytes accessed | tf_op | source)
XLA Modules:
  0.0 140.3 jit_solution(18362107739506503981)
XLA Ops:
  6.5 9.5 %all-to-all-start = ((f32[1,4,32,384]{3,1,0,2:T(4,128)}), f32[1,4,32,384]{3,1,0,2:T(4,128)S(1)}, u32[]{:S(2)}, u32[]{:S(2)}) async-start(f32[1,4,32,384]{3,1,0,2:T(4,128)} %bitcast.28), calls=%async_computation | async-start | bytes 393216 | tf_op jit(solution)/shard_map/all_to_all | solution.py:185
  16.1 0.0 copy-start.1
  16.1 1.4 copy-done.1
  17.5 0.0 copy-start.2
  17.5 0.7 copy-done.2
  18.2 2.0 %shard_map.56 = (bf16[768,512]{1,0:T(8,128)(2,1)S(1)}, bf16[768,512]{1,0:T(8,128)(2,1)}) custom-call(f32[768,512]{1,0:T(8,128)S(1)} %copy-done.1, s32[6,128]{1,0:T(8,128)S(1)} %bitcast.22, s32[1,512]{1,0:T(1,128)} %bitcast.29), custom_call_target="tpu_custom_call" | custom-call | flops 2000000 | bytes 3200000 | tf_op jit(solution)/shard_map/pallas_call | solution.py:189
  20.2 2.2 %shard_map.55 = (s32[16,128]{1,0:T(8,128)S(1)}, bf16[512,2048]{1,0:T(8,128)(2,1)S(1)}) custom-call(s32[1]{0:T(128)} %constant.19.clone.1.round_ref, s32[16,128]{1,0:T(8,128)} %bitcast.24), custom_call_target="tpu_custom_call" | custom-call | flops 4000000 | bytes 2100000 | tf_op jit(solution)/shard_map/pallas_call | solution.py:178
  22.3 0.1 pad_add_fusion.place_ref
  22.4 0.0 all-to-all-done
  22.4 0.0 copy-start.3
  22.4 0.7 copy-done.3
  23.1 0.9 shard_map.57
  24.0 0.0 copy-start.4
  24.0 29.0 %all_to_all.41.x_ref = f32[16,24,128]{2,1,0:T(8,128)S(1)} all-to-all(f32[16,24,128]{2,1,0:T(8,128)S(1)} %bitcast.21), channel_id=1, replica_groups=mesh['row'=16,'z'=16,'core'=2] {'z'}, dimensions={0} | all-to-all | bytes 393216 | tf_op jit(solution)/shard_map/all_to_all | solution.py:193
  53.0 0.7 shard_map.58
  53.7 34.9 %all_gather.6.t_ref = f32[384,512]{1,0:T(8,128)S(1)} all-gather(f32[24,512]{1,0:T(8,128)S(1)} %shard_map.58), channel_id=1, replica_groups=mesh['row'=16,'z'=16,'core'=2] {'z'}, dimensions={0}, use_global_device_ids=true | all-gather | bytes 835584 | tf_op jit(solution)/shard_map/all_gather | solution.py:197
  88.6 1.9 %collective-permute-start.1 = (f32[384,512]{1,0:T(8,128)S(1)}, f32[384,512]{1,0:T(8,128)S(1)}, u32[]{:S(2)}, u32[]{:S(2)}) collective-permute-start(f32[384,512]{1,0:T(8,128)S(1)} %all_gather.6.t_ref), channel_id=1, source_target_pairs={{0,1},{1,0},{2,3},{3,2},{4,5},{5,4},{6,7},{7,6},{8,9},{9,8},{10,11... | collective-permute-start | bytes 2359304 | tf_op jit(solution)/shard_map/ppermute | solution.py:198
  90.6 0.0 copy-done.4
  90.6 1.5 %shard_map.59.mine_ref = f32[512,512]{1,0:T(8,128)S(1)} custom-call(s32[3]{0:T(128)S(1)} %pad_add_fusion.place_ref, f32[384,512]{1,0:T(8,128)S(1)} %all_gather.6.t_ref, bf16[768,512]{1,0:T(8,128)(2,1)S(1)} %get-tuple-element.162.hi_ref, bf16[768,512]{1,0:T(8,128)(2,1)S(1)} %copy-done.4), custom_call_target="tpu_custom_call" | custom-call | flops 600000000 | bytes 3000000 | tf_op jit(solution)/shard_map/pallas_call | solution.py:201
  92.1 0.7 collective-permute-done.1.t_ref
  92.8 1.5 %shard_map.60 = f32[512,512]{1,0:T(8,128)S(1)} custom-call(s32[3]{0:T(128)S(1)} %pad_add_fusion.place_ref, f32[384,512]{1,0:T(8,128)S(1)} %collective-permute-done.1.t_ref, bf16[768,512]{1,0:T(8,128)(2,1)S(1)} %get-tuple-element.162.hi_ref, bf16[768,512]{1,0:T(8,128)(2,1)S(1)} %copy-done.4, f32[512,512]{1,0:T(8,128)S(1)} %shard_map.59.mine_ref), custom_call_target="tpu_custom_call" | custom-call | flops 600000000 | bytes 3000000 | tf_op jit(solution)/shard_map/pallas_call | solution.py:202
  94.4 0.0 copy-start.7
  94.4 0.0 copy-start.8
  94.4 0.0 copy-start.5
  94.4 22.3 %all_to_all.42.x_ref = f32[16,32,512]{2,1,0:T(8,128)S(1)} all-to-all(f32[16,32,512]{2,1,0:T(8,128)S(1)} %bitcast.18), channel_id=1, replica_groups=mesh['row'=16,'z'=16,'core'=2] {'row'}, dimensions={0} | all-to-all | bytes 2097152 | tf_op jit(solution)/shard_map/all_to_all | solution.py:204
  116.7 0.9 shard_map.61
  117.6 5.6 %all-to-all-start.3 = ((f32[16,16,512]{2,1,0:T(8,128)}), f32[16,16,512]{2,1,0:T(8,128)S(1)}, u32[]{:S(2)}, u32[]{:S(2)}) async-start(f32[16,16,512]{2,1,0:T(8,128)} %get-tuple-element.69), calls=%async_computation.3 | async-start | bytes 1048576 | tf_op jit(solution)/shard_map/all_to_all | solution.py:208
  123.2 0.7 reduce_max.9
  124.5 7.2 %all-to-all-done.3 = f32[16,16,512]{2,1,0:T(8,128)S(1)} async-done(((f32[16,16,512]{2,1,0:T(8,128)}), f32[16,16,512]{2,1,0:T(8,128)S(1)}, u32[]{:S(2)}, u32[]{:S(2)}) %all-to-all-start.3) | async-done | bytes 524320 | tf_op jit(solution)/shard_map/all_to_all | solution.py:208
  131.7 0.0 copy-done.7
  131.7 0.0 copy-done.8
  131.7 1.0 shard_map.62
  132.7 0.0 copy-done.5
  132.7 0.0 copy-start.6
  132.7 0.7 copy-done.6
  (1 shorter events, 0.0 us)
Async XLA Ops:
  6.5 15.9 %all-to-all-start = ((f32[1,4,32,384]{3,1,0,2:T(4,128)}), f32[1,4,32,384]{3,1,0,2:T(4,128)S(1)}, u32[]{:S(2)}, u32[]{:S(2)}) async-start(f32[1,4,32,384]{3,1,0,2:T(4,128)} %bitcast.28), calls=%async_computation | async-start | bytes 393216 | tf_op jit(solution)/shard_map/all_to_all | solution.py:185
  16.1 1.4 %copy-start.1 = (f32[768,512]{1,0:T(8,128)S(1)}, f32[768,512]{1,0:T(8,128)}, u32[]{:S(2)}) copy-start(f32[768,512]{1,0:T(8,128)} %v_ref.1) | copy-start | bytes 4718596
  17.5 0.7 copy-start.2
  22.4 0.7 copy-start.3
  24.0 66.5 %copy-start.4 = (bf16[768,512]{1,0:T(8,128)(2,1)S(1)}, bf16[768,512]{1,0:T(8,128)(2,1)}, u32[]{:S(2)}) copy-start(bf16[768,512]{1,0:T(8,128)(2,1)} %get-tuple-element.163.lo_ref) | copy-start | bytes 2359300
  88.6 4.2 %collective-permute-start.1 = (f32[384,512]{1,0:T(8,128)S(1)}, f32[384,512]{1,0:T(8,128)S(1)}, u32[]{:S(2)}, u32[]{:S(2)}) collective-permute-start(f32[384,512]{1,0:T(8,128)S(1)} %all_gather.6.t_ref), channel_id=1, source_target_pairs={{0,1},{1,0},{2,3},{3,2},{4,5},{5,4},{6,7},{7,6},{8,9},{9,8},{10,11... | collective-permute-start | bytes 2359304 | tf_op jit(solution)/shard_map/ppermute | solution.py:198
  94.4 37.4 %copy-start.7 = (s32[2048]{0:T(1024)S(1)}, s32[2048]{0:T(1024)}, u32[]{:S(2)}) copy-start(s32[2048]{0:T(1024)} %param.9) | copy-start | bytes 24580
  94.4 37.3 %copy-start.8 = (s32[512]{0:T(512)S(1)}, s32[512]{0:T(512)}, u32[]{:S(2)}) copy-start(s32[512]{0:T(512)} %param.11) | copy-start | bytes 6148
  94.4 38.3 %copy-start.5 = (bf16[768,512]{1,0:T(8,128)(2,1)S(1)}, bf16[768,512]{1,0:T(8,128)(2,1)}, u32[]{:S(2)}) copy-start(bf16[768,512]{1,0:T(8,128)(2,1)} %get-tuple-element.163.lo_ref) | copy-start | bytes 2359300
  117.6 14.1 %all-to-all-start.3 = ((f32[16,16,512]{2,1,0:T(8,128)}), f32[16,16,512]{2,1,0:T(8,128)S(1)}, u32[]{:S(2)}, u32[]{:S(2)}) async-start(f32[16,16,512]{2,1,0:T(8,128)} %get-tuple-element.69), calls=%async_computation.3 | async-start | bytes 1048576 | tf_op jit(solution)/shard_map/all_to_all | solution.py:208
  132.7 0.7 copy-start.6

commit v4 on v0

v4 whole, which is shorter than its diff:
```python
import jax
import jax.numpy as jnp
from jax import lax
from jax.experimental import pallas as pl
from jax.experimental.pallas import tpu as pltpu
from jax.sharding import Mesh
from jax.sharding import PartitionSpec as P

BLOCK = 128
BLOCKS = 16
LABELS = 8
GROUP = 4
GROUPS = BLOCKS // GROUP
CAP = 160
PART = CAP // 4
SLOTS = GROUPS * CAP
CD_DEV = 96
WIDE = 128
F32, BF16, I32 = jnp.float32, jnp.bfloat16, jnp.int32


def call(kernel, out_shape, in_specs=None, cost=(1_000_000, 1_000_000), **kwargs):
    return pl.pallas_call(
        kernel,
        out_shape=out_shape,
        compiler_params=pltpu.CompilerParams(vmem_limit_bytes=48 * 1024 * 1024),
        cost_estimate=pl.CostEstimate(flops=cost[0], bytes_accessed=cost[1], transcendentals=0),
        **({} if in_specs is None else {"in_specs": in_specs}),
        **kwargs,
    )


def split3(x):
    hi = x.astype(BF16)
    rest = x - hi.astype(F32)
    mid = rest.astype(BF16)
    return hi, mid, (rest - mid.astype(F32)).astype(BF16)


def down(row):
    return jnp.transpose(jnp.broadcast_to(row, (BLOCK, BLOCK)))


def deal_kernel(x_ref, out_ref):
    rows = BLOCKS
    for z in range(GROUP):
        for core in range(2):
            for row in range(rows):
                start = ((row * GROUP + z) * 2 + core) * CD_DEV
                to = (z * 2 + core) * rows + row
                if start + WIDE <= x_ref.shape[1]:
                    out_ref[to] = x_ref[:, start : start + WIDE]
                else:
                    rest = jnp.zeros((x_ref.shape[0], WIDE - CD_DEV), F32)
                    out_ref[to] = jnp.concatenate([x_ref[:, start : start + CD_DEV], rest], axis=1)


def ranks(ij):
    label = lax.broadcasted_iota(I32, (BLOCKS, LABELS, BLOCK), 1)
    same = (jnp.broadcast_to(ij[:, None, :], label.shape) == label).astype(F32)
    upto = lax.broadcasted_iota(I32, (BLOCK, BLOCK), 0) <= lax.broadcasted_iota(I32, (BLOCK, BLOCK), 1)
    count = jnp.dot(
        same.reshape(BLOCKS * LABELS, BLOCK).astype(BF16), upto.astype(BF16), preferred_element_type=F32
    ).reshape(BLOCKS, LABELS, BLOCK)
    rows = []
    for b in range(BLOCKS):
        if b % GROUP == 0:
            before = jnp.zeros((1, LABELS, 1), F32)
        rows.append(jnp.sum((count[b : b + 1] - 1.0 + before) * same[b : b + 1], axis=1))
        before = before + count[b : b + 1, :, BLOCK - 1 :]
    return jnp.concatenate(rows, axis=0).astype(I32)


def table_kernel(place_ref, round_ref, ij_ref, cd_ref, rank_ref, chosen_ref, keep_ref):
    core, z, group = place_ref[0], place_ref[1], place_ref[2]
    rank_ref[...] = ranks(ij_ref[...])
    cd = cd_ref[pl.ds(z * 2 + core, 1), :]
    want = lax.broadcasted_iota(I32, (CAP, BLOCK), 0)
    for b in range(GROUP):
        at = slice(b * BLOCK, (b + 1) * BLOCK)
        here = rank_ref[pl.ds(group * GROUP + b, 1), :] - round_ref[0] * CAP
        chosen_ref[:, at] = jnp.where(want == here, 1.0, 0.0).astype(BF16)
        keep_ref[at, :] = jnp.where(down(ij_ref[pl.ds(group * GROUP + b, 1), :]) == cd, 1.0, 0.0)


def pack_kernel(x_ref, chosen_ref, keep_ref, first_ref, out_ref):
    total = jnp.zeros((CAP, WIDE), F32)
    for b in range(GROUP):
        at = slice(b * BLOCK, (b + 1) * BLOCK)
        x = x_ref[b * 32 : (b + 1) * 32].reshape(BLOCK, WIDE)
        x = jnp.where(keep_ref[at, :] > 0.0, x, 0.0)
        hi = x.astype(BF16)
        lo = (x - hi.astype(F32)).astype(BF16)
        for part in (hi, lo):
            total += jnp.dot(chosen_ref[:, at], part, preferred_element_type=F32)
    lane = lax.broadcasted_iota(I32, (PART, WIDE), 1)
    last = total[3 * PART :]
    for k in range(3):
        at = slice(k * PART, (k + 1) * PART)
        out_ref[at, :] = jnp.where(lane < CD_DEV, total[at], pltpu.roll(last, 96 - 32 * k, 1))


def panel_kernel(v_ref, cd_ref, ab_ref, hi_ref, lo_ref, kept_ref):
    for j in range(v_ref.shape[0] // BLOCK):
        cd = down(cd_ref[j : j + 1, :])
        for k in range(v_ref.shape[1] // BLOCK):
            at = (slice(j * BLOCK, (j + 1) * BLOCK), slice(k * BLOCK, (k + 1) * BLOCK))
            kept_ref[at] = jnp.where(cd == ab_ref[:, at[1]], v_ref[at], 0.0)
    nothing = jnp.zeros((WIDE - CD_DEV, v_ref.shape[1]), BF16)
    for core in range(2):
        for z in range(GROUP):
            start, to = (z * 2 + core) * CD_DEV, (core * GROUP + z) * WIDE
            v = kept_ref[start : start + CD_DEV, :]
            hi = v.astype(BF16)
            hi_ref[to : to + CD_DEV, :] = hi
            lo_ref[to : to + CD_DEV, :] = (v - hi.astype(F32)).astype(BF16)
            hi_ref[to + CD_DEV : to + WIDE, :] = nothing
            lo_ref[to + CD_DEV : to + WIDE, :] = nothing


def unfold(x):
    lane = lax.broadcasted_iota(I32, (PART, WIDE), 1)
    rolled = [pltpu.roll(x[k * PART : (k + 1) * PART], 32 + 32 * k, 1) for k in range(3)]
    last = jnp.where(lane < 32, rolled[0], jnp.where(lane < 64, rolled[1], rolled[2]))
    return jnp.concatenate([x, last], axis=0)


def product(t_ref, core, hi_ref, lo_ref):
    rows = pl.ds(pl.multiple_of(core * GROUP * WIDE, GROUP * WIDE), GROUP * WIDE)
    t = jnp.concatenate(
        [jnp.concatenate([unfold(t_ref[g * GROUP + z]) for z in range(GROUP)], axis=1) for g in range(GROUPS)], axis=0
    )
    t_hi = t.astype(BF16)
    t_lo = (t - t_hi.astype(F32)).astype(BF16)
    total = None
    for a, b in ((t_hi, hi_ref), (t_hi, lo_ref), (t_lo, hi_ref)):
        term = jnp.dot(a, b[rows, :], preferred_element_type=F32)
        total = term if total is None else total + term
    return total


def mine_kernel(place_ref, t_ref, hi_ref, lo_ref, out_ref):
    out_ref[...] = product(t_ref, place_ref[0], hi_ref, lo_ref)


def other_kernel(place_ref, t_ref, hi_ref, lo_ref, mine_ref, out_ref):
    out_ref[...] = mine_ref[...] + product(t_ref, 1 - place_ref[0], hi_ref, lo_ref)


def sum_kernel(x_ref, copies_ref):
    total = x_ref[0]
    for b in range(1, BLOCKS):
        total = total + x_ref[b]
    for b in range(copies_ref.shape[0]):
        copies_ref[b] = total


def spread(a, slots, labels, ab_ref, out_ref):
    chosen = jnp.where(lax.broadcasted_iota(I32, (a.shape[0], BLOCK), 0) == slots, 1.0, 0.0).astype(BF16)
    total = None
    for part in split3(a):
        term = lax.dot_general(chosen, part, (((0,), (0,)), ((), ())), preferred_element_type=F32)
        total = term if total is None else total + term
    ij = down(labels)
    for k in range(out_ref.shape[1] // BLOCK):
        cols = slice(k * BLOCK, (k + 1) * BLOCK)
        out_ref[:, cols] = jnp.where(ij == ab_ref[:, cols], 0.5 * total[:, cols], 0.0)


def expand_kernel(place_ref, round_ref, a_ref, rank_ref, ij_ref, ab_ref, out_ref):
    row = place_ref[3]
    slots = rank_ref[pl.ds(row, 1), :] - round_ref[0] * CAP
    spread(a_ref[...], slots, ij_ref[pl.ds(row, 1), :], ab_ref, out_ref)


def body(amplitudes, integrals, ij_irrep, cd_irrep, ab_irrep):
    smem = pl.BlockSpec(memory_space=pltpu.SMEM)
    vmem = pl.BlockSpec(memory_space=pltpu.VMEM)
    anywhere = pl.BlockSpec(memory_space=pl.ANY)
    shape = jax.ShapeDtypeStruct
    row = ("x", "y")
    place = jnp.stack([lax.axis_index(axis) for axis in ("core", "zl", "zh", row)]).astype(I32)
    ij = ij_irrep.reshape(BLOCKS, BLOCK)
    cd = cd_irrep.reshape(-1, BLOCK)
    cd_own = jnp.pad(cd_irrep.reshape(-1, CD_DEV), ((0, 0), (0, WIDE - CD_DEV)), constant_values=-1)
    ab = ab_irrep.reshape(1, -1)
    cds, abs_ = integrals.shape
    devices = 2 * GROUP * BLOCKS

    dealt = call(deal_kernel, shape((devices, 4, WIDE), F32), [vmem])(amplitudes)
    arrived = lax.all_to_all(dealt, ("zl", "core", "x", "y"), split_axis=0, concat_axis=0, tiled=True)
    v_hi, v_lo = call(
        panel_kernel,
        [shape((2 * GROUP * WIDE, abs_), BF16)] * 2,
        [vmem] * 3,
        (2_000_000, 3_200_000),
        scratch_shapes=[pltpu.VMEM((cds, abs_), F32)],
    )(integrals, cd, ab)

    def tables(number):
        return call(
            table_kernel,
            [shape((BLOCKS, BLOCK), I32), shape((CAP, GROUP * BLOCK), BF16), shape((GROUP * BLOCK, WIDE), F32)],
            [smem, smem, vmem, vmem],
        )(place, number, ij, cd_own)

    def products(chosen, keep):
        packed = call(pack_kernel, shape((3 * PART, WIDE), F32), [vmem] * 3 + [anywhere])(arrived, chosen, keep, v_hi)
        gathered = lax.all_gather(packed, ("zh", "zl"), axis=0, tiled=True)
        other = lax.ppermute(gathered, "core", [(0, 1), (1, 0)])
        pieces = (BLOCKS, 3 * PART, WIDE)
        cost = (1_000_000_000, 3_000_000)
        full = shape((SLOTS, abs_), F32)
        half = call(mine_kernel, full, [smem] + [vmem] * 3, cost)(place, gathered.reshape(pieces), v_hi, v_lo)
        return call(other_kernel, full, [smem] + [vmem] * 4, cost)(place, other.reshape(pieces), v_hi, v_lo, half)

    def expand(number, a):
        return call(expand_kernel, shape((BLOCK, abs_), F32), [smem] * 2 + [vmem] * 4)(place, number, a, rank, ij, ab)

    start = jnp.zeros((1,), I32)
    rank, chosen, keep = tables(start)
    partial = lax.all_to_all(products(chosen, keep), row, split_axis=0, concat_axis=0, tiled=True)
    copies = call(sum_kernel, shape((4, PART, abs_), F32), [vmem])(partial.reshape(BLOCKS, PART, abs_))
    out = expand(start, lax.all_to_all(copies.reshape(CAP, abs_), "y", split_axis=0, concat_axis=0, tiled=True))
    most = jnp.max(rank)

    def again(state):
        number, out = state
        _, chosen, keep = tables(number[None])
        whole = lax.psum(products(chosen, keep), row)
        mine = lax.dynamic_slice_in_dim(whole, lax.axis_index("x") * CAP, CAP, 0)
        return number + 1, out + expand(number[None], mine)

    return lax.while_loop(lambda state: state[0] * CAP <= most, again, (jnp.int32(1), out))[1]


def solution(mesh):
    finer = Mesh(mesh.devices.reshape(4, 4, 4, 4, 2), ("x", "y", "zh", "zl", "core"))
    col = ("zh", "zl", "core")
    in_specs = (P(col + ("x", "y"), None), P(("x", "y"), col), P(), P(("x", "y")), P(col))
    out_specs = P(("x", "y"), col)
    return jax.shard_map(body, mesh=finer, in_specs=in_specs, out_specs=out_specs, check_vma=False)
```

time: 215 us -> 122 us (0.57)
  waiting for transfers between devices: 168 us -> 13.6 us
  blocking collectives: 15.3 us -> 61.5 us
  starting transfers between devices: 0.04 us -> 18.2 us
  matrix products: 15.2 us -> 0 us
  Pallas kernels: 0 us -> 8.47 us
  local copies, waits for them, and re-layouts: 0.74 us -> 4.49 us
    reduce_scatter x1 -> x0, waiting for transfers between devices: 90 us -> none  [body(): lax.psum_scatter(partial_sum, 'row', scatter_dimension=0, tiled=True)]
    all_gather x1 -> x0, waiting for transfers between devices: 77.9 us -> none  [body(): lax.all_gather(regrouped, 'col', axis=0, tiled=True)]
    all_gather x0 -> x1, blocking collectives: none -> 38.6 us  [products(): gathered = lax.all_gather(packed, ('zh', 'zl'), axis=0, tiled=True)]
    all_to_all x0 -> x2, starting transfers between devices: none -> 16.3 us  [the longest x1 12.8 us: body(): lax.all_to_all(dealt, ('zl', 'core', 'x', 'y'), split_axis=0, concat_axis...]
    dot_general x1 -> x0, matrix products: 15.2 us -> none  [body(): jnp.dot(masked, panel, precision=lax.Precision.HIGHEST, preferred_element...]
    all_to_all x0 -> x2, waiting for transfers between devices: none -> 12.8 us  [the longest x1 6.5 us: body(): lax.all_to_all(copies.reshape(CAP, abs_), 'y', split_axis=0, concat_axis=...]
    pallas_call x0 -> x8, Pallas kernels: none -> 8.47 us  [the longest x1 1.77 us: products(): call(other_kernel, full, [smem] + [vmem] * 4, cost)]
    all_to_all x1, blocking collectives: 15.3 us -> 23 us  [body(): lax.all_to_all(products(chosen, keep), row, split_axis=0, concat_axis=0,...]
  transfers between devices with their start and end apart: 2 -> 3, of which waited for: 2 -> 3; matrix products, arithmetic and copies ran while one was open for 0% -> 1% of each run, Pallas kernels for 0% -> 3%
where the time goes in v4:
time: 122 us; the launch traced here: 121 us
  blocking collectives  61.5 us (50%)
  starting transfers between devices  18.2 us (15%)
  waiting for transfers between devices  13.6 us (11%)
  between operations  13.5 us (11%)
  Pallas kernels  8.47 us (7%)
  local copies, waits for them, and re-layouts  4.49 us (4%)
    all_gather x1, blocking collectives, products(): gathered = lax.all_gather(packed, ('zh', 'zl'), axis=0, tiled=True)  38.6 us
    all_to_all x1, blocking collectives, body(): lax.all_to_all(products(chosen, keep), row, split_axis=0, concat_axis=0,...  23 us
    all_to_all x1, starting transfers between devices, body(): lax.all_to_all(dealt, ('zl', 'core', 'x', 'y'), split_axis=0, concat_axis...  12.8 us
    all_to_all x1, waiting for transfers between devices, body(): lax.all_to_all(copies.reshape(CAP, abs_), 'y', split_axis=0, concat_axis=...  6.5 us
    all_to_all x1, waiting for transfers between devices, body(): lax.all_to_all(dealt, ('zl', 'core', 'x', 'y'), split_axis=0, concat_axis...  6.34 us
    unnamed x12, local copies, waits for them, and re-layouts  3.72 us
    all_to_all x1, starting transfers between devices, body(): lax.all_to_all(copies.reshape(CAP, abs_), 'y', split_axis=0, concat_axis=...  3.45 us
  transfers between devices with their start and end apart: 3, of which 3 were waited for; matrix products, arithmetic and copies ran while one was open for 1% of the time, Pallas kernels for 3%

profile of v4, /device:TPU:6, one launch (start us, length us, event | category | flops | bytes accessed | tf_op | source)
XLA Modules:
  0.0 120.9 jit_solution(6218471828660299568)
XLA Ops:
  6.5 0.0 copy-start.1
  6.5 0.9 copy-done.1
  7.5 1.0 shard_map.55
  8.4 12.8 %all-to-all-start = ((f32[128,4,128]{2,1,0:T(4,128)}), f32[128,4,128]{2,1,0:T(4,128)S(1)}, u32[]{:S(2)}, u32[]{:S(2)}) async-start(f32[128,4,128]{2,1,0:T(4,128)} %shard_map.55), calls=%async_computation | async-start | bytes 524288 | tf_op jit(solution)/shard_map/all_to_all | solution.py:191
  21.3 0.8 reshape.33
  22.0 0.1 pad_add_fusion.place_ref
  22.1 1.0 shard_map.56
  23.1 0.0 copy-start
  23.1 1.4 %copy-done = f32[768,512]{1,0:T(8,128)S(1)} copy-done((f32[768,512]{1,0:T(8,128)S(1)}, f32[768,512]{1,0:T(8,128)}, u32[]{:S(2)}) %copy-start) | copy-done | bytes 1572888
  24.5 0.0 copy-start.2
  24.5 0.7 copy-done.2
  25.2 1.0 shard_map.57
  26.2 6.3 %all-to-all-done.x_ref = f32[128,4,128]{2,1,0:T(4,128)S(1)} async-done(((f32[128,4,128]{2,1,0:T(4,128)}), f32[128,4,128]{2,1,0:T(4,128)S(1)}, u32[]{:S(2)}, u32[]{:S(2)}) %all-to-all-start) | async-done | bytes 262176 | tf_op jit(solution)/shard_map/all_to_all | solution.py:191
  32.6 0.3 shard_map.58
  32.9 38.6 %all_gather.6 = f32[1920,128]{1,0:T(8,128)S(1)} all-gather(f32[120,128]{1,0:T(8,128)S(1)} %shard_map.58), channel_id=1, replica_groups=mesh['x'=4,'y'=4,'zh'=4,'zl'=4,'core'=2] {'zh','zl'}, dimensions={0}, use_global_device_ids=true | all-gather | bytes 1044480 | tf_op jit(solution)/shard_map/all_gather | solution.py:209
  71.5 1.9 %collective-permute-start.1 = (f32[1920,128]{1,0:T(8,128)S(1)}, f32[1920,128]{1,0:T(8,128)S(1)}, u32[]{:S(2)}, u32[]{:S(2)}) collective-permute-start(f32[1920,128]{1,0:T(8,128)S(1)} %all_gather.6), channel_id=1, source_target_pairs={{0,1},{1,0},{2,3},{3,2},{4,5},{5,4},{6,7},{7,6},{8,9},{9,8},{10,11... | collective-permute-start | bytes 2949128 | tf_op jit(solution)/shard_map/ppermute | solution.py:210
  73.4 1.8 %shard_map.59.mine_ref = f32[640,512]{1,0:T(8,128)S(1)} custom-call(s32[4]{0:T(128)S(1)} %pad_add_fusion.place_ref, f32[16,120,128]{2,1,0:T(8,128)S(1)} %bitcast.23, bf16[1024,512]{1,0:T(8,128)(2,1)S(1)} %get-tuple-element.177.first_ref.hi_ref, bf16[1024,512]{1,0:T(8,128)(2,1)S(1)} %get-tuple-element.178.lo_ref), custom_call_target="tpu_custom_call" | custom-call | flops 1000000000 | bytes 3000000 | tf_op jit(solution)/shard_map/pallas_call | solution.py:214
  75.1 0.8 collective-permute-done.1
  75.9 1.8 %shard_map.60 = f32[640,512]{1,0:T(8,128)S(1)} custom-call(s32[4]{0:T(128)S(1)} %pad_add_fusion.place_ref, f32[16,120,128]{2,1,0:T(8,128)S(1)} %bitcast.25, bf16[1024,512]{1,0:T(8,128)(2,1)S(1)} %get-tuple-element.177.first_ref.hi_ref, bf16[1024,512]{1,0:T(8,128)(2,1)S(1)} %get-tuple-element.178.lo_ref, f32[640,512]{1,0:T(8,128)S(1)} %shard_map.59.mine_ref), custom_call_target="tpu_custom_call" | custom-call | flops 1000000000 | bytes 3000000 | tf_op jit(solution)/shard_map/pallas_call | solution.py:215
  77.7 23.0 %all_to_all.22.x_ref = f32[16,40,512]{2,1,0:T(8,128)S(1)} all-to-all(f32[16,40,512]{2,1,0:T(8,128)S(1)} %bitcast.22), channel_id=1, replica_groups=mesh['x'=4,'y'=4,'zh'=4,'zl'=4,'core'=2] {'x','y'}, dimensions={0} | all-to-all | bytes 2621440 | tf_op jit(solution)/shard_map/all_to_all | solution.py:222
  100.6 0.0 copy-start.4
  100.6 0.0 copy-start.5
  100.6 0.8 shard_map.61
  101.4 3.5 %all-to-all-start.2 = ((f32[4,40,512]{2,1,0:T(8,128)}), f32[4,40,512]{2,1,0:T(8,128)S(1)}, u32[]{:S(2)}, u32[]{:S(2)}) async-start(f32[4,40,512]{2,1,0:T(8,128)} %shard_map.61), calls=%async_computation.2 | async-start | bytes 655360 | tf_op jit(solution)/shard_map/all_to_all | solution.py:224
  104.9 0.6 reduce_max.9
  105.5 6.5 %all-to-all-done.2 = f32[4,40,512]{2,1,0:T(8,128)S(1)} async-done(((f32[4,40,512]{2,1,0:T(8,128)}), f32[4,40,512]{2,1,0:T(8,128)S(1)}, u32[]{:S(2)}, u32[]{:S(2)}) %all-to-all-start.2) | async-done | bytes 327712 | tf_op jit(solution)/shard_map/all_to_all | solution.py:224
  112.0 0.0 copy-done.4
  112.0 0.0 copy-done.5
  112.0 0.8 shard_map.62
  112.8 0.6 while.10
  113.4 0.0 copy-start.3
  113.4 0.7 copy-done.3
  (1 shorter events, 0.0 us)
Async XLA Ops:
  6.5 0.9 copy-start.1
  8.4 24.1 %all-to-all-start = ((f32[128,4,128]{2,1,0:T(4,128)}), f32[128,4,128]{2,1,0:T(4,128)S(1)}, u32[]{:S(2)}, u32[]{:S(2)}) async-start(f32[128,4,128]{2,1,0:T(4,128)} %shard_map.55), calls=%async_computation | async-start | bytes 524288 | tf_op jit(solution)/shard_map/all_to_all | solution.py:191
  23.1 1.4 %copy-start = (f32[768,512]{1,0:T(8,128)S(1)}, f32[768,512]{1,0:T(8,128)}, u32[]{:S(2)}) copy-start(f32[768,512]{1,0:T(8,128)} %v_ref.1) | copy-start | bytes 4718596
  24.5 0.7 copy-start.2
  71.5 4.4 %collective-permute-start.1 = (f32[1920,128]{1,0:T(8,128)S(1)}, f32[1920,128]{1,0:T(8,128)S(1)}, u32[]{:S(2)}, u32[]{:S(2)}) collective-permute-start(f32[1920,128]{1,0:T(8,128)S(1)} %all_gather.6), channel_id=1, source_target_pairs={{0,1},{1,0},{2,3},{3,2},{4,5},{5,4},{6,7},{7,6},{8,9},{9,8},{10,11... | collective-permute-start | bytes 2949128 | tf_op jit(solution)/shard_map/ppermute | solution.py:210
  100.6 11.4 %copy-start.4 = (s32[2048]{0:T(1024)S(1)}, s32[2048]{0:T(1024)}, u32[]{:S(2)}) copy-start(s32[2048]{0:T(1024)} %param.9) | copy-start | bytes 24580
  100.6 11.4 %copy-start.5 = (s32[512]{0:T(512)S(1)}, s32[512]{0:T(512)}, u32[]{:S(2)}) copy-start(s32[512]{0:T(512)} %param.11) | copy-start | bytes 6148
  101.4 10.6 %all-to-all-start.2 = ((f32[4,40,512]{2,1,0:T(8,128)}), f32[4,40,512]{2,1,0:T(8,128)S(1)}, u32[]{:S(2)}, u32[]{:S(2)}) async-start(f32[4,40,512]{2,1,0:T(8,128)} %shard_map.61), calls=%async_computation.2 | async-start | bytes 655360 | tf_op jit(solution)/shard_map/all_to_all | solution.py:224
  113.4 0.7 copy-start.3

commit v5 on v4

--- a/solution.py
+++ b/solution.py
@@ -147,12 +147,11 @@
     out_ref[...] = mine_ref[...] + product(t_ref, 1 - place_ref[0], hi_ref, lo_ref)
 
 
-def sum_kernel(x_ref, copies_ref):
+def sum_kernel(x_ref, out_ref):
     total = x_ref[0]
     for b in range(1, BLOCKS):
         total = total + x_ref[b]
-    for b in range(copies_ref.shape[0]):
-        copies_ref[b] = total
+    out_ref[...] = total
 
 
 def spread(a, slots, labels, ab_ref, out_ref):
@@ -214,22 +213,22 @@
         half = call(mine_kernel, full, [smem] + [vmem] * 3, cost)(place, gathered.reshape(pieces), v_hi, v_lo)
         return call(other_kernel, full, [smem] + [vmem] * 4, cost)(place, other.reshape(pieces), v_hi, v_lo, half)
 
-    def expand(number, a):
-        return call(expand_kernel, shape((BLOCK, abs_), F32), [smem] * 2 + [vmem] * 4)(place, number, a, rank, ij, ab)
+    def one_round(number, rank, chosen, keep):
+        partial = lax.all_to_all(products(chosen, keep), row, split_axis=0, concat_axis=0, tiled=True)
+        summed = call(sum_kernel, shape((PART, abs_), F32), [vmem])(partial.reshape(BLOCKS, PART, abs_))
+        summed = lax.all_gather(summed, "y", axis=0, tiled=True)
+        return call(expand_kernel, shape((BLOCK, abs_), F32), [smem] * 2 + [vmem] * 4)(
+            place, number, summed, rank, ij, ab
+        )
 
     start = jnp.zeros((1,), I32)
     rank, chosen, keep = tables(start)
-    partial = lax.all_to_all(products(chosen, keep), row, split_axis=0, concat_axis=0, tiled=True)
-    copies = call(sum_kernel, shape((4, PART, abs_), F32), [vmem])(partial.reshape(BLOCKS, PART, abs_))
-    out = expand(start, lax.all_to_all(copies.reshape(CAP, abs_), "y", split_axis=0, concat_axis=0, tiled=True))
+    out = one_round(start, rank, chosen, keep)
     most = jnp.max(rank)
 
     def again(state):
         number, out = state
-        _, chosen, keep = tables(number[None])
-        whole = lax.psum(products(chosen, keep), row)
-        mine = lax.dynamic_slice_in_dim(whole, lax.axis_index("x") * CAP, CAP, 0)
-        return number + 1, out + expand(number[None], mine)
+        return number + 1, out + one_round(number[None], *tables(number[None]))
 
     return lax.while_loop(lambda state: state[0] * CAP <= most, again, (jnp.int32(1), out))[1]
 

time: 122 us -> 113 us (0.926)
  between operations: 13.5 us -> 0.09 us
  waiting for transfers between devices: 13.6 us -> 25.6 us
  blocking collectives: 61.5 us -> 50.9 us
  starting transfers between devices: 18.2 us -> 20.6 us
    all_to_all x1 -> x0, blocking collectives: 23 us -> none  [body(): lax.all_to_all(products(chosen, keep), row, split_axis=0, concat_axis=0,...]
    all_gather x0 -> x1, blocking collectives: none -> 12.4 us  [one_round(): summed = lax.all_gather(summed, 'y', axis=0, tiled=True)]
    all_to_all x1, waiting for transfers between devices: 6.5 us -> 18.5 us  [one_round(): lax.all_to_all(products(chosen, keep), row, split_axis=0, concat_axis=0,...]
    all_to_all x1, starting transfers between devices: 3.45 us -> 5.89 us  [one_round(): lax.all_to_all(products(chosen, keep), row, split_axis=0, concat_axis=0,...]
where the time goes in v5:
time: 113 us; the launch traced here: 112 us
  blocking collectives  50.9 us (45%)
  waiting for transfers between devices  25.6 us (23%)
  starting transfers between devices  20.6 us (18%)
  Pallas kernels  9.52 us (8%)
  local copies, waits for them, and re-layouts  3.8 us (3%)
    all_gather x1, blocking collectives, products(): gathered = lax.all_gather(packed, ('zh', 'zl'), axis=0, tiled=True)  38.5 us
    all_to_all x1, waiting for transfers between devices, one_round(): lax.all_to_all(products(chosen, keep), row, split_axis=0, concat_axis=0,...  18.5 us
    all_to_all x1, starting transfers between devices, body(): lax.all_to_all(dealt, ('zl', 'core', 'x', 'y'), split_axis=0, concat_axis...  12.8 us
    all_gather x1, blocking collectives, one_round(): summed = lax.all_gather(summed, 'y', axis=0, tiled=True)  12.4 us
    all_to_all x1, waiting for transfers between devices, body(): lax.all_to_all(dealt, ('zl', 'core', 'x', 'y'), split_axis=0, concat_axis...  6.34 us
    all_to_all x1, starting transfers between devices, one_round(): lax.all_to_all(products(chosen, keep), row, split_axis=0, concat_axis=0,...  5.89 us
    unnamed x12, local copies, waits for them, and re-layouts  3.03 us
    pallas_call x1, Pallas kernels, products(): call(other_kernel, full, [smem] + [vmem] * 4, cost)  2.83 us
  transfers between devices with their start and end apart: 3, of which 3 were waited for; matrix products, arithmetic and copies ran while one was open for 1% of the time, Pallas kernels for 3%

profile of v5, /device:TPU:6, one launch (start us, length us, event | category | flops | bytes accessed | tf_op | source)
XLA Modules:
  0.0 111.8 jit_solution(15050283252883074269)
XLA Ops:
  0.0 0.0 copy-start.1
  0.0 0.9 copy-done.1
  0.9 1.0 shard_map.55
  1.9 12.8 %all-to-all-start.1 = ((f32[128,4,128]{2,1,0:T(4,128)}), f32[128,4,128]{2,1,0:T(4,128)S(1)}, u32[]{:S(2)}, u32[]{:S(2)}) async-start(f32[128,4,128]{2,1,0:T(4,128)} %shard_map.55), calls=%async_computation.1 | async-start | bytes 524288 | tf_op jit(solution)/shard_map/all_to_all | solution.py:190
  14.7 0.8 reshape.33
  15.5 0.1 pad_add_fusion.place_ref
  15.6 1.0 shard_map.56
  16.6 0.0 copy-start
  16.6 1.4 %copy-done = f32[768,512]{1,0:T(8,128)S(1)} copy-done((f32[768,512]{1,0:T(8,128)S(1)}, f32[768,512]{1,0:T(8,128)}, u32[]{:S(2)}) %copy-start) | copy-done | bytes 1572888
  18.0 0.0 copy-start.2
  18.0 0.7 copy-done.2
  18.7 1.0 shard_map.57
  19.7 6.3 %all-to-all-done.1.x_ref = f32[128,4,128]{2,1,0:T(4,128)S(1)} async-done(((f32[128,4,128]{2,1,0:T(4,128)}), f32[128,4,128]{2,1,0:T(4,128)S(1)}, u32[]{:S(2)}, u32[]{:S(2)}) %all-to-all-start.1) | async-done | bytes 262176 | tf_op jit(solution)/shard_map/all_to_all | solution.py:190
  26.0 0.0 copy-start.3
  26.0 0.3 shard_map.58
  26.4 38.5 %all_gather.12 = f32[1920,128]{1,0:T(8,128)S(1)} all-gather(f32[120,128]{1,0:T(8,128)S(1)} %shard_map.58), channel_id=1, replica_groups=mesh['x'=4,'y'=4,'zh'=4,'zl'=4,'core'=2] {'zh','zl'}, dimensions={0}, use_global_device_ids=true | all-gather | bytes 1044480 | tf_op jit(solution)/shard_map/all_gather | solution.py:208
  64.9 0.0 copy-done.3
  64.9 1.9 %collective-permute-start.1 = (f32[1920,128]{1,0:T(8,128)S(1)}, f32[1920,128]{1,0:T(8,128)S(1)}, u32[]{:S(2)}, u32[]{:S(2)}) collective-permute-start(f32[1920,128]{1,0:T(8,128)S(1)} %all_gather.12), channel_id=1, source_target_pairs={{0,1},{1,0},{2,3},{3,2},{4,5},{5,4},{6,7},{7,6},{8,9},{9,8},{10,11... | collective-permute-start | bytes 2949128 | tf_op jit(solution)/shard_map/ppermute | solution.py:209
  66.8 1.8 %shard_map.59.mine_ref = f32[640,512]{1,0:T(8,128)S(1)} custom-call(s32[4]{0:T(128)S(1)} %pad_add_fusion.place_ref, f32[16,120,128]{2,1,0:T(8,128)S(1)} %bitcast.24, bf16[1024,512]{1,0:T(8,128)(2,1)S(1)} %get-tuple-element.167.first_ref.hi_ref, bf16[1024,512]{1,0:T(8,128)(2,1)S(1)} %get-tuple-element.168.lo_ref), custom_call_target="tpu_custom_call" | custom-call | flops 1000000000 | bytes 3000000 | tf_op jit(solution)/shard_map/pallas_call | solution.py:213
  68.5 0.8 collective-permute-done.1
  69.3 2.8 %shard_map.60 = f32[640,512]{1,0:T(8,128)} custom-call(s32[4]{0:T(128)S(1)} %pad_add_fusion.place_ref, f32[16,120,128]{2,1,0:T(8,128)S(1)} %bitcast.25, bf16[1024,512]{1,0:T(8,128)(2,1)S(1)} %get-tuple-element.167.first_ref.hi_ref, bf16[1024,512]{1,0:T(8,128)(2,1)S(1)} %get-tuple-element.168.lo_ref, f32[640,512]{1,0:T(8,128)S(1)} %shard_map.59.mine_ref), custom_call_target="tpu_custom_call" | custom-call | flops 1000000000 | bytes 3000000 | tf_op jit(solution)/shard_map/pallas_call | solution.py:214
  72.1 5.9 %all-to-all-start.2 = ((f32[16,40,512]{2,1,0:T(8,128)}), f32[16,40,512]{2,1,0:T(8,128)S(1)}, u32[]{:S(2)}, u32[]{:S(2)}) async-start(f32[16,40,512]{2,1,0:T(8,128)} %bitcast.13), calls=%async_computation.2 | async-start | bytes 2621440 | tf_op jit(solution)/shard_map/all_to_all | solution.py:217
  78.0 0.0 copy-start.4
  78.0 0.0 copy-start.5
  78.1 0.6 reduce_max.9
  78.7 18.5 %all-to-all-done.2.x_ref = f32[16,40,512]{2,1,0:T(8,128)S(1)} async-done(((f32[16,40,512]{2,1,0:T(8,128)}), f32[16,40,512]{2,1,0:T(8,128)S(1)}, u32[]{:S(2)}, u32[]{:S(2)}) %all-to-all-start.2) | async-done | bytes 1310752 | tf_op jit(solution)/shard_map/all_to_all | solution.py:217
  97.2 0.1 shard_map.61
  97.2 12.4 %all_gather.13.a_ref = f32[160,512]{1,0:T(8,128)S(1)} all-gather(f32[40,512]{1,0:T(8,128)S(1)} %shard_map.61), channel_id=1, replica_groups=mesh['x'=4,'y'=4,'zh'=4,'zl'=4,'core'=2] {'y'}, dimensions={0}, use_global_device_ids=true | all-gather | bytes 409600 | tf_op jit(solution)/shard_map/all_gather | solution.py:219
  109.6 0.0 copy-done.4
  109.6 0.0 copy-done.5
  109.6 1.5 %shard_map.62 = f32[128,512]{1,0:T(8,128)} custom-call(s32[4]{0:T(128)S(1)} %pad_add_fusion.place_ref, s32[1]{0:T(128)} %constant.30.clone.1.round_ref, f32[160,512]{1,0:T(8,128)S(1)} %all_gather.13.a_ref, s32[16,128]{1,0:T(8,128)S(1)} %get-tuple-element.70.rank_ref, s32[16,128]{1,0:T(8,128)S(1)} %bitcast.28, s32[1,512]{1,0:T(1,128)S(1)} %bitcast.31), custom_call_target="tpu_custom_call" | custom-call | flops 1000000 | bytes 1000000 | tf_op jit(solution)/shard_map/pallas_call | solution.py:220
  111.2 0.6 while.10
  (1 shorter events, 0.0 us)
Async XLA Ops:
  0.0 0.9 copy-start.1
  1.9 24.1 %all-to-all-start.1 = ((f32[128,4,128]{2,1,0:T(4,128)}), f32[128,4,128]{2,1,0:T(4,128)S(1)}, u32[]{:S(2)}, u32[]{:S(2)}) async-start(f32[128,4,128]{2,1,0:T(4,128)} %shard_map.55), calls=%async_computation.1 | async-start | bytes 524288 | tf_op jit(solution)/shard_map/all_to_all | solution.py:190
  16.6 1.4 %copy-start = (f32[768,512]{1,0:T(8,128)S(1)}, f32[768,512]{1,0:T(8,128)}, u32[]{:S(2)}) copy-start(f32[768,512]{1,0:T(8,128)} %v_ref.1) | copy-start | bytes 4718596
  18.0 0.7 copy-start.2
  26.0 38.8 %copy-start.3 = (f32[128,4,128]{2,1,0:T(4,128)}, f32[128,4,128]{2,1,0:T(4,128)S(1)}, u32[]{:S(2)}) copy-start(f32[128,4,128]{2,1,0:T(4,128)S(1)} %all-to-all-done.1.x_ref) | copy-start | bytes 786436
  64.9 4.4 %collective-permute-start.1 = (f32[1920,128]{1,0:T(8,128)S(1)}, f32[1920,128]{1,0:T(8,128)S(1)}, u32[]{:S(2)}, u32[]{:S(2)}) collective-permute-start(f32[1920,128]{1,0:T(8,128)S(1)} %all_gather.12), channel_id=1, source_target_pairs={{0,1},{1,0},{2,3},{3,2},{4,5},{5,4},{6,7},{7,6},{8,9},{9,8},{10,11... | collective-permute-start | bytes 2949128 | tf_op jit(solution)/shard_map/ppermute | solution.py:209
  72.1 25.0 %all-to-all-start.2 = ((f32[16,40,512]{2,1,0:T(8,128)}), f32[16,40,512]{2,1,0:T(8,128)S(1)}, u32[]{:S(2)}, u32[]{:S(2)}) async-start(f32[16,40,512]{2,1,0:T(8,128)} %bitcast.13), calls=%async_computation.2 | async-start | bytes 2621440 | tf_op jit(solution)/shard_map/all_to_all | solution.py:217
  78.0 31.6 %copy-start.4 = (s32[2048]{0:T(1024)S(1)}, s32[2048]{0:T(1024)}, u32[]{:S(2)}) copy-start(s32[2048]{0:T(1024)} %param.9) | copy-start | bytes 24580
  78.0 31.6 %copy-start.5 = (s32[512]{0:T(512)S(1)}, s32[512]{0:T(512)}, u32[]{:S(2)}) copy-start(s32[512]{0:T(512)} %param.11) | copy-start | bytes 6148

commit v6 on v5

--- a/solution.py
+++ b/solution.py
@@ -68,12 +68,14 @@
             before = jnp.zeros((1, LABELS, 1), F32)
         rows.append(jnp.sum((count[b : b + 1] - 1.0 + before) * same[b : b + 1], axis=1))
         before = before + count[b : b + 1, :, BLOCK - 1 :]
-    return jnp.concatenate(rows, axis=0).astype(I32)
-
-
-def table_kernel(place_ref, round_ref, ij_ref, cd_ref, rank_ref, chosen_ref, keep_ref):
+    return jnp.concatenate(rows, axis=0)
+
+
+def table_kernel(place_ref, round_ref, ij_ref, cd_ref, most_ref, rank_ref, chosen_ref, keep_ref):
     core, z, group = place_ref[0], place_ref[1], place_ref[2]
-    rank_ref[...] = ranks(ij_ref[...])
+    rank = ranks(ij_ref[...])
+    most_ref[0] = jnp.max(rank).astype(I32)
+    rank_ref[...] = rank.astype(I32)
     cd = cd_ref[pl.ds(z * 2 + core, 1), :]
     want = lax.broadcasted_iota(I32, (CAP, BLOCK), 0)
     for b in range(GROUP):
@@ -147,11 +149,12 @@
     out_ref[...] = mine_ref[...] + product(t_ref, 1 - place_ref[0], hi_ref, lo_ref)
 
 
-def sum_kernel(x_ref, out_ref):
+def sum_kernel(x_ref, copies_ref):
     total = x_ref[0]
     for b in range(1, BLOCKS):
         total = total + x_ref[b]
-    out_ref[...] = total
+    for b in range(copies_ref.shape[0]):
+        copies_ref[b] = total
 
 
 def spread(a, slots, labels, ab_ref, out_ref):
@@ -199,8 +202,14 @@
     def tables(number):
         return call(
             table_kernel,
-            [shape((BLOCKS, BLOCK), I32), shape((CAP, GROUP * BLOCK), BF16), shape((GROUP * BLOCK, WIDE), F32)],
+            [
+                shape((1,), I32),
+                shape((BLOCKS, BLOCK), I32),
+                shape((CAP, GROUP * BLOCK), BF16),
+                shape((GROUP * BLOCK, WIDE), F32),
+            ],
             [smem, smem, vmem, vmem],
+            out_specs=[smem, vmem, vmem, vmem],
         )(place, number, ij, cd_own)
 
     def products(chosen, keep):
@@ -215,22 +224,21 @@
 
     def one_round(number, rank, chosen, keep):
         partial = lax.all_to_all(products(chosen, keep), row, split_axis=0, concat_axis=0, tiled=True)
-        summed = call(sum_kernel, shape((PART, abs_), F32), [vmem])(partial.reshape(BLOCKS, PART, abs_))
-        summed = lax.all_gather(summed, "y", axis=0, tiled=True)
+        copies = call(sum_kernel, shape((4, PART, abs_), F32), [vmem])(partial.reshape(BLOCKS, PART, abs_))
+        summed = lax.all_to_all(copies.reshape(CAP, abs_), "y", split_axis=0, concat_axis=0, tiled=True)
         return call(expand_kernel, shape((BLOCK, abs_), F32), [smem] * 2 + [vmem] * 4)(
             place, number, summed, rank, ij, ab
         )
 
     start = jnp.zeros((1,), I32)
-    rank, chosen, keep = tables(start)
+    most, rank, chosen, keep = tables(start)
     out = one_round(start, rank, chosen, keep)
-    most = jnp.max(rank)
 
     def again(state):
         number, out = state
-        return number + 1, out + one_round(number[None], *tables(number[None]))
-
-    return lax.while_loop(lambda state: state[0] * CAP <= most, again, (jnp.int32(1), out))[1]
+        return number + 1, out + one_round(number[None], *tables(number[None])[1:])
+
+    return lax.while_loop(lambda state: state[0] * CAP <= most[0], again, (jnp.int32(1), out))[1]
 
 
 def solution(mesh):

time: 113 us -> 109 us (0.965)
  waiting for transfers between devices: 25.6 us -> 13.6 us
  blocking collectives: 50.9 us -> 61.5 us
  starting transfers between devices: 20.6 us -> 18.2 us
    all_to_all x0 -> x1, blocking collectives: none -> 23 us  [one_round(): lax.all_to_all(products(chosen, keep), row, split_axis=0, concat_axis=0,...]
    all_gather x1 -> x0, blocking collectives: 12.4 us -> none  [one_round(): summed = lax.all_gather(summed, 'y', axis=0, tiled=True)]
    all_to_all x1, waiting for transfers between devices: 18.5 us -> 7.07 us  [one_round(): lax.all_to_all(copies.reshape(CAP, abs_), 'y', split_axis=0, concat_axis=...]
    all_to_all x1, starting transfers between devices: 5.89 us -> 3.45 us  [one_round(): lax.all_to_all(copies.reshape(CAP, abs_), 'y', split_axis=0, concat_axis=...]
    pallas_call x2, Pallas kernels: 1.06 us -> 2.35 us  [the longest x1 1.57 us: tables(): call(table_kernel, [shape((1,), I32), shape((BLOCKS, BLOCK), I32), shape(...]
  transfers between devices with their start and end apart: 3 -> 3, of which waited for: 3 -> 3; matrix products, arithmetic and copies ran while one was open for 1% -> 1% of each run, Pallas kernels for 3% -> 4%
where the time goes in v6:
time: 109 us; the launch traced here: 108 us
  blocking collectives  61.5 us (56%)
  starting transfers between devices  18.2 us (17%)
  waiting for transfers between devices  13.6 us (12%)
  Pallas kernels  9.04 us (8%)
  local copies, waits for them, and re-layouts  4.49 us (4%)
    all_gather x1, blocking collectives, products(): gathered = lax.all_gather(packed, ('zh', 'zl'), axis=0, tiled=True)  38.5 us
    all_to_all x1, blocking collectives, one_round(): lax.all_to_all(products(chosen, keep), row, split_axis=0, concat_axis=0,...  23 us
    all_to_all x1, starting transfers between devices, body(): lax.all_to_all(dealt, ('zl', 'core', 'x', 'y'), split_axis=0, concat_axis...  12.8 us
    all_to_all x1, waiting for transfers between devices, one_round(): lax.all_to_all(copies.reshape(CAP, abs_), 'y', split_axis=0, concat_axis=...  7.07 us
    all_to_all x1, waiting for transfers between devices, body(): lax.all_to_all(dealt, ('zl', 'core', 'x', 'y'), split_axis=0, concat_axis...  5.76 us
    unnamed x12, local copies, waits for them, and re-layouts  3.72 us
    all_to_all x1, starting transfers between devices, one_round(): lax.all_to_all(copies.reshape(CAP, abs_), 'y', split_axis=0, concat_axis=...  3.45 us
  transfers between devices with their start and end apart: 3, of which 3 were waited for; matrix products, arithmetic and copies ran while one was open for 1% of the time, Pallas kernels for 4%

profile of v6, /device:TPU:6, one launch (start us, length us, event | category | flops | bytes accessed | tf_op | source)
XLA Modules:
  0.0 107.7 jit_solution(3005542187701027038)
XLA Ops:
  0.0 0.0 copy-start.1
  0.0 0.9 copy-done.1
  0.9 1.0 shard_map.55
  1.9 12.8 %all-to-all-start.2 = ((f32[128,4,128]{2,1,0:T(4,128)}), f32[128,4,128]{2,1,0:T(4,128)S(1)}, u32[]{:S(2)}, u32[]{:S(2)}) async-start(f32[128,4,128]{2,1,0:T(4,128)} %shard_map.55), calls=%async_computation.2 | async-start | bytes 524288 | tf_op jit(solution)/shard_map/all_to_all | solution.py:193
  14.7 0.8 reshape.41
  15.5 0.1 pad_add_fusion.place_ref
  15.6 1.6 %shard_map.56 = (s32[1]{0:T(128)}, s32[16,128]{1,0:T(8,128)S(1)}, bf16[160,512]{1,0:T(8,128)(2,1)S(1)}, f32[512,128]{1,0:T(8,128)S(1)}) custom-call(s32[4]{0:T(128)S(1)} %pad_add_fusion.place_ref, s32[1]{0:T(128)} %constant.29.clone.1.round_ref, s32[16,128]{1,0:T(8,128)} %bitcast.37, s32[8,128]{1,0:T(8,128)S(1)} %pad.4.cd_ref), custom_call_target="tpu_custom_call" | custom-call | flops 1000000 | bytes 1000000 | tf_op jit(solution)/shard_map/pallas_call | solution.py:203
  17.1 0.0 copy-start
  17.2 1.4 %copy-done = f32[768,512]{1,0:T(8,128)S(1)} copy-done((f32[768,512]{1,0:T(8,128)S(1)}, f32[768,512]{1,0:T(8,128)}, u32[]{:S(2)}) %copy-start) | copy-done | bytes 1572888
  18.6 0.0 copy-start.2
  18.6 0.7 copy-done.2
  19.2 1.0 shard_map.57
  20.3 5.8 %all-to-all-done.2.x_ref = f32[128,4,128]{2,1,0:T(4,128)S(1)} async-done(((f32[128,4,128]{2,1,0:T(4,128)}), f32[128,4,128]{2,1,0:T(4,128)S(1)}, u32[]{:S(2)}, u32[]{:S(2)}) %all-to-all-start.2) | async-done | bytes 262176 | tf_op jit(solution)/shard_map/all_to_all | solution.py:193
  26.0 0.3 shard_map.58
  26.4 38.5 %all_gather.6 = f32[1920,128]{1,0:T(8,128)S(1)} all-gather(f32[120,128]{1,0:T(8,128)S(1)} %shard_map.58), channel_id=1, replica_groups=mesh['x'=4,'y'=4,'zh'=4,'zl'=4,'core'=2] {'zh','zl'}, dimensions={0}, use_global_device_ids=true | all-gather | bytes 1044480 | tf_op jit(solution)/shard_map/all_gather | solution.py:217
  64.9 1.9 %collective-permute-start.1 = (f32[1920,128]{1,0:T(8,128)S(1)}, f32[1920,128]{1,0:T(8,128)S(1)}, u32[]{:S(2)}, u32[]{:S(2)}) collective-permute-start(f32[1920,128]{1,0:T(8,128)S(1)} %all_gather.6), channel_id=1, source_target_pairs={{0,1},{1,0},{2,3},{3,2},{4,5},{5,4},{6,7},{7,6},{8,9},{9,8},{10,11... | collective-permute-start | bytes 2949128 | tf_op jit(solution)/shard_map/ppermute | solution.py:218
  66.8 1.8 %shard_map.59.mine_ref = f32[640,512]{1,0:T(8,128)S(1)} custom-call(s32[4]{0:T(128)S(1)} %pad_add_fusion.place_ref, f32[16,120,128]{2,1,0:T(8,128)S(1)} %bitcast.33, bf16[1024,512]{1,0:T(8,128)(2,1)S(1)} %get-tuple-element.169.first_ref.hi_ref, bf16[1024,512]{1,0:T(8,128)(2,1)S(1)} %get-tuple-element.170.lo_ref), custom_call_target="tpu_custom_call" | custom-call | flops 1000000000 | bytes 3000000 | tf_op jit(solution)/shard_map/pallas_call | solution.py:222
  68.6 0.8 collective-permute-done.1
  69.4 1.8 %shard_map.60 = f32[640,512]{1,0:T(8,128)S(1)} custom-call(s32[4]{0:T(128)S(1)} %pad_add_fusion.place_ref, f32[16,120,128]{2,1,0:T(8,128)S(1)} %bitcast.35, bf16[1024,512]{1,0:T(8,128)(2,1)S(1)} %get-tuple-element.169.first_ref.hi_ref, bf16[1024,512]{1,0:T(8,128)(2,1)S(1)} %get-tuple-element.170.lo_ref, f32[640,512]{1,0:T(8,128)S(1)} %shard_map.59.mine_ref), custom_call_target="tpu_custom_call" | custom-call | flops 1000000000 | bytes 3000000 | tf_op jit(solution)/shard_map/pallas_call | solution.py:223
  71.1 23.0 %all_to_all.39.x_ref = f32[16,40,512]{2,1,0:T(8,128)S(1)} all-to-all(f32[16,40,512]{2,1,0:T(8,128)S(1)} %bitcast.32), channel_id=1, replica_groups=mesh['x'=4,'y'=4,'zh'=4,'zl'=4,'core'=2] {'x','y'}, dimensions={0} | all-to-all | bytes 2621440 | tf_op jit(solution)/shard_map/all_to_all | solution.py:226
  94.1 0.0 copy-start.4
  94.1 0.0 copy-start.5
  94.1 0.8 shard_map.61
  94.9 3.5 %all-to-all-start.4 = ((f32[4,40,512]{2,1,0:T(8,128)}), f32[4,40,512]{2,1,0:T(8,128)S(1)}, u32[]{:S(2)}, u32[]{:S(2)}) async-start(f32[4,40,512]{2,1,0:T(8,128)} %shard_map.61), calls=%async_computation.4 | async-start | bytes 655360 | tf_op jit(solution)/shard_map/all_to_all | solution.py:228
  98.3 7.1 %all-to-all-done.4 = f32[4,40,512]{2,1,0:T(8,128)S(1)} async-done(((f32[4,40,512]{2,1,0:T(8,128)}), f32[4,40,512]{2,1,0:T(8,128)S(1)}, u32[]{:S(2)}, u32[]{:S(2)}) %all-to-all-start.4) | async-done | bytes 327712 | tf_op jit(solution)/shard_map/all_to_all | solution.py:228
  105.4 0.0 copy-done.4
  105.4 0.0 copy-done.5
  105.4 0.8 shard_map.62
  106.3 0.7 while.10
  107.0 0.0 copy-start.3
  107.0 0.7 copy-done.3
  (1 shorter events, 0.0 us)
Async XLA Ops:
  0.0 0.9 copy-start.1
  1.9 24.1 %all-to-all-start.2 = ((f32[128,4,128]{2,1,0:T(4,128)}), f32[128,4,128]{2,1,0:T(4,128)S(1)}, u32[]{:S(2)}, u32[]{:S(2)}) async-start(f32[128,4,128]{2,1,0:T(4,128)} %shard_map.55), calls=%async_computation.2 | async-start | bytes 524288 | tf_op jit(solution)/shard_map/all_to_all | solution.py:193
  17.1 1.4 %copy-start = (f32[768,512]{1,0:T(8,128)S(1)}, f32[768,512]{1,0:T(8,128)}, u32[]{:S(2)}) copy-start(f32[768,512]{1,0:T(8,128)} %v_ref.1) | copy-start | bytes 4718596
  18.6 0.7 copy-start.2
  64.9 4.4 %collective-permute-start.1 = (f32[1920,128]{1,0:T(8,128)S(1)}, f32[1920,128]{1,0:T(8,128)S(1)}, u32[]{:S(2)}, u32[]{:S(2)}) collective-permute-start(f32[1920,128]{1,0:T(8,128)S(1)} %all_gather.6), channel_id=1, source_target_pairs={{0,1},{1,0},{2,3},{3,2},{4,5},{5,4},{6,7},{7,6},{8,9},{9,8},{10,11... | collective-permute-start | bytes 2949128 | tf_op jit(solution)/shard_map/ppermute | solution.py:218
  94.1 11.3 %copy-start.4 = (s32[2048]{0:T(1024)S(1)}, s32[2048]{0:T(1024)}, u32[]{:S(2)}) copy-start(s32[2048]{0:T(1024)} %param.9) | copy-start | bytes 24580
  94.1 11.3 %copy-start.5 = (s32[512]{0:T(512)S(1)}, s32[512]{0:T(512)}, u32[]{:S(2)}) copy-start(s32[512]{0:T(512)} %param.11) | copy-start | bytes 6148
  94.9 10.5 %all-to-all-start.4 = ((f32[4,40,512]{2,1,0:T(8,128)}), f32[4,40,512]{2,1,0:T(8,128)S(1)}, u32[]{:S(2)}, u32[]{:S(2)}) async-start(f32[4,40,512]{2,1,0:T(8,128)} %shard_map.61), calls=%async_computation.4 | async-start | bytes 655360 | tf_op jit(solution)/shard_map/all_to_all | solution.py:228
  107.0 0.7 copy-start.3

commit v7 on v6

--- a/solution.py
+++ b/solution.py
@@ -19,11 +19,11 @@
 F32, BF16, I32 = jnp.float32, jnp.bfloat16, jnp.int32
 
 
-def call(kernel, out_shape, in_specs=None, cost=(1_000_000, 1_000_000), **kwargs):
+def call(kernel, out_shape, in_specs=None, cost=(1_000_000, 1_000_000), vmem_limit=48 * 1024 * 1024, **kwargs):
     return pl.pallas_call(
         kernel,
         out_shape=out_shape,
-        compiler_params=pltpu.CompilerParams(vmem_limit_bytes=48 * 1024 * 1024),
+        compiler_params=pltpu.CompilerParams(vmem_limit_bytes=vmem_limit),
         cost_estimate=pl.CostEstimate(flops=cost[0], bytes_accessed=cost[1], transcendentals=0),
         **({} if in_specs is None else {"in_specs": in_specs}),
         **kwargs,
@@ -41,18 +41,26 @@
     return jnp.transpose(jnp.broadcast_to(row, (BLOCK, BLOCK)))
 
 
-def deal_kernel(x_ref, out_ref):
-    rows = BLOCKS
-    for z in range(GROUP):
-        for core in range(2):
-            for row in range(rows):
-                start = ((row * GROUP + z) * 2 + core) * CD_DEV
-                to = (z * 2 + core) * rows + row
-                if start + WIDE <= x_ref.shape[1]:
-                    out_ref[to] = x_ref[:, start : start + WIDE]
-                else:
-                    rest = jnp.zeros((x_ref.shape[0], WIDE - CD_DEV), F32)
-                    out_ref[to] = jnp.concatenate([x_ref[:, start : start + CD_DEV], rest], axis=1)
+def deal_kernel(x_ref, out_ref, held_ref, done_ref):
+    pieces = 4
+    width = x_ref.shape[1] // pieces
+    copies = []
+    for k in range(pieces):
+        cols = slice(k * width, (k + 1) * width)
+        copies.append(pltpu.make_async_copy(x_ref.at[:, cols], held_ref.at[:, cols], done_ref.at[k]))
+        copies[-1].start()
+    rest = jnp.zeros((x_ref.shape[0], WIDE - CD_DEV), F32)
+    for k in range(pieces):
+        copies[k].wait()
+        for row in range(k * BLOCKS // pieces, (k + 1) * BLOCKS // pieces):
+            for z in range(GROUP):
+                for core in range(2):
+                    start = ((row * GROUP + z) * 2 + core) * CD_DEV
+                    to = (z * 2 + core) * BLOCKS + row
+                    if start + WIDE <= (k + 1) * width:
+                        out_ref[to] = held_ref[:, start : start + WIDE]
+                    else:
+                        out_ref[to] = jnp.concatenate([held_ref[:, start : start + CD_DEV], rest], axis=1)
 
 
 def ranks(ij):
@@ -102,7 +110,7 @@
         out_ref[at, :] = jnp.where(lane < CD_DEV, total[at], pltpu.roll(last, 96 - 32 * k, 1))
 
 
-def panel_kernel(v_ref, cd_ref, ab_ref, hi_ref, lo_ref, kept_ref):
+def panel_kernel(v_ref, cd_ref, ab_ref, out_ref, kept_ref):
     for j in range(v_ref.shape[0] // BLOCK):
         cd = down(cd_ref[j : j + 1, :])
         for k in range(v_ref.shape[1] // BLOCK):
@@ -111,13 +119,14 @@
     nothing = jnp.zeros((WIDE - CD_DEV, v_ref.shape[1]), BF16)
     for core in range(2):
         for z in range(GROUP):
-            start, to = (z * 2 + core) * CD_DEV, (core * GROUP + z) * WIDE
+            start = (z * 2 + core) * CD_DEV
             v = kept_ref[start : start + CD_DEV, :]
             hi = v.astype(BF16)
-            hi_ref[to : to + CD_DEV, :] = hi
-            lo_ref[to : to + CD_DEV, :] = (v - hi.astype(F32)).astype(BF16)
-            hi_ref[to + CD_DEV : to + WIDE, :] = nothing
-            lo_ref[to + CD_DEV : to + WIDE, :] = nothing
+            lo = (v - hi.astype(F32)).astype(BF16)
+            for k, part in enumerate((hi, lo, hi)):
+                to = ((core * 3 + k) * GROUP + z) * WIDE
+                out_ref[to : to + CD_DEV, :] = part
+                out_ref[to + CD_DEV : to + WIDE, :] = nothing
 
 
 def unfold(x):
@@ -127,26 +136,23 @@
     return jnp.concatenate([x, last], axis=0)
 
 
-def product(t_ref, core, hi_ref, lo_ref):
-    rows = pl.ds(pl.multiple_of(core * GROUP * WIDE, GROUP * WIDE), GROUP * WIDE)
+def product(t_ref, core, v_ref):
+    depth = 3 * GROUP * WIDE
+    rows = pl.ds(pl.multiple_of(core * depth, depth), depth)
     t = jnp.concatenate(
         [jnp.concatenate([unfold(t_ref[g * GROUP + z]) for z in range(GROUP)], axis=1) for g in range(GROUPS)], axis=0
     )
-    t_hi = t.astype(BF16)
-    t_lo = (t - t_hi.astype(F32)).astype(BF16)
-    total = None
-    for a, b in ((t_hi, hi_ref), (t_hi, lo_ref), (t_lo, hi_ref)):
-        term = jnp.dot(a, b[rows, :], preferred_element_type=F32)
-        total = term if total is None else total + term
-    return total
-
-
-def mine_kernel(place_ref, t_ref, hi_ref, lo_ref, out_ref):
-    out_ref[...] = product(t_ref, place_ref[0], hi_ref, lo_ref)
-
-
-def other_kernel(place_ref, t_ref, hi_ref, lo_ref, mine_ref, out_ref):
-    out_ref[...] = mine_ref[...] + product(t_ref, 1 - place_ref[0], hi_ref, lo_ref)
+    hi = t.astype(BF16)
+    lo = (t - hi.astype(F32)).astype(BF16)
+    return jnp.dot(jnp.concatenate([hi, hi, lo], axis=1), v_ref[rows, :], preferred_element_type=F32)
+
+
+def mine_kernel(place_ref, t_ref, v_ref, out_ref):
+    out_ref[...] = product(t_ref, place_ref[0], v_ref)
+
+
+def other_kernel(place_ref, t_ref, v_ref, mine_ref, out_ref):
+    out_ref[...] = mine_ref[...] + product(t_ref, 1 - place_ref[0], v_ref)
 
 
 def sum_kernel(x_ref, copies_ref):
@@ -189,11 +195,17 @@
     cds, abs_ = integrals.shape
     devices = 2 * GROUP * BLOCKS
 
-    dealt = call(deal_kernel, shape((devices, 4, WIDE), F32), [vmem])(amplitudes)
+    dealt = call(
+        deal_kernel,
+        shape((devices, 4, WIDE), F32),
+        [pl.BlockSpec(memory_space=pltpu.HBM)],
+        vmem_limit=None,
+        scratch_shapes=[pltpu.VMEM(amplitudes.shape, F32), pltpu.SemaphoreType.DMA((4,))],
+    )(amplitudes)
     arrived = lax.all_to_all(dealt, ("zl", "core", "x", "y"), split_axis=0, concat_axis=0, tiled=True)
-    v_hi, v_lo = call(
+    panel = call(
         panel_kernel,
-        [shape((2 * GROUP * WIDE, abs_), BF16)] * 2,
+        shape((6 * GROUP * WIDE, abs_), BF16),
         [vmem] * 3,
         (2_000_000, 3_200_000),
         scratch_shapes=[pltpu.VMEM((cds, abs_), F32)],
@@ -213,14 +225,14 @@
         )(place, number, ij, cd_own)
 
     def products(chosen, keep):
-        packed = call(pack_kernel, shape((3 * PART, WIDE), F32), [vmem] * 3 + [anywhere])(arrived, chosen, keep, v_hi)
+        packed = call(pack_kernel, shape((3 * PART, WIDE), F32), [vmem] * 3 + [anywhere])(arrived, chosen, keep, panel)
         gathered = lax.all_gather(packed, ("zh", "zl"), axis=0, tiled=True)
         other = lax.ppermute(gathered, "core", [(0, 1), (1, 0)])
         pieces = (BLOCKS, 3 * PART, WIDE)
         cost = (1_000_000_000, 3_000_000)
         full = shape((SLOTS, abs_), F32)
-        half = call(mine_kernel, full, [smem] + [vmem] * 3, cost)(place, gathered.reshape(pieces), v_hi, v_lo)
-        return call(other_kernel, full, [smem] + [vmem] * 4, cost)(place, other.reshape(pieces), v_hi, v_lo, half)
+        half = call(mine_kernel, full, [smem] + [vmem] * 2, cost)(place, gathered.reshape(pieces), panel)
+        return call(other_kernel, full, [smem] + [vmem] * 3, cost)(place, other.reshape(pieces), panel, half)
 
     def one_round(number, rank, chosen, keep):
         partial = lax.all_to_all(products(chosen, keep), row, split_axis=0, concat_axis=0, tiled=True)

time: 109 us -> 110 us (level)
  Pallas kernels: 9.04 us -> 12.5 us
  waiting for transfers between devices: 13.6 us -> 11.8 us
  local copies, waits for them, and re-layouts: 4.49 us -> 3.23 us
    pallas_call x4, Pallas kernels: 5.52 us -> 8.28 us  [the longest x1 2.73 us: body(): call(panel_kernel, shape((6 * GROUP * WIDE, abs_), BF16), [vmem] * 3, (20...]
    all_to_all x1, waiting for transfers between devices: 5.76 us -> 4.06 us  [body(): lax.all_to_all(dealt, ('zl', 'core', 'x', 'y'), split_axis=0, concat_axis...]
    unnamed x12 -> x14, local copies, waits for them, and re-layouts: 3.72 us -> 2.46 us
  transfers between devices with their start and end apart: 3 -> 3, of which waited for: 3 -> 3; matrix products, arithmetic and copies ran while one was open for 1% -> 1% of each run, Pallas kernels for 4% -> 6%
where the time goes in v7:
time: 110 us; the launch traced here: 109 us
  blocking collectives  61.9 us (56%)
  starting transfers between devices  18.2 us (17%)
  Pallas kernels  12.5 us (11%)
  waiting for transfers between devices  11.8 us (11%)
  local copies, waits for them, and re-layouts  3.23 us (3%)
    all_gather x1, blocking collectives, products(): gathered = lax.all_gather(packed, ('zh', 'zl'), axis=0, tiled=True)  38.7 us
    all_to_all x1, blocking collectives, one_round(): lax.all_to_all(products(chosen, keep), row, split_axis=0, concat_axis=0,...  23.2 us
    all_to_all x1, starting transfers between devices, body(): lax.all_to_all(dealt, ('zl', 'core', 'x', 'y'), split_axis=0, concat_axis...  12.8 us
    all_to_all x1, waiting for transfers between devices, one_round(): lax.all_to_all(copies.reshape(CAP, abs_), 'y', split_axis=0, concat_axis=...  6.99 us
    all_to_all x1, waiting for transfers between devices, body(): lax.all_to_all(dealt, ('zl', 'core', 'x', 'y'), split_axis=0, concat_axis...  4.06 us
    all_to_all x1, starting transfers between devices, one_round(): lax.all_to_all(copies.reshape(CAP, abs_), 'y', split_axis=0, concat_axis=...  3.45 us
    pallas_call x1, Pallas kernels, body(): call(panel_kernel, shape((6 * GROUP * WIDE, abs_), BF16), [vmem] * 3, (20...  2.73 us
    unnamed x14, local copies, waits for them, and re-layouts  2.46 us
  transfers between devices with their start and end apart: 3, of which 3 were waited for; matrix products, arithmetic and copies ran while one was open for 1% of the time, Pallas kernels for 6%

profile of v7, /device:TPU:6, one launch (start us, length us, event | category | flops | bytes accessed | tf_op | source)
XLA Modules:
  0.0 108.5 jit_solution(11386447587785103509)
XLA Ops:
  0.0 2.0 %shard_map.55 = f32[128,4,128]{2,1,0:T(4,128)} custom-call(f32[4,12288]{1,0:T(4,128)} %x_ref.1), custom_call_target="tpu_custom_call" | custom-call | flops 1000000 | bytes 1000000 | tf_op jit(solution)/shard_map/pallas_call | solution.py:198
  2.0 12.8 %all-to-all-start.2 = ((f32[128,4,128]{2,1,0:T(4,128)}), f32[128,4,128]{2,1,0:T(4,128)S(1)}, u32[]{:S(2)}, u32[]{:S(2)}) async-start(f32[128,4,128]{2,1,0:T(4,128)} %shard_map.55), calls=%async_computation.2 | async-start | bytes 524288 | tf_op jit(solution)/shard_map/all_to_all | solution.py:205
  14.9 0.8 reshape.41
  15.6 0.1 pad_add_fusion.place_ref
  15.7 1.6 %shard_map.56 = (s32[1]{0:T(128)}, s32[16,128]{1,0:T(8,128)S(1)}, bf16[160,512]{1,0:T(8,128)(2,1)S(1)}, f32[512,128]{1,0:T(8,128)S(1)}) custom-call(s32[4]{0:T(128)S(1)} %pad_add_fusion.place_ref, s32[1]{0:T(128)} %constant.29.clone.1.round_ref, s32[16,128]{1,0:T(8,128)} %bitcast.37, s32[8,128]{1,0:T(8,128)S(1)} %pad.4.cd_ref), custom_call_target="tpu_custom_call" | custom-call | flops 1000000 | bytes 1000000 | tf_op jit(solution)/shard_map/pallas_call | solution.py:215
  17.3 0.0 copy-start
  17.3 1.4 %copy-done = f32[768,512]{1,0:T(8,128)S(1)} copy-done((f32[768,512]{1,0:T(8,128)S(1)}, f32[768,512]{1,0:T(8,128)}, u32[]{:S(2)}) %copy-start) | copy-done | bytes 1572888
  18.7 0.0 copy-start.1
  18.7 0.7 copy-done.1
  19.4 2.7 %shard_map.57.first_ref.v_ref = bf16[3072,512]{1,0:T(8,128)(2,1)} custom-call(f32[768,512]{1,0:T(8,128)S(1)} %copy-done, s32[6,128]{1,0:T(8,128)S(1)} %bitcast.36, s32[1,512]{1,0:T(1,128)} %bitcast.40), custom_call_target="tpu_custom_call" | custom-call | flops 2000000 | bytes 3200000 | tf_op jit(solution)/shard_map/pallas_call | solution.py:206
  22.1 4.1 %all-to-all-done.2.x_ref = f32[128,4,128]{2,1,0:T(4,128)S(1)} async-done(((f32[128,4,128]{2,1,0:T(4,128)}), f32[128,4,128]{2,1,0:T(4,128)S(1)}, u32[]{:S(2)}, u32[]{:S(2)}) %all-to-all-start.2) | async-done | bytes 262176 | tf_op jit(solution)/shard_map/all_to_all | solution.py:205
  26.2 0.0 copy-start.4
  26.2 0.0 copy-start.2
  26.2 0.3 shard_map.58
  26.5 0.4 copy-done.4
  26.9 38.7 %all_gather.6 = f32[1920,128]{1,0:T(8,128)S(1)} all-gather(f32[120,128]{1,0:T(8,128)S(1)} %shard_map.58), channel_id=1, replica_groups=mesh['x'=4,'y'=4,'zh'=4,'zl'=4,'core'=2] {'zh','zl'}, dimensions={0}, use_global_device_ids=true | all-gather | bytes 1044480 | tf_op jit(solution)/shard_map/all_gather | solution.py:229
  65.5 1.9 %collective-permute-start.1 = (f32[1920,128]{1,0:T(8,128)S(1)}, f32[1920,128]{1,0:T(8,128)S(1)}, u32[]{:S(2)}, u32[]{:S(2)}) collective-permute-start(f32[1920,128]{1,0:T(8,128)S(1)} %all_gather.6), channel_id=1, source_target_pairs={{0,1},{1,0},{2,3},{3,2},{4,5},{5,4},{6,7},{7,6},{8,9},{9,8},{10,11... | collective-permute-start | bytes 2949128 | tf_op jit(solution)/shard_map/ppermute | solution.py:230
  67.4 0.0 copy-done.2
  67.5 1.8 %shard_map.59.mine_ref = f32[640,512]{1,0:T(8,128)S(1)} custom-call(s32[4]{0:T(128)S(1)} %pad_add_fusion.place_ref, f32[16,120,128]{2,1,0:T(8,128)S(1)} %bitcast.33, bf16[3072,512]{1,0:T(8,128)(2,1)S(1)} %copy-done.2), custom_call_target="tpu_custom_call" | custom-call | flops 1000000000 | bytes 3000000 | tf_op jit(solution)/shard_map/pallas_call | solution.py:234
  69.2 0.7 collective-permute-done.1
  70.0 1.8 %shard_map.60 = f32[640,512]{1,0:T(8,128)S(1)} custom-call(s32[4]{0:T(128)S(1)} %pad_add_fusion.place_ref, f32[16,120,128]{2,1,0:T(8,128)S(1)} %bitcast.35, bf16[3072,512]{1,0:T(8,128)(2,1)S(1)} %copy-done.2, f32[640,512]{1,0:T(8,128)S(1)} %shard_map.59.mine_ref), custom_call_target="tpu_custom_call" | custom-call | flops 1000000000 | bytes 3000000 | tf_op jit(solution)/shard_map/pallas_call | solution.py:235
  71.7 0.0 copy-start.3
  71.8 23.2 %all_to_all.39.x_ref = f32[16,40,512]{2,1,0:T(8,128)S(1)} all-to-all(f32[16,40,512]{2,1,0:T(8,128)S(1)} %bitcast.32), channel_id=1, replica_groups=mesh['x'=4,'y'=4,'zh'=4,'zl'=4,'core'=2] {'x','y'}, dimensions={0} | all-to-all | bytes 2621440 | tf_op jit(solution)/shard_map/all_to_all | solution.py:238
  95.0 0.0 copy-start.5
  95.0 0.0 copy-start.6
  95.0 0.8 shard_map.61
  95.8 3.5 %all-to-all-start.4 = ((f32[4,40,512]{2,1,0:T(8,128)}), f32[4,40,512]{2,1,0:T(8,128)S(1)}, u32[]{:S(2)}, u32[]{:S(2)}) async-start(f32[4,40,512]{2,1,0:T(8,128)} %shard_map.61), calls=%async_computation.4 | async-start | bytes 655360 | tf_op jit(solution)/shard_map/all_to_all | solution.py:240
  99.3 7.0 %all-to-all-done.4 = f32[4,40,512]{2,1,0:T(8,128)S(1)} async-done(((f32[4,40,512]{2,1,0:T(8,128)}), f32[4,40,512]{2,1,0:T(8,128)S(1)}, u32[]{:S(2)}, u32[]{:S(2)}) %all-to-all-start.4) | async-done | bytes 327712 | tf_op jit(solution)/shard_map/all_to_all | solution.py:240
  106.3 0.0 copy-done.5
  106.3 0.0 copy-done.6
  106.3 1.5 %shard_map.62 = f32[128,512]{1,0:T(8,128)} custom-call(s32[4]{0:T(128)S(1)} %pad_add_fusion.place_ref, s32[1]{0:T(128)} %constant.29.clone.1.round_ref, f32[160,512]{1,0:T(8,128)S(1)} %bitcast.34, s32[16,128]{1,0:T(8,128)S(1)} %get-tuple-element.62.rank_ref, s32[16,128]{1,0:T(8,128)S(1)} %bitcast.38, s32[1,512]{1,0:T(1,128)S(1)} %bitcast.41), custom_call_target="tpu_custom_call" | custom-call | flops 1000000 | bytes 1000000 | tf_op jit(solution)/shard_map/pallas_call | solution.py:241
  107.8 0.0 copy-done.3
  107.8 0.7 while.10
  (1 shorter events, 0.0 us)
Async XLA Ops:
  2.0 24.2 %all-to-all-start.2 = ((f32[128,4,128]{2,1,0:T(4,128)}), f32[128,4,128]{2,1,0:T(4,128)S(1)}, u32[]{:S(2)}, u32[]{:S(2)}) async-start(f32[128,4,128]{2,1,0:T(4,128)} %shard_map.55), calls=%async_computation.2 | async-start | bytes 524288 | tf_op jit(solution)/shard_map/all_to_all | solution.py:205
  17.3 1.4 %copy-start = (f32[768,512]{1,0:T(8,128)S(1)}, f32[768,512]{1,0:T(8,128)}, u32[]{:S(2)}) copy-start(f32[768,512]{1,0:T(8,128)} %v_ref.1) | copy-start | bytes 4718596
  18.7 0.7 copy-start.1
  26.2 0.7 copy-start.4
  26.2 41.3 %copy-start.2 = (bf16[3072,512]{1,0:T(8,128)(2,1)S(1)}, bf16[3072,512]{1,0:T(8,128)(2,1)}, u32[]{:S(2)}) copy-start(bf16[3072,512]{1,0:T(8,128)(2,1)} %shard_map.57.first_ref.v_ref) | copy-start | bytes 9437188
  65.5 4.4 %collective-permute-start.1 = (f32[1920,128]{1,0:T(8,128)S(1)}, f32[1920,128]{1,0:T(8,128)S(1)}, u32[]{:S(2)}, u32[]{:S(2)}) collective-permute-start(f32[1920,128]{1,0:T(8,128)S(1)} %all_gather.6), channel_id=1, source_target_pairs={{0,1},{1,0},{2,3},{3,2},{4,5},{5,4},{6,7},{7,6},{8,9},{9,8},{10,11... | collective-permute-start | bytes 2949128 | tf_op jit(solution)/shard_map/ppermute | solution.py:230
  71.7 36.1 %copy-start.3 = (bf16[3072,512]{1,0:T(8,128)(2,1)S(1)}, bf16[3072,512]{1,0:T(8,128)(2,1)}, u32[]{:S(2)}) copy-start(bf16[3072,512]{1,0:T(8,128)(2,1)} %shard_map.57.first_ref.v_ref) | copy-start | bytes 9437188
  95.0 11.3 %copy-start.5 = (s32[2048]{0:T(1024)S(1)}, s32[2048]{0:T(1024)}, u32[]{:S(2)}) copy-start(s32[2048]{0:T(1024)} %param.9) | copy-start | bytes 24580
  95.0 11.3 %copy-start.6 = (s32[512]{0:T(512)S(1)}, s32[512]{0:T(512)}, u32[]{:S(2)}) copy-start(s32[512]{0:T(512)} %param.11) | copy-start | bytes 6148
  95.8 10.5 %all-to-all-start.4 = ((f32[4,40,512]{2,1,0:T(8,128)}), f32[4,40,512]{2,1,0:T(8,128)S(1)}, u32[]{:S(2)}, u32[]{:S(2)}) async-start(f32[4,40,512]{2,1,0:T(8,128)} %shard_map.61), calls=%async_computation.4 | async-start | bytes 655360 | tf_op jit(solution)/shard_map/all_to_all | solution.py:240

commit v8 on v6

--- a/solution.py
+++ b/solution.py
@@ -14,6 +14,7 @@
 CAP = 160
 PART = CAP // 4
 SLOTS = GROUPS * CAP
+AWAY = (0, 3, -3, 6, -6)
 CD_DEV = 96
 WIDE = 128
 F32, BF16, I32 = jnp.float32, jnp.bfloat16, jnp.int32
@@ -100,6 +101,23 @@
     for k in range(3):
         at = slice(k * PART, (k + 1) * PART)
         out_ref[at, :] = jnp.where(lane < CD_DEV, total[at], pltpu.roll(last, 96 - 32 * k, 1))
+
+
+def join_kernel(*refs):
+    for k, ref in enumerate(refs[:-1]):
+        refs[-1][k] = ref[...]
+
+
+def order_kernel(place_ref, held_ref, above_ref, below_ref, far_ref, out_ref):
+    z = place_ref[2] * GROUP + place_ref[1]
+    for at, ref in ((z, held_ref), (z + 1, above_ref), (z - 1, below_ref)):
+        for k, away in enumerate(AWAY):
+            out_ref[(at + away) & (BLOCKS - 1)] = ref[k]
+    out_ref[(z + 8) & (BLOCKS - 1)] = far_ref[...]
+
+
+def from_z(value, step):
+    return lax.ppermute(value, ("zh", "zl"), [((z + step) % BLOCKS, z) for z in range(BLOCKS)])
 
 
 def panel_kernel(v_ref, cd_ref, ab_ref, hi_ref, lo_ref, kept_ref):
@@ -214,13 +232,16 @@
 
     def products(chosen, keep):
         packed = call(pack_kernel, shape((3 * PART, WIDE), F32), [vmem] * 3 + [anywhere])(arrived, chosen, keep, v_hi)
-        gathered = lax.all_gather(packed, ("zh", "zl"), axis=0, tiled=True)
+        pieces = (BLOCKS, 3 * PART, WIDE)
+        first = [packed] + [from_z(packed, away) for away in AWAY[1:]]
+        held = call(join_kernel, shape((len(AWAY),) + pieces[1:], F32), [vmem] * len(AWAY))(*first)
+        above, below, far = from_z(held, 1), from_z(held, -1), from_z(first[3], 2)
+        gathered = call(order_kernel, shape(pieces, F32), [smem] + [vmem] * 4)(place, held, above, below, far)
         other = lax.ppermute(gathered, "core", [(0, 1), (1, 0)])
-        pieces = (BLOCKS, 3 * PART, WIDE)
         cost = (1_000_000_000, 3_000_000)
         full = shape((SLOTS, abs_), F32)
-        half = call(mine_kernel, full, [smem] + [vmem] * 3, cost)(place, gathered.reshape(pieces), v_hi, v_lo)
-        return call(other_kernel, full, [smem] + [vmem] * 4, cost)(place, other.reshape(pieces), v_hi, v_lo, half)
+        half = call(mine_kernel, full, [smem] + [vmem] * 3, cost)(place, gathered, v_hi, v_lo)
+        return call(other_kernel, full, [smem] + [vmem] * 4, cost)(place, other, v_hi, v_lo, half)
 
     def one_round(number, rank, chosen, keep):
         partial = lax.all_to_all(products(chosen, keep), row, split_axis=0, concat_axis=0, tiled=True)

time: 109 us -> 119 us (1.092)
  blocking collectives: 61.5 us -> 22.9 us
  starting transfers between devices: 18.2 us -> 49.1 us
  waiting for transfers between devices: 13.6 us -> 30.6 us
    all_gather x1 -> x0, blocking collectives: 38.5 us -> none  [products(): gathered = lax.all_gather(packed, ('zh', 'zl'), axis=0, tiled=True)]
    ppermute x0 -> x7, starting transfers between devices: none -> 30.9 us  [from_z(): lax.ppermute(value, ('zh', 'zl'), [((z + step) % BLOCKS, z) for z in rang...]
    ppermute x0 -> x7, waiting for transfers between devices: none -> 17.1 us  [from_z(): lax.ppermute(value, ('zh', 'zl'), [((z + step) % BLOCKS, z) for z in rang...]
  transfers between devices with their start and end apart: 3 -> 10, of which waited for: 3 -> 7; matrix products, arithmetic and copies ran while one was open for 1% -> 1% of each run, Pallas kernels for 4% -> 4%
where the time goes in v8:
time: 119 us; the launch traced here: 118 us
  starting transfers between devices  49.1 us (41%)
  waiting for transfers between devices  30.6 us (26%)
  blocking collectives  22.9 us (19%)
  Pallas kernels  9.68 us (8%)
  local copies, waits for them, and re-layouts  4.49 us (4%)
    ppermute x7, starting transfers between devices, from_z(): lax.ppermute(value, ('zh', 'zl'), [((z + step) % BLOCKS, z) for z in rang...  30.9 us
    all_to_all x1, blocking collectives, one_round(): lax.all_to_all(products(chosen, keep), row, split_axis=0, concat_axis=0,...  22.9 us
    ppermute x7, waiting for transfers between devices, from_z(): lax.ppermute(value, ('zh', 'zl'), [((z + step) % BLOCKS, z) for z in rang...  17.1 us
    all_to_all x1, starting transfers between devices, body(): lax.all_to_all(dealt, ('zl', 'core', 'x', 'y'), split_axis=0, concat_axis...  12.8 us
    all_to_all x1, waiting for transfers between devices, one_round(): lax.all_to_all(copies.reshape(CAP, abs_), 'y', split_axis=0, concat_axis=...  6.99 us
    all_to_all x1, waiting for transfers between devices, body(): lax.all_to_all(dealt, ('zl', 'core', 'x', 'y'), split_axis=0, concat_axis...  5.76 us
    unnamed x12, local copies, waits for them, and re-layouts  3.72 us
    all_to_all x1, starting transfers between devices, one_round(): lax.all_to_all(copies.reshape(CAP, abs_), 'y', split_axis=0, concat_axis=...  3.45 us
  transfers between devices with their start and end apart: 10, of which 7 were waited for; matrix products, arithmetic and copies ran while one was open for 1% of the time, Pallas kernels for 4%

profile of v8, /device:TPU:6, one launch (start us, length us, event | category | flops | bytes accessed | tf_op | source)
XLA Modules:
  0.0 117.7 jit_solution(12326789087133737890)
XLA Ops:
  0.0 0.0 copy-start.1
  0.0 0.9 copy-done.1
  0.9 1.0 shard_map.55
  1.9 12.8 %all-to-all-start.2 = ((f32[128,4,128]{2,1,0:T(4,128)}), f32[128,4,128]{2,1,0:T(4,128)S(1)}, u32[]{:S(2)}, u32[]{:S(2)}) async-start(f32[128,4,128]{2,1,0:T(4,128)} %shard_map.55), calls=%async_computation.2 | async-start | bytes 524288 | tf_op jit(solution)/shard_map/all_to_all | solution.py:211
  14.7 0.8 reshape.29
  15.5 0.1 pad_add_fusion.place_ref
  15.6 1.6 %shard_map.56 = (s32[1]{0:T(128)}, s32[16,128]{1,0:T(8,128)S(1)}, bf16[160,512]{1,0:T(8,128)(2,1)S(1)}, f32[512,128]{1,0:T(8,128)S(1)}) custom-call(s32[4]{0:T(128)S(1)} %pad_add_fusion.place_ref, s32[1]{0:T(128)} %constant.29.clone.1.round_ref, s32[16,128]{1,0:T(8,128)} %bitcast.25, s32[8,128]{1,0:T(8,128)S(1)} %pad.4.cd_ref), custom_call_target="tpu_custom_call" | custom-call | flops 1000000 | bytes 1000000 | tf_op jit(solution)/shard_map/pallas_call | solution.py:221
  17.1 0.0 copy-start
  17.2 1.4 %copy-done = f32[768,512]{1,0:T(8,128)S(1)} copy-done((f32[768,512]{1,0:T(8,128)S(1)}, f32[768,512]{1,0:T(8,128)}, u32[]{:S(2)}) %copy-start) | copy-done | bytes 1572888
  18.6 0.0 copy-start.2
  18.6 0.7 copy-done.2
  19.2 1.0 shard_map.57
  20.3 5.8 %all-to-all-done.2.x_ref = f32[128,4,128]{2,1,0:T(4,128)S(1)} async-done(((f32[128,4,128]{2,1,0:T(4,128)}), f32[128,4,128]{2,1,0:T(4,128)S(1)}, u32[]{:S(2)}, u32[]{:S(2)}) %all-to-all-start.2) | async-done | bytes 262176 | tf_op jit(solution)/shard_map/all_to_all | solution.py:211
  26.0 0.3 shard_map.58.refs_0_
  26.4 10.8 %collective-permute-start.10 = (f32[120,128]{1,0:T(8,128)S(1)}, f32[120,128]{1,0:T(8,128)S(1)}, u32[]{:S(2)}, u32[]{:S(2)}) collective-permute-start(f32[120,128]{1,0:T(8,128)S(1)} %shard_map.58.refs_0_), channel_id=1, source_target_pairs={{12,0},{14,2},{16,4},{18,6},{20,8},{22,10},{24,12},{26,14},{28,16}... | collective-permute-start | bytes 184328 | tf_op jit(solution)/shard_map/ppermute | solution.py:120
  37.2 1.9 %collective-permute-start.11 = (f32[120,128]{1,0:T(8,128)S(1)}, f32[120,128]{1,0:T(8,128)S(1)}, u32[]{:S(2)}, u32[]{:S(2)}) collective-permute-start(f32[120,128]{1,0:T(8,128)S(1)} %shard_map.58.refs_0_), channel_id=1, source_target_pairs={{20,0},{22,2},{24,4},{26,6},{28,8},{30,10},{0,12},{2,14},{4,16},{6... | collective-permute-start | bytes 184328 | tf_op jit(solution)/shard_map/ppermute | solution.py:120
  39.1 8.1 %collective-permute-start.8 = (f32[120,128]{1,0:T(8,128)S(1)}, f32[120,128]{1,0:T(8,128)S(1)}, u32[]{:S(2)}, u32[]{:S(2)}) collective-permute-start(f32[120,128]{1,0:T(8,128)S(1)} %shard_map.58.refs_0_), channel_id=1, source_target_pairs={{6,0},{8,2},{10,4},{12,6},{14,8},{16,10},{18,12},{20,14},{22,16},{... | collective-permute-start | bytes 184328 | tf_op jit(solution)/shard_map/ppermute | solution.py:120
  47.2 1.9 %collective-permute-start.9 = (f32[120,128]{1,0:T(8,128)S(1)}, f32[120,128]{1,0:T(8,128)S(1)}, u32[]{:S(2)}, u32[]{:S(2)}) collective-permute-start(f32[120,128]{1,0:T(8,128)S(1)} %shard_map.58.refs_0_), channel_id=1, source_target_pairs={{26,0},{28,2},{30,4},{0,6},{2,8},{4,10},{6,12},{8,14},{10,16},{12,... | collective-permute-start | bytes 184328 | tf_op jit(solution)/shard_map/ppermute | solution.py:120
  49.1 0.0 collective-permute-done.10.refs_3_
  49.1 7.5 %collective-permute-done.11.refs_4_ = f32[120,128]{1,0:T(8,128)S(1)} collective-permute-done((f32[120,128]{1,0:T(8,128)S(1)}, f32[120,128]{1,0:T(8,128)S(1)}, u32[]{:S(2)}, u32[]{:S(2)}) %collective-permute-start.11) | collective-permute-done | bytes 61472 | tf_op jit(solution)/shard_map/ppermute | solution.py:120
  56.6 0.0 collective-permute-done.8.refs_1_
  56.6 3.6 %collective-permute-done.9.refs_2_ = f32[120,128]{1,0:T(8,128)S(1)} collective-permute-done((f32[120,128]{1,0:T(8,128)S(1)}, f32[120,128]{1,0:T(8,128)S(1)}, u32[]{:S(2)}, u32[]{:S(2)}) %collective-permute-start.9) | collective-permute-done | bytes 61472 | tf_op jit(solution)/shard_map/ppermute | solution.py:120
  60.3 1.9 %collective-permute-start.12 = (f32[5,120,128]{2,1,0:T(8,128)S(1)}, f32[5,120,128]{2,1,0:T(8,128)S(1)}, u32[]{:S(2)}, u32[]{:S(2)}) collective-permute-start(f32[5,120,128]{2,1,0:T(8,128)S(1)} %shard_map.59.held_ref), channel_id=1, source_target_pairs={{2,0},{4,2},{6,4},{8,6},{10,8},{12,10},{14,12},{16,14},{18,16},{20... | collective-permute-start | bytes 921608 | tf_op jit(solution)/shard_map/ppermute | solution.py:120
  62.2 3.9 %collective-permute-start.13 = (f32[5,120,128]{2,1,0:T(8,128)S(1)}, f32[5,120,128]{2,1,0:T(8,128)S(1)}, u32[]{:S(2)}, u32[]{:S(2)}) collective-permute-start(f32[5,120,128]{2,1,0:T(8,128)S(1)} %shard_map.59.held_ref), channel_id=1, source_target_pairs={{30,0},{0,2},{2,4},{4,6},{6,8},{8,10},{10,12},{12,14},{14,16},{16,... | collective-permute-start | bytes 921608 | tf_op jit(solution)/shard_map/ppermute | solution.py:120
  66.1 2.3 %collective-permute-start.14 = (f32[120,128]{1,0:T(8,128)S(1)}, f32[120,128]{1,0:T(8,128)S(1)}, u32[]{:S(2)}, u32[]{:S(2)}) collective-permute-start(f32[120,128]{1,0:T(8,128)S(1)} %collective-permute-done.10.refs_3_), channel_id=1, source_target_pairs={{4,0},{6,2},{8,4},{10,6},{12,8},{14,10},{16,12},{18,14},{20,16},{2... | collective-permute-start | bytes 184328 | tf_op jit(solution)/shard_map/ppermute | solution.py:120
  68.5 5.8 %collective-permute-done.14.far_ref = f32[120,128]{1,0:T(8,128)S(1)} collective-permute-done((f32[120,128]{1,0:T(8,128)S(1)}, f32[120,128]{1,0:T(8,128)S(1)}, u32[]{:S(2)}, u32[]{:S(2)}) %collective-permute-start.14) | collective-permute-done | bytes 61472 | tf_op jit(solution)/shard_map/ppermute | solution.py:120
  74.3 0.0 collective-permute-done.12.above_ref
  74.3 0.2 collective-permute-done.13.below_ref
  74.5 0.6 shard_map.60.t_ref
  75.1 1.9 %collective-permute-start.15 = (f32[16,120,128]{2,1,0:T(8,128)S(1)}, f32[16,120,128]{2,1,0:T(8,128)S(1)}, u32[]{:S(2)}, u32[]{:S(2)}) collective-permute-start(f32[16,120,128]{2,1,0:T(8,128)S(1)} %shard_map.60.t_ref), channel_id=1, source_target_pairs={{0,1},{1,0},{2,3},{3,2},{4,5},{5,4},{6,7},{7,6},{8,9},{9,8},{10,11... | collective-permute-start | bytes 2949128 | tf_op jit(solution)/shard_map/ppermute | solution.py:240
  77.0 1.8 %shard_map.61.mine_ref = f32[640,512]{1,0:T(8,128)S(1)} custom-call(s32[4]{0:T(128)S(1)} %pad_add_fusion.place_ref, f32[16,120,128]{2,1,0:T(8,128)S(1)} %shard_map.60.t_ref, bf16[1024,512]{1,0:T(8,128)(2,1)S(1)} %get-tuple-element.169.first_ref.hi_ref, bf16[1024,512]{1,0:T(8,128)(2,1)S(1)} %get-tuple-element.170.lo_ref), custom_call_target="tpu_custom_call" | custom-call | flops 1000000000 | bytes 3000000 | tf_op jit(solution)/shard_map/pallas_call | solution.py:243
  78.8 0.8 collective-permute-done.15.t_ref
  79.6 1.8 %shard_map.62 = f32[640,512]{1,0:T(8,128)S(1)} custom-call(s32[4]{0:T(128)S(1)} %pad_add_fusion.place_ref, f32[16,120,128]{2,1,0:T(8,128)S(1)} %collective-permute-done.15.t_ref, bf16[1024,512]{1,0:T(8,128)(2,1)S(1)} %get-tuple-element.169.first_ref.hi_ref, bf16[1024,512]{1,0:T(8,128)(2,1)S(1)} %get-tuple-element.170.lo_ref, f32[640,512]{1,0:T(8,128)S(1)} %shard_map.61.mine_ref), custom_call_target="tpu_custom_call" | custom-call | flops 1000000000 | bytes 3000000 | tf_op jit(solution)/shard_map/pallas_call | solution.py:244
  81.3 22.9 %all_to_all.39.x_ref = f32[16,40,512]{2,1,0:T(8,128)S(1)} all-to-all(f32[16,40,512]{2,1,0:T(8,128)S(1)} %bitcast.22), channel_id=1, replica_groups=mesh['x'=4,'y'=4,'zh'=4,'zl'=4,'core'=2] {'x','y'}, dimensions={0} | all-to-all | bytes 2621440 | tf_op jit(solution)/shard_map/all_to_all | solution.py:247
  104.2 0.0 copy-start.4
  104.2 0.0 copy-start.5
  104.2 0.8 shard_map.63
  105.0 3.5 %all-to-all-start.4 = ((f32[4,40,512]{2,1,0:T(8,128)}), f32[4,40,512]{2,1,0:T(8,128)S(1)}, u32[]{:S(2)}, u32[]{:S(2)}) async-start(f32[4,40,512]{2,1,0:T(8,128)} %shard_map.63), calls=%async_computation.4 | async-start | bytes 655360 | tf_op jit(solution)/shard_map/all_to_all | solution.py:249
  108.5 7.0 %all-to-all-done.4 = f32[4,40,512]{2,1,0:T(8,128)S(1)} async-done(((f32[4,40,512]{2,1,0:T(8,128)}), f32[4,40,512]{2,1,0:T(8,128)S(1)}, u32[]{:S(2)}, u32[]{:S(2)}) %all-to-all-start.4) | async-done | bytes 327712 | tf_op jit(solution)/shard_map/all_to_all | solution.py:249
  115.5 0.0 copy-done.4
  115.5 0.0 copy-done.5
  115.5 0.8 shard_map.64
  116.3 0.6 while.10
  117.0 0.0 copy-start.3
  117.0 0.7 copy-done.3
  (2 shorter events, 0.0 us)
Async XLA Ops:
  0.0 0.9 copy-start.1
  1.9 24.1 %all-to-all-start.2 = ((f32[128,4,128]{2,1,0:T(4,128)}), f32[128,4,128]{2,1,0:T(4,128)S(1)}, u32[]{:S(2)}, u32[]{:S(2)}) async-start(f32[128,4,128]{2,1,0:T(4,128)} %shard_map.55), calls=%async_computation.2 | async-start | bytes 524288 | tf_op jit(solution)/shard_map/all_to_all | solution.py:211
  17.1 1.4 %copy-start = (f32[768,512]{1,0:T(8,128)S(1)}, f32[768,512]{1,0:T(8,128)}, u32[]{:S(2)}) copy-start(f32[768,512]{1,0:T(8,128)} %v_ref.1) | copy-start | bytes 4718596
  18.6 0.7 copy-start.2
  26.4 22.7 %collective-permute-start.10 = (f32[120,128]{1,0:T(8,128)S(1)}, f32[120,128]{1,0:T(8,128)S(1)}, u32[]{:S(2)}, u32[]{:S(2)}) collective-permute-start(f32[120,128]{1,0:T(8,128)S(1)} %shard_map.58.refs_0_), channel_id=1, source_target_pairs={{12,0},{14,2},{16,4},{18,6},{20,8},{22,10},{24,12},{26,14},{28,16}... | collective-permute-start | bytes 184328 | tf_op jit(solution)/shard_map/ppermute | solution.py:120
  37.2 19.4 %collective-permute-start.11 = (f32[120,128]{1,0:T(8,128)S(1)}, f32[120,128]{1,0:T(8,128)S(1)}, u32[]{:S(2)}, u32[]{:S(2)}) collective-permute-start(f32[120,128]{1,0:T(8,128)S(1)} %shard_map.58.refs_0_), channel_id=1, source_target_pairs={{20,0},{22,2},{24,4},{26,6},{28,8},{30,10},{0,12},{2,14},{4,16},{6... | collective-permute-start | bytes 184328 | tf_op jit(solution)/shard_map/ppermute | solution.py:120
  39.1 17.5 %collective-permute-start.8 = (f32[120,128]{1,0:T(8,128)S(1)}, f32[120,128]{1,0:T(8,128)S(1)}, u32[]{:S(2)}, u32[]{:S(2)}) collective-permute-start(f32[120,128]{1,0:T(8,128)S(1)} %shard_map.58.refs_0_), channel_id=1, source_target_pairs={{6,0},{8,2},{10,4},{12,6},{14,8},{16,10},{18,12},{20,14},{22,16},{... | collective-permute-start | bytes 184328 | tf_op jit(solution)/shard_map/ppermute | solution.py:120
  47.2 13.0 %collective-permute-start.9 = (f32[120,128]{1,0:T(8,128)S(1)}, f32[120,128]{1,0:T(8,128)S(1)}, u32[]{:S(2)}, u32[]{:S(2)}) collective-permute-start(f32[120,128]{1,0:T(8,128)S(1)} %shard_map.58.refs_0_), channel_id=1, source_target_pairs={{26,0},{28,2},{30,4},{0,6},{2,8},{4,10},{6,12},{8,14},{10,16},{12,... | collective-permute-start | bytes 184328 | tf_op jit(solution)/shard_map/ppermute | solution.py:120
  60.3 14.0 %collective-permute-start.12 = (f32[5,120,128]{2,1,0:T(8,128)S(1)}, f32[5,120,128]{2,1,0:T(8,128)S(1)}, u32[]{:S(2)}, u32[]{:S(2)}) collective-permute-start(f32[5,120,128]{2,1,0:T(8,128)S(1)} %shard_map.59.held_ref), channel_id=1, source_target_pairs={{2,0},{4,2},{6,4},{8,6},{10,8},{12,10},{14,12},{16,14},{18,16},{20... | collective-permute-start | bytes 921608 | tf_op jit(solution)/shard_map/ppermute | solution.py:120
  62.2 12.3 %collective-permute-start.13 = (f32[5,120,128]{2,1,0:T(8,128)S(1)}, f32[5,120,128]{2,1,0:T(8,128)S(1)}, u32[]{:S(2)}, u32[]{:S(2)}) collective-permute-start(f32[5,120,128]{2,1,0:T(8,128)S(1)} %shard_map.59.held_ref), channel_id=1, source_target_pairs={{30,0},{0,2},{2,4},{4,6},{6,8},{8,10},{10,12},{12,14},{14,16},{16,... | collective-permute-start | bytes 921608 | tf_op jit(solution)/shard_map/ppermute | solution.py:120
  66.1 8.2 %collective-permute-start.14 = (f32[120,128]{1,0:T(8,128)S(1)}, f32[120,128]{1,0:T(8,128)S(1)}, u32[]{:S(2)}, u32[]{:S(2)}) collective-permute-start(f32[120,128]{1,0:T(8,128)S(1)} %collective-permute-done.10.refs_3_), channel_id=1, source_target_pairs={{4,0},{6,2},{8,4},{10,6},{12,8},{14,10},{16,12},{18,14},{20,16},{2... | collective-permute-start | bytes 184328 | tf_op jit(solution)/shard_map/ppermute | solution.py:120
  75.1 4.5 %collective-permute-start.15 = (f32[16,120,128]{2,1,0:T(8,128)S(1)}, f32[16,120,128]{2,1,0:T(8,128)S(1)}, u32[]{:S(2)}, u32[]{:S(2)}) collective-permute-start(f32[16,120,128]{2,1,0:T(8,128)S(1)} %shard_map.60.t_ref), channel_id=1, source_target_pairs={{0,1},{1,0},{2,3},{3,2},{4,5},{5,4},{6,7},{7,6},{8,9},{9,8},{10,11... | collective-permute-start | bytes 2949128 | tf_op jit(solution)/shard_map/ppermute | solution.py:240
  104.2 11.3 %copy-start.4 = (s32[2048]{0:T(1024)S(1)}, s32[2048]{0:T(1024)}, u32[]{:S(2)}) copy-start(s32[2048]{0:T(1024)} %param.9) | copy-start | bytes 24580
  104.2 11.3 %copy-start.5 = (s32[512]{0:T(512)S(1)}, s32[512]{0:T(512)}, u32[]{:S(2)}) copy-start(s32[512]{0:T(512)} %param.11) | copy-start | bytes 6148
  105.0 10.5 %all-to-all-start.4 = ((f32[4,40,512]{2,1,0:T(8,128)}), f32[4,40,512]{2,1,0:T(8,128)S(1)}, u32[]{:S(2)}, u32[]{:S(2)}) async-start(f32[4,40,512]{2,1,0:T(8,128)} %shard_map.63), calls=%async_computation.4 | async-start | bytes 655360 | tf_op jit(solution)/shard_map/all_to_all | solution.py:249
  117.0 0.7 copy-start.3

commit v9 on v6

--- a/solution.py
+++ b/solution.py
@@ -71,18 +71,27 @@
     return jnp.concatenate(rows, axis=0)
 
 
-def table_kernel(place_ref, round_ref, ij_ref, cd_ref, most_ref, rank_ref, chosen_ref, keep_ref):
-    core, z, group = place_ref[0], place_ref[1], place_ref[2]
+def table_kernel(place_ref, round_ref, ij_ref, cd_ref, ab_ref, most_ref, chosen_ref, keep_ref, spot_ref, like_ref):
+    core, z, group, row = place_ref[0], place_ref[1], place_ref[2], place_ref[3]
     rank = ranks(ij_ref[...])
     most_ref[0] = jnp.max(rank).astype(I32)
-    rank_ref[...] = rank.astype(I32)
+    rank = rank.astype(I32) - round_ref[0] * CAP
+    want = lax.broadcasted_iota(I32, (CAP, BLOCK), 0)
+    block = lax.broadcasted_iota(I32, rank.shape, 0)
+
+    def row_of(index):
+        return jnp.sum(jnp.where(block == index, rank, 0), axis=0, keepdims=True)
+
     cd = cd_ref[pl.ds(z * 2 + core, 1), :]
-    want = lax.broadcasted_iota(I32, (CAP, BLOCK), 0)
     for b in range(GROUP):
         at = slice(b * BLOCK, (b + 1) * BLOCK)
-        here = rank_ref[pl.ds(group * GROUP + b, 1), :] - round_ref[0] * CAP
-        chosen_ref[:, at] = jnp.where(want == here, 1.0, 0.0).astype(BF16)
+        chosen_ref[:, at] = jnp.where(want == row_of(group * GROUP + b), 1.0, 0.0).astype(BF16)
         keep_ref[at, :] = jnp.where(down(ij_ref[pl.ds(group * GROUP + b, 1), :]) == cd, 1.0, 0.0)
+    spot_ref[...] = jnp.where(want == row_of(row), 1.0, 0.0).astype(BF16)
+    ij = down(ij_ref[pl.ds(row, 1), :])
+    for k in range(like_ref.shape[1] // BLOCK):
+        at = slice(k * BLOCK, (k + 1) * BLOCK)
+        like_ref[:, at] = jnp.where(ij == ab_ref[:, at], 1.0, 0.0)
 
 
 def pack_kernel(x_ref, chosen_ref, keep_ref, first_ref, out_ref):
@@ -157,22 +166,12 @@
         copies_ref[b] = total
 
 
-def spread(a, slots, labels, ab_ref, out_ref):
-    chosen = jnp.where(lax.broadcasted_iota(I32, (a.shape[0], BLOCK), 0) == slots, 1.0, 0.0).astype(BF16)
+def expand_kernel(a_ref, spot_ref, like_ref, out_ref):
     total = None
-    for part in split3(a):
-        term = lax.dot_general(chosen, part, (((0,), (0,)), ((), ())), preferred_element_type=F32)
+    for part in split3(a_ref[...]):
+        term = lax.dot_general(spot_ref[...], part, (((0,), (0,)), ((), ())), preferred_element_type=F32)
         total = term if total is None else total + term
-    ij = down(labels)
-    for k in range(out_ref.shape[1] // BLOCK):
-        cols = slice(k * BLOCK, (k + 1) * BLOCK)
-        out_ref[:, cols] = jnp.where(ij == ab_ref[:, cols], 0.5 * total[:, cols], 0.0)
-
-
-def expand_kernel(place_ref, round_ref, a_ref, rank_ref, ij_ref, ab_ref, out_ref):
-    row = place_ref[3]
-    slots = rank_ref[pl.ds(row, 1), :] - round_ref[0] * CAP
-    spread(a_ref[...], slots, ij_ref[pl.ds(row, 1), :], ab_ref, out_ref)
+    out_ref[...] = jnp.where(like_ref[...] > 0.0, 0.5 * total, 0.0)
 
 
 def body(amplitudes, integrals, ij_irrep, cd_irrep, ab_irrep):
@@ -204,13 +203,14 @@
             table_kernel,
             [
                 shape((1,), I32),
-                shape((BLOCKS, BLOCK), I32),
                 shape((CAP, GROUP * BLOCK), BF16),
                 shape((GROUP * BLOCK, WIDE), F32),
+                shape((CAP, BLOCK), BF16),
+                shape((BLOCK, abs_), F32),
             ],
-            [smem, smem, vmem, vmem],
-            out_specs=[smem, vmem, vmem, vmem],
-        )(place, number, ij, cd_own)
+            [smem] * 2 + [vmem] * 3,
+            out_specs=[smem] + [vmem] * 4,
+        )(place, number, ij, cd_own, ab)
 
     def products(chosen, keep):
         packed = call(pack_kernel, shape((3 * PART, WIDE), F32), [vmem] * 3 + [anywhere])(arrived, chosen, keep, v_hi)
@@ -222,21 +222,18 @@
         half = call(mine_kernel, full, [smem] + [vmem] * 3, cost)(place, gathered.reshape(pieces), v_hi, v_lo)
         return call(other_kernel, full, [smem] + [vmem] * 4, cost)(place, other.reshape(pieces), v_hi, v_lo, half)
 
-    def one_round(number, rank, chosen, keep):
+    def one_round(chosen, keep, spot, like):
         partial = lax.all_to_all(products(chosen, keep), row, split_axis=0, concat_axis=0, tiled=True)
         copies = call(sum_kernel, shape((4, PART, abs_), F32), [vmem])(partial.reshape(BLOCKS, PART, abs_))
         summed = lax.all_to_all(copies.reshape(CAP, abs_), "y", split_axis=0, concat_axis=0, tiled=True)
-        return call(expand_kernel, shape((BLOCK, abs_), F32), [smem] * 2 + [vmem] * 4)(
-            place, number, summed, rank, ij, ab
-        )
-
-    start = jnp.zeros((1,), I32)
-    most, rank, chosen, keep = tables(start)
-    out = one_round(start, rank, chosen, keep)
+        return call(expand_kernel, shape((BLOCK, abs_), F32), [vmem] * 3)(summed, spot, like)
+
+    most, *matrices = tables(jnp.zeros((1,), I32))
+    out = one_round(*matrices)
 
     def again(state):
         number, out = state
-        return number + 1, out + one_round(number[None], *tables(number[None])[1:])
+        return number + 1, out + one_round(*tables(number[None])[1:])
 
     return lax.while_loop(lambda state: state[0] * CAP <= most[0], again, (jnp.int32(1), out))[1]
 

time: 109 us -> 108 us (level)
  no operation moved by 1% of the time
where the time goes in v9:
time: 108 us; the launch traced here: 107 us
  blocking collectives  61.5 us (57%)
  starting transfers between devices  18.2 us (17%)
  waiting for transfers between devices  13.6 us (13%)
  Pallas kernels  8.51 us (8%)
  local copies, waits for them, and re-layouts  4.49 us (4%)
    all_gather x1, blocking collectives, products(): gathered = lax.all_gather(packed, ('zh', 'zl'), axis=0, tiled=True)  38.5 us
    all_to_all x1, blocking collectives, one_round(): lax.all_to_all(products(chosen, keep), row, split_axis=0, concat_axis=0,...  23 us
    all_to_all x1, starting transfers between devices, body(): lax.all_to_all(dealt, ('zl', 'core', 'x', 'y'), split_axis=0, concat_axis...  12.8 us
    all_to_all x1, waiting for transfers between devices, one_round(): lax.all_to_all(copies.reshape(CAP, abs_), 'y', split_axis=0, concat_axis=...  7.07 us
    all_to_all x1, waiting for transfers between devices, body(): lax.all_to_all(dealt, ('zl', 'core', 'x', 'y'), split_axis=0, concat_axis...  5.75 us
    unnamed x12, local copies, waits for them, and re-layouts  3.72 us
    all_to_all x1, starting transfers between devices, one_round(): lax.all_to_all(copies.reshape(CAP, abs_), 'y', split_axis=0, concat_axis=...  3.45 us
  transfers between devices with their start and end apart: 3, of which 3 were waited for; matrix products, arithmetic and copies ran while one was open for 1% of the time, Pallas kernels for 4%

profile of v9, /device:TPU:6, one launch (start us, length us, event | category | flops | bytes accessed | tf_op | source)
XLA Modules:
  0.0 107.1 jit_solution(13450828052430877808)
XLA Ops:
  0.0 0.0 copy-start.1
  0.0 0.9 copy-done.1
  0.9 1.0 shard_map.55
  1.9 12.8 %all-to-all-start.2 = ((f32[128,4,128]{2,1,0:T(4,128)}), f32[128,4,128]{2,1,0:T(4,128)S(1)}, u32[]{:S(2)}, u32[]{:S(2)}) async-start(f32[128,4,128]{2,1,0:T(4,128)} %shard_map.55), calls=%async_computation.2 | async-start | bytes 524288 | tf_op jit(solution)/shard_map/all_to_all | solution.py:192
  14.7 0.8 reshape.41
  15.5 0.1 pad_add_fusion.place_ref
  15.6 1.6 %shard_map.56 = (s32[1]{0:T(128)}, bf16[160,512]{1,0:T(8,128)(2,1)S(1)}, f32[512,128]{1,0:T(8,128)S(1)}, bf16[160,128]{1,0:T(8,128)(2,1)S(1)}, f32[128,512]{1,0:T(8,128)S(1)}) custom-call(s32[4]{0:T(128)S(1)} %pad_add_fusion.place_ref, s32[1]{0:T(128)} %constant.29.clone.1.round_ref, s32[16,128]{1,0:T(8,128)} %bitcast.37, s32[8,128]{1,0:T(8,128)S(1)} %pad.4.cd_ref, ...), custom_call_target="tpu_custom_call" | custom-call | flops 1000000 | bytes 1000000 | tf_op jit(solution)/shard_map/pallas_call | solution.py:202
  17.2 0.0 copy-start
  17.2 1.4 %copy-done = f32[768,512]{1,0:T(8,128)S(1)} copy-done((f32[768,512]{1,0:T(8,128)S(1)}, f32[768,512]{1,0:T(8,128)}, u32[]{:S(2)}) %copy-start) | copy-done | bytes 1572888
  18.6 0.0 copy-start.2
  18.6 0.7 copy-done.2
  19.3 1.0 shard_map.57
  20.3 5.7 %all-to-all-done.2.x_ref = f32[128,4,128]{2,1,0:T(4,128)S(1)} async-done(((f32[128,4,128]{2,1,0:T(4,128)}), f32[128,4,128]{2,1,0:T(4,128)S(1)}, u32[]{:S(2)}, u32[]{:S(2)}) %all-to-all-start.2) | async-done | bytes 262176 | tf_op jit(solution)/shard_map/all_to_all | solution.py:192
  26.0 0.3 shard_map.58
  26.4 38.5 %all_gather.6 = f32[1920,128]{1,0:T(8,128)S(1)} all-gather(f32[120,128]{1,0:T(8,128)S(1)} %shard_map.58), channel_id=1, replica_groups=mesh['x'=4,'y'=4,'zh'=4,'zl'=4,'core'=2] {'zh','zl'}, dimensions={0}, use_global_device_ids=true | all-gather | bytes 1044480 | tf_op jit(solution)/shard_map/all_gather | solution.py:217
  64.9 1.9 %collective-permute-start.1 = (f32[1920,128]{1,0:T(8,128)S(1)}, f32[1920,128]{1,0:T(8,128)S(1)}, u32[]{:S(2)}, u32[]{:S(2)}) collective-permute-start(f32[1920,128]{1,0:T(8,128)S(1)} %all_gather.6), channel_id=1, source_target_pairs={{0,1},{1,0},{2,3},{3,2},{4,5},{5,4},{6,7},{7,6},{8,9},{9,8},{10,11... | collective-permute-start | bytes 2949128 | tf_op jit(solution)/shard_map/ppermute | solution.py:218
  66.8 1.8 %shard_map.59.mine_ref = f32[640,512]{1,0:T(8,128)S(1)} custom-call(s32[4]{0:T(128)S(1)} %pad_add_fusion.place_ref, f32[16,120,128]{2,1,0:T(8,128)S(1)} %bitcast.33, bf16[1024,512]{1,0:T(8,128)(2,1)S(1)} %get-tuple-element.175.first_ref.hi_ref, bf16[1024,512]{1,0:T(8,128)(2,1)S(1)} %get-tuple-element.176.lo_ref), custom_call_target="tpu_custom_call" | custom-call | flops 1000000000 | bytes 3000000 | tf_op jit(solution)/shard_map/pallas_call | solution.py:222
  68.6 0.8 collective-permute-done.1
  69.4 1.8 %shard_map.60 = f32[640,512]{1,0:T(8,128)S(1)} custom-call(s32[4]{0:T(128)S(1)} %pad_add_fusion.place_ref, f32[16,120,128]{2,1,0:T(8,128)S(1)} %bitcast.35, bf16[1024,512]{1,0:T(8,128)(2,1)S(1)} %get-tuple-element.175.first_ref.hi_ref, bf16[1024,512]{1,0:T(8,128)(2,1)S(1)} %get-tuple-element.176.lo_ref, f32[640,512]{1,0:T(8,128)S(1)} %shard_map.59.mine_ref), custom_call_target="tpu_custom_call" | custom-call | flops 1000000000 | bytes 3000000 | tf_op jit(solution)/shard_map/pallas_call | solution.py:223
  71.1 23.0 %all_to_all.39.x_ref = f32[16,40,512]{2,1,0:T(8,128)S(1)} all-to-all(f32[16,40,512]{2,1,0:T(8,128)S(1)} %bitcast.32), channel_id=1, replica_groups=mesh['x'=4,'y'=4,'zh'=4,'zl'=4,'core'=2] {'x','y'}, dimensions={0} | all-to-all | bytes 2621440 | tf_op jit(solution)/shard_map/all_to_all | solution.py:226
  94.1 0.0 copy-start.4
  94.1 0.0 copy-start.5
  94.1 0.8 shard_map.61
  94.9 3.5 %all-to-all-start.4 = ((f32[4,40,512]{2,1,0:T(8,128)}), f32[4,40,512]{2,1,0:T(8,128)S(1)}, u32[]{:S(2)}, u32[]{:S(2)}) async-start(f32[4,40,512]{2,1,0:T(8,128)} %shard_map.61), calls=%async_computation.4 | async-start | bytes 655360 | tf_op jit(solution)/shard_map/all_to_all | solution.py:228
  98.3 7.1 %all-to-all-done.4 = f32[4,40,512]{2,1,0:T(8,128)S(1)} async-done(((f32[4,40,512]{2,1,0:T(8,128)}), f32[4,40,512]{2,1,0:T(8,128)S(1)}, u32[]{:S(2)}, u32[]{:S(2)}) %all-to-all-start.4) | async-done | bytes 327712 | tf_op jit(solution)/shard_map/all_to_all | solution.py:228
  105.4 0.3 shard_map.62
  105.7 0.0 copy-done.4
  105.7 0.0 copy-done.5
  105.7 0.7 while.10
  106.4 0.0 copy-start.3
  106.4 0.7 copy-done.3
  (1 shorter events, 0.0 us)
Async XLA Ops:
  0.0 0.9 copy-start.1
  1.9 24.1 %all-to-all-start.2 = ((f32[128,4,128]{2,1,0:T(4,128)}), f32[128,4,128]{2,1,0:T(4,128)S(1)}, u32[]{:S(2)}, u32[]{:S(2)}) async-start(f32[128,4,128]{2,1,0:T(4,128)} %shard_map.55), calls=%async_computation.2 | async-start | bytes 524288 | tf_op jit(solution)/shard_map/all_to_all | solution.py:192
  17.2 1.4 %copy-start = (f32[768,512]{1,0:T(8,128)S(1)}, f32[768,512]{1,0:T(8,128)}, u32[]{:S(2)}) copy-start(f32[768,512]{1,0:T(8,128)} %v_ref.1) | copy-start | bytes 4718596
  18.6 0.7 copy-start.2
  64.9 4.4 %collective-permute-start.1 = (f32[1920,128]{1,0:T(8,128)S(1)}, f32[1920,128]{1,0:T(8,128)S(1)}, u32[]{:S(2)}, u32[]{:S(2)}) collective-permute-start(f32[1920,128]{1,0:T(8,128)S(1)} %all_gather.6), channel_id=1, source_target_pairs={{0,1},{1,0},{2,3},{3,2},{4,5},{5,4},{6,7},{7,6},{8,9},{9,8},{10,11... | collective-permute-start | bytes 2949128 | tf_op jit(solution)/shard_map/ppermute | solution.py:218
  94.1 11.6 %copy-start.4 = (s32[2048]{0:T(1024)S(1)}, s32[2048]{0:T(1024)}, u32[]{:S(2)}) copy-start(s32[2048]{0:T(1024)} %param.9) | copy-start | bytes 24580
  94.1 11.6 %copy-start.5 = (s32[512]{0:T(512)S(1)}, s32[512]{0:T(512)}, u32[]{:S(2)}) copy-start(s32[512]{0:T(512)} %param.11) | copy-start | bytes 6148
  94.9 10.5 %all-to-all-start.4 = ((f32[4,40,512]{2,1,0:T(8,128)}), f32[4,40,512]{2,1,0:T(8,128)S(1)}, u32[]{:S(2)}, u32[]{:S(2)}) async-start(f32[4,40,512]{2,1,0:T(8,128)} %shard_map.61), calls=%async_computation.4 | async-start | bytes 655360 | tf_op jit(solution)/shard_map/all_to_all | solution.py:228
  106.4 0.7 copy-start.3

commit v10 on v9

--- a/solution.py
+++ b/solution.py
@@ -71,10 +71,11 @@
     return jnp.concatenate(rows, axis=0)
 
 
-def table_kernel(place_ref, round_ref, ij_ref, cd_ref, ab_ref, most_ref, chosen_ref, keep_ref, spot_ref, like_ref):
+def table_kernel(place_ref, round_ref, ij_ref, cd_ref, ab_ref, most_ref, next_ref, chosen_ref, keep_ref, spot_ref, like_ref):
     core, z, group, row = place_ref[0], place_ref[1], place_ref[2], place_ref[3]
     rank = ranks(ij_ref[...])
     most_ref[0] = jnp.max(rank).astype(I32)
+    next_ref[0] = round_ref[0] + 1
     rank = rank.astype(I32) - round_ref[0] * CAP
     want = lax.broadcasted_iota(I32, (CAP, BLOCK), 0)
     block = lax.broadcasted_iota(I32, rank.shape, 0)
@@ -203,13 +204,14 @@
             table_kernel,
             [
                 shape((1,), I32),
+                shape((1,), I32),
                 shape((CAP, GROUP * BLOCK), BF16),
                 shape((GROUP * BLOCK, WIDE), F32),
                 shape((CAP, BLOCK), BF16),
                 shape((BLOCK, abs_), F32),
             ],
             [smem] * 2 + [vmem] * 3,
-            out_specs=[smem] + [vmem] * 4,
+            out_specs=[smem] * 2 + [vmem] * 4,
         )(place, number, ij, cd_own, ab)
 
     def products(chosen, keep):
@@ -228,14 +230,15 @@
         summed = lax.all_to_all(copies.reshape(CAP, abs_), "y", split_axis=0, concat_axis=0, tiled=True)
         return call(expand_kernel, shape((BLOCK, abs_), F32), [vmem] * 3)(summed, spot, like)
 
-    most, *matrices = tables(jnp.zeros((1,), I32))
+    most, following, *matrices = tables(jnp.zeros((1,), I32))
     out = one_round(*matrices)
 
     def again(state):
         number, out = state
-        return number + 1, out + one_round(*tables(number[None])[1:])
-
-    return lax.while_loop(lambda state: state[0] * CAP <= most[0], again, (jnp.int32(1), out))[1]
+        _, following, *matrices = tables(number)
+        return following, out + one_round(*matrices)
+
+    return lax.while_loop(lambda state: state[0][0] * CAP <= most[0], again, (following, out))[1]
 
 
 def solution(mesh):

time: 108 us -> 107 us (level)
  blocking collectives: 61.5 us -> 71 us
  waiting for transfers between devices: 13.6 us -> 6.51 us
  starting transfers between devices: 18.2 us -> 14.7 us
    all_to_all x0 -> x1, blocking collectives: none -> 9.5 us  [one_round(): lax.all_to_all(copies.reshape(CAP, abs_), 'y', split_axis=0, concat_axis=...]
    all_to_all x1 -> x0, waiting for transfers between devices: 7.07 us -> none  [one_round(): lax.all_to_all(copies.reshape(CAP, abs_), 'y', split_axis=0, concat_axis=...]
    all_to_all x1 -> x0, starting transfers between devices: 3.45 us -> none  [one_round(): lax.all_to_all(copies.reshape(CAP, abs_), 'y', split_axis=0, concat_axis=...]
  transfers between devices with their start and end apart: 3 -> 2, of which waited for: 3 -> 2; matrix products, arithmetic and copies ran while one was open for 1% -> 1% of each run, Pallas kernels for 4% -> 4%
where the time goes in v10:
time: 107 us; the launch traced here: 106 us
  blocking collectives  71 us (66%)
  starting transfers between devices  14.7 us (14%)
  Pallas kernels  7.79 us (7%)
  waiting for transfers between devices  6.51 us (6%)
  local copies, waits for them, and re-layouts  4.49 us (4%)
  loops' own time  1.2 us (1%)
    all_gather x1, blocking collectives, products(): gathered = lax.all_gather(packed, ('zh', 'zl'), axis=0, tiled=True)  38.5 us
    all_to_all x1, blocking collectives, one_round(): lax.all_to_all(products(chosen, keep), row, split_axis=0, concat_axis=0,...  23 us
    all_to_all x1, starting transfers between devices, body(): lax.all_to_all(dealt, ('zl', 'core', 'x', 'y'), split_axis=0, concat_axis...  12.8 us
    all_to_all x1, blocking collectives, one_round(): lax.all_to_all(copies.reshape(CAP, abs_), 'y', split_axis=0, concat_axis=...  9.5 us
    all_to_all x1, waiting for transfers between devices, body(): lax.all_to_all(dealt, ('zl', 'core', 'x', 'y'), split_axis=0, concat_axis...  5.74 us
    unnamed x12, local copies, waits for them, and re-layouts  3.72 us
  transfers between devices with their start and end apart: 2, of which 2 were waited for; matrix products, arithmetic and copies ran while one was open for 1% of the time, Pallas kernels for 4%

profile of v10, /device:TPU:6, one launch (start us, length us, event | category | flops | bytes accessed | tf_op | source)
XLA Modules:
  0.0 105.9 jit_solution(352731061591553769)
XLA Ops:
  0.0 0.0 copy-start.1
  0.0 0.9 copy-done.1
  0.9 1.0 shard_map.56
  1.9 12.8 %all-to-all-start.2 = ((f32[128,4,128]{2,1,0:T(4,128)}), f32[128,4,128]{2,1,0:T(4,128)S(1)}, u32[]{:S(2)}, u32[]{:S(2)}) async-start(f32[128,4,128]{2,1,0:T(4,128)} %shard_map.56), calls=%async_computation.2 | async-start | bytes 524288 | tf_op jit(solution)/shard_map/all_to_all | solution.py:193
  14.7 0.8 reshape.44
  15.5 0.1 pad_add_fusion.place_ref
  15.6 1.6 %shard_map.55 = (s32[1]{0:T(128)}, s32[1]{0:T(128)}, bf16[160,512]{1,0:T(8,128)(2,1)S(1)}, f32[512,128]{1,0:T(8,128)S(1)}, bf16[160,128]{1,0:T(8,128)(2,1)S(1)}, /*index=5*/f32[128,512]{1,0:T(8,128)S(1)}) custom-call(s32[4]{0:T(128)S(1)} %pad_add_fusion.place_ref, s32[1]{0:T(128)} %constant.26.clone.1.round_ref, s32[16,128]{1,0:T(8,128)} %bitcast.25, ...), custom_call_target="tpu_custom_call" | custom-call | flops 1000000 | bytes 1000000 | tf_op jit(solution)/shard_map/pallas_call | solution.py:203
  17.2 0.0 copy-start
  17.2 1.4 %copy-done = f32[768,512]{1,0:T(8,128)S(1)} copy-done((f32[768,512]{1,0:T(8,128)S(1)}, f32[768,512]{1,0:T(8,128)}, u32[]{:S(2)}) %copy-start) | copy-done | bytes 1572888
  18.6 0.0 copy-start.2
  18.6 0.7 copy-done.2
  19.3 1.0 shard_map.57
  20.3 5.7 %all-to-all-done.2.x_ref = f32[128,4,128]{2,1,0:T(4,128)S(1)} async-done(((f32[128,4,128]{2,1,0:T(4,128)}), f32[128,4,128]{2,1,0:T(4,128)S(1)}, u32[]{:S(2)}, u32[]{:S(2)}) %all-to-all-start.2) | async-done | bytes 262176 | tf_op jit(solution)/shard_map/all_to_all | solution.py:193
  26.0 0.3 shard_map.58
  26.4 38.5 %all_gather.6 = f32[1920,128]{1,0:T(8,128)S(1)} all-gather(f32[120,128]{1,0:T(8,128)S(1)} %shard_map.58), channel_id=1, replica_groups=mesh['x'=4,'y'=4,'zh'=4,'zl'=4,'core'=2] {'zh','zl'}, dimensions={0}, use_global_device_ids=true | all-gather | bytes 1044480 | tf_op jit(solution)/shard_map/all_gather | solution.py:219
  64.9 1.9 %collective-permute-start.1 = (f32[1920,128]{1,0:T(8,128)S(1)}, f32[1920,128]{1,0:T(8,128)S(1)}, u32[]{:S(2)}, u32[]{:S(2)}) collective-permute-start(f32[1920,128]{1,0:T(8,128)S(1)} %all_gather.6), channel_id=1, source_target_pairs={{0,1},{1,0},{2,3},{3,2},{4,5},{5,4},{6,7},{7,6},{8,9},{9,8},{10,11... | collective-permute-start | bytes 2949128 | tf_op jit(solution)/shard_map/ppermute | solution.py:220
  66.8 1.8 %shard_map.59.mine_ref = f32[640,512]{1,0:T(8,128)S(1)} custom-call(s32[4]{0:T(128)S(1)} %pad_add_fusion.place_ref, f32[16,120,128]{2,1,0:T(8,128)S(1)} %bitcast.21, bf16[1024,512]{1,0:T(8,128)(2,1)S(1)} %get-tuple-element.118.first_ref.hi_ref, bf16[1024,512]{1,0:T(8,128)(2,1)S(1)} %get-tuple-element.119.lo_ref), custom_call_target="tpu_custom_call" | custom-call | flops 1000000000 | bytes 3000000 | tf_op jit(solution)/shard_map/pallas_call | solution.py:224
  68.6 0.8 collective-permute-done.1
  69.4 1.8 %shard_map.60 = f32[640,512]{1,0:T(8,128)S(1)} custom-call(s32[4]{0:T(128)S(1)} %pad_add_fusion.place_ref, f32[16,120,128]{2,1,0:T(8,128)S(1)} %bitcast.23, bf16[1024,512]{1,0:T(8,128)(2,1)S(1)} %get-tuple-element.118.first_ref.hi_ref, bf16[1024,512]{1,0:T(8,128)(2,1)S(1)} %get-tuple-element.119.lo_ref, f32[640,512]{1,0:T(8,128)S(1)} %shard_map.59.mine_ref), custom_call_target="tpu_custom_call" | custom-call | flops 1000000000 | bytes 3000000 | tf_op jit(solution)/shard_map/pallas_call | solution.py:225
  71.1 23.0 %all_to_all.37.x_ref = f32[16,40,512]{2,1,0:T(8,128)S(1)} all-to-all(f32[16,40,512]{2,1,0:T(8,128)S(1)} %bitcast.20), channel_id=1, replica_groups=mesh['x'=4,'y'=4,'zh'=4,'zl'=4,'core'=2] {'x','y'}, dimensions={0} | all-to-all | bytes 2621440 | tf_op jit(solution)/shard_map/all_to_all | solution.py:228
  94.1 0.0 copy-start.4
  94.1 0.0 copy-start.5
  94.1 0.1 shard_map.61
  94.2 9.5 %all_to_all.38 = f32[4,40,512]{2,1,0:T(8,128)S(1)} all-to-all(f32[4,40,512]{2,1,0:T(8,128)S(1)} %shard_map.61), channel_id=1, replica_groups=mesh['x'=4,'y'=4,'zh'=4,'zl'=4,'core'=2] {'y'}, dimensions={0} | all-to-all | bytes 655360 | tf_op jit(solution)/shard_map/all_to_all | solution.py:230
  103.7 0.3 shard_map.62
  104.0 0.0 copy-done.4
  104.0 0.0 copy-done.5
  104.0 1.2 %while.9 = (s32[1]{0:T(128)}, f32[128,512]{1,0:T(8,128)S(1)}, s32[1]{0:T(128)}, s32[4]{0:T(128)S(1)}, s32[16,128]{1,0:T(8,128)S(1)}, /*index=5*/s32[8,128]{1,0:T...) while((s32[1]{0:T(128)}, f32[128,512]{1,0:T(8,128)S(1)}, ...), condition=%region_1.2_spmd, body=%region_0.1_spmd | while | flops 2004065536 | bytes 19040020 | solution.py:241
  105.2 0.0 copy-start.3
  105.2 0.7 copy-done.3
  (1 shorter events, 0.0 us)
Async XLA Ops:
  0.0 0.9 copy-start.1
  1.9 24.1 %all-to-all-start.2 = ((f32[128,4,128]{2,1,0:T(4,128)}), f32[128,4,128]{2,1,0:T(4,128)S(1)}, u32[]{:S(2)}, u32[]{:S(2)}) async-start(f32[128,4,128]{2,1,0:T(4,128)} %shard_map.56), calls=%async_computation.2 | async-start | bytes 524288 | tf_op jit(solution)/shard_map/all_to_all | solution.py:193
  17.2 1.4 %copy-start = (f32[768,512]{1,0:T(8,128)S(1)}, f32[768,512]{1,0:T(8,128)}, u32[]{:S(2)}) copy-start(f32[768,512]{1,0:T(8,128)} %v_ref.1) | copy-start | bytes 4718596
  18.6 0.7 copy-start.2
  64.9 4.4 %collective-permute-start.1 = (f32[1920,128]{1,0:T(8,128)S(1)}, f32[1920,128]{1,0:T(8,128)S(1)}, u32[]{:S(2)}, u32[]{:S(2)}) collective-permute-start(f32[1920,128]{1,0:T(8,128)S(1)} %all_gather.6), channel_id=1, source_target_pairs={{0,1},{1,0},{2,3},{3,2},{4,5},{5,4},{6,7},{7,6},{8,9},{9,8},{10,11... | collective-permute-start | bytes 2949128 | tf_op jit(solution)/shard_map/ppermute | solution.py:220
  94.1 9.9 %copy-start.4 = (s32[2048]{0:T(1024)S(1)}, s32[2048]{0:T(1024)}, u32[]{:S(2)}) copy-start(s32[2048]{0:T(1024)} %param.9) | copy-start | bytes 24580
  94.1 9.9 %copy-start.5 = (s32[512]{0:T(512)S(1)}, s32[512]{0:T(512)}, u32[]{:S(2)}) copy-start(s32[512]{0:T(512)} %param.11) | copy-start | bytes 6148
  105.2 0.7 copy-start.3

commit v11 on v10

--- a/solution.py
+++ b/solution.py
@@ -47,7 +47,7 @@
         for core in range(2):
             for row in range(rows):
                 start = ((row * GROUP + z) * 2 + core) * CD_DEV
-                to = (z * 2 + core) * rows + row
+                to = (row * GROUP + z) * 2 + core
                 if start + WIDE <= x_ref.shape[1]:
                     out_ref[to] = x_ref[:, start : start + WIDE]
                 else:
@@ -99,7 +99,7 @@
     total = jnp.zeros((CAP, WIDE), F32)
     for b in range(GROUP):
         at = slice(b * BLOCK, (b + 1) * BLOCK)
-        x = x_ref[b * 32 : (b + 1) * 32].reshape(BLOCK, WIDE)
+        x = jnp.concatenate([x_ref[:, 2 * b + core].reshape(BLOCK // 2, WIDE) for core in range(2)], axis=0)
         x = jnp.where(keep_ref[at, :] > 0.0, x, 0.0)
         hi = x.astype(BF16)
         lo = (x - hi.astype(F32)).astype(BF16)
@@ -190,7 +190,8 @@
     devices = 2 * GROUP * BLOCKS
 
     dealt = call(deal_kernel, shape((devices, 4, WIDE), F32), [vmem])(amplitudes)
-    arrived = lax.all_to_all(dealt, ("zl", "core", "x", "y"), split_axis=0, concat_axis=0, tiled=True)
+    arrived = lax.all_to_all(dealt, ("x", "y", "zl", "core"), split_axis=0, concat_axis=0, tiled=True)
+    arrived = arrived.reshape(BLOCKS, 2 * GROUP, 4, WIDE)
     v_hi, v_lo = call(
         panel_kernel,
         [shape((2 * GROUP * WIDE, abs_), BF16)] * 2,

time: 107 us -> 108 us (level)
  no operation moved by 1% of the time
where the time goes in v11:
time: 108 us; the launch traced here: 106 us
  blocking collectives  71.4 us (66%)
  starting transfers between devices  15.3 us (14%)
  Pallas kernels  7.81 us (7%)
  waiting for transfers between devices  5.99 us (6%)
  local copies, waits for them, and re-layouts  4.49 us (4%)
  loops' own time  1.2 us (1%)
    all_gather x1, blocking collectives, products(): gathered = lax.all_gather(packed, ('zh', 'zl'), axis=0, tiled=True)  38.1 us
    all_to_all x1, blocking collectives, one_round(): lax.all_to_all(products(chosen, keep), row, split_axis=0, concat_axis=0,...  23.8 us
    all_to_all x1, starting transfers between devices, body(): lax.all_to_all(dealt, ('x', 'y', 'zl', 'core'), split_axis=0, concat_axis...  13.3 us
    all_to_all x1, blocking collectives, one_round(): lax.all_to_all(copies.reshape(CAP, abs_), 'y', split_axis=0, concat_axis=...  9.52 us
    all_to_all x1, waiting for transfers between devices, body(): lax.all_to_all(dealt, ('x', 'y', 'zl', 'core'), split_axis=0, concat_axis...  5.23 us
    unnamed x12, local copies, waits for them, and re-layouts  3.72 us
  transfers between devices with their start and end apart: 2, of which 2 were waited for; matrix products, arithmetic and copies ran while one was open for 1% of the time, Pallas kernels for 4%

profile of v11, /device:TPU:6, one launch (start us, length us, event | category | flops | bytes accessed | tf_op | source)
XLA Modules:
  0.0 106.4 jit_solution(2432586078144039514)
XLA Ops:
  0.0 0.0 copy-start.1
  0.0 0.9 copy-done.1
  0.9 1.0 shard_map.56
  1.9 13.3 %all-to-all-start.2 = ((f32[128,4,128]{2,1,0:T(4,128)}), f32[128,4,128]{2,1,0:T(4,128)S(1)}, u32[]{:S(2)}, u32[]{:S(2)}) async-start(f32[128,4,128]{2,1,0:T(4,128)} %shard_map.56), calls=%async_computation.2 | async-start | bytes 524288 | tf_op jit(solution)/shard_map/all_to_all | solution.py:193
  15.3 0.8 reshape.47
  16.0 0.1 pad_add_fusion.place_ref
  16.1 1.6 %shard_map.55 = (s32[1]{0:T(128)}, s32[1]{0:T(128)}, bf16[160,512]{1,0:T(8,128)(2,1)S(1)}, f32[512,128]{1,0:T(8,128)S(1)}, bf16[160,128]{1,0:T(8,128)(2,1)S(1)}, /*index=5*/f32[128,512]{1,0:T(8,128)S(1)}) custom-call(s32[4]{0:T(128)S(1)} %pad_add_fusion.place_ref, s32[1]{0:T(128)} %constant.26.clone.1.round_ref, s32[16,128]{1,0:T(8,128)} %bitcast.28, ...), custom_call_target="tpu_custom_call" | custom-call | flops 1000000 | bytes 1000000 | tf_op jit(solution)/shard_map/pallas_call | solution.py:204
  17.7 0.0 copy-start
  17.7 1.4 %copy-done = f32[768,512]{1,0:T(8,128)S(1)} copy-done((f32[768,512]{1,0:T(8,128)S(1)}, f32[768,512]{1,0:T(8,128)}, u32[]{:S(2)}) %copy-start) | copy-done | bytes 1572888
  19.1 0.0 copy-start.2
  19.1 0.7 copy-done.2
  19.8 1.0 shard_map.57
  20.8 5.2 %all-to-all-done.2 = f32[128,4,128]{2,1,0:T(4,128)S(1)} async-done(((f32[128,4,128]{2,1,0:T(4,128)}), f32[128,4,128]{2,1,0:T(4,128)S(1)}, u32[]{:S(2)}, u32[]{:S(2)}) %all-to-all-start.2) | async-done | bytes 262176 | tf_op jit(solution)/shard_map/all_to_all | solution.py:193
  26.1 0.3 shard_map.58
  26.4 38.1 %all_gather.6 = f32[1920,128]{1,0:T(8,128)S(1)} all-gather(f32[120,128]{1,0:T(8,128)S(1)} %shard_map.58), channel_id=1, replica_groups=mesh['x'=4,'y'=4,'zh'=4,'zl'=4,'core'=2] {'zh','zl'}, dimensions={0}, use_global_device_ids=true | all-gather | bytes 1044480 | tf_op jit(solution)/shard_map/all_gather | solution.py:220
  64.5 1.9 %collective-permute-start.1 = (f32[1920,128]{1,0:T(8,128)S(1)}, f32[1920,128]{1,0:T(8,128)S(1)}, u32[]{:S(2)}, u32[]{:S(2)}) collective-permute-start(f32[1920,128]{1,0:T(8,128)S(1)} %all_gather.6), channel_id=1, source_target_pairs={{0,1},{1,0},{2,3},{3,2},{4,5},{5,4},{6,7},{7,6},{8,9},{9,8},{10,11... | collective-permute-start | bytes 2949128 | tf_op jit(solution)/shard_map/ppermute | solution.py:221
  66.5 1.8 %shard_map.59.mine_ref = f32[640,512]{1,0:T(8,128)S(1)} custom-call(s32[4]{0:T(128)S(1)} %pad_add_fusion.place_ref, f32[16,120,128]{2,1,0:T(8,128)S(1)} %bitcast.22, bf16[1024,512]{1,0:T(8,128)(2,1)S(1)} %get-tuple-element.118.first_ref.hi_ref, bf16[1024,512]{1,0:T(8,128)(2,1)S(1)} %get-tuple-element.119.lo_ref), custom_call_target="tpu_custom_call" | custom-call | flops 1000000000 | bytes 3000000 | tf_op jit(solution)/shard_map/pallas_call | solution.py:225
  68.2 0.8 collective-permute-done.1
  69.0 1.8 %shard_map.60 = f32[640,512]{1,0:T(8,128)S(1)} custom-call(s32[4]{0:T(128)S(1)} %pad_add_fusion.place_ref, f32[16,120,128]{2,1,0:T(8,128)S(1)} %bitcast.24, bf16[1024,512]{1,0:T(8,128)(2,1)S(1)} %get-tuple-element.118.first_ref.hi_ref, bf16[1024,512]{1,0:T(8,128)(2,1)S(1)} %get-tuple-element.119.lo_ref, f32[640,512]{1,0:T(8,128)S(1)} %shard_map.59.mine_ref), custom_call_target="tpu_custom_call" | custom-call | flops 1000000000 | bytes 3000000 | tf_op jit(solution)/shard_map/pallas_call | solution.py:226
  70.8 23.8 %all_to_all.37.x_ref = f32[16,40,512]{2,1,0:T(8,128)S(1)} all-to-all(f32[16,40,512]{2,1,0:T(8,128)S(1)} %bitcast.21), channel_id=1, replica_groups=mesh['x'=4,'y'=4,'zh'=4,'zl'=4,'core'=2] {'x','y'}, dimensions={0} | all-to-all | bytes 2621440 | tf_op jit(solution)/shard_map/all_to_all | solution.py:229
  94.6 0.0 copy-start.4
  94.6 0.0 copy-start.5
  94.6 0.1 shard_map.61
  94.6 9.5 %all_to_all.38 = f32[4,40,512]{2,1,0:T(8,128)S(1)} all-to-all(f32[4,40,512]{2,1,0:T(8,128)S(1)} %shard_map.61), channel_id=1, replica_groups=mesh['x'=4,'y'=4,'zh'=4,'zl'=4,'core'=2] {'y'}, dimensions={0} | all-to-all | bytes 655360 | tf_op jit(solution)/shard_map/all_to_all | solution.py:231
  104.2 0.3 shard_map.62
  104.4 0.0 copy-done.4
  104.5 0.0 copy-done.5
  104.5 1.2 %while.9 = (s32[1]{0:T(128)}, f32[128,512]{1,0:T(8,128)S(1)}, s32[1]{0:T(128)}, s32[4]{0:T(128)S(1)}, s32[16,128]{1,0:T(8,128)S(1)}, /*index=5*/s32[8,128]{1,0:T...) while((s32[1]{0:T(128)}, f32[128,512]{1,0:T(8,128)S(1)}, ...), condition=%region_1.2_spmd, body=%region_0.1_spmd | while | flops 2004065536 | bytes 19040020 | solution.py:242
  105.7 0.0 copy-start.3
  105.7 0.7 copy-done.3
  (1 shorter events, 0.0 us)
Async XLA Ops:
  0.0 0.9 copy-start.1
  1.9 24.2 %all-to-all-start.2 = ((f32[128,4,128]{2,1,0:T(4,128)}), f32[128,4,128]{2,1,0:T(4,128)S(1)}, u32[]{:S(2)}, u32[]{:S(2)}) async-start(f32[128,4,128]{2,1,0:T(4,128)} %shard_map.56), calls=%async_computation.2 | async-start | bytes 524288 | tf_op jit(solution)/shard_map/all_to_all | solution.py:193
  17.7 1.4 %copy-start = (f32[768,512]{1,0:T(8,128)S(1)}, f32[768,512]{1,0:T(8,128)}, u32[]{:S(2)}) copy-start(f32[768,512]{1,0:T(8,128)} %v_ref.1) | copy-start | bytes 4718596
  19.1 0.7 copy-start.2
  64.5 4.4 %collective-permute-start.1 = (f32[1920,128]{1,0:T(8,128)S(1)}, f32[1920,128]{1,0:T(8,128)S(1)}, u32[]{:S(2)}, u32[]{:S(2)}) collective-permute-start(f32[1920,128]{1,0:T(8,128)S(1)} %all_gather.6), channel_id=1, source_target_pairs={{0,1},{1,0},{2,3},{3,2},{4,5},{5,4},{6,7},{7,6},{8,9},{9,8},{10,11... | collective-permute-start | bytes 2949128 | tf_op jit(solution)/shard_map/ppermute | solution.py:221
  94.6 9.9 %copy-start.4 = (s32[2048]{0:T(1024)S(1)}, s32[2048]{0:T(1024)}, u32[]{:S(2)}) copy-start(s32[2048]{0:T(1024)} %param.9) | copy-start | bytes 24580
  94.6 9.9 %copy-start.5 = (s32[512]{0:T(512)S(1)}, s32[512]{0:T(512)}, u32[]{:S(2)}) copy-start(s32[512]{0:T(512)} %param.11) | copy-start | bytes 6148
  105.7 0.7 copy-start.3
